TPU v7x, 128 devices: a whole 4x4x4 slice. The times are simulated.
128 devices in a mesh: tensor: 8 (over z_lo, y), dp: 16 (over x, z_hi, core).
Axes of the slice: x: 4, y: 4, z: 4 (z_hi: 2, z_lo: 2; z = z_hi * 2 + z_lo), core: 2. Of those that a mesh axis runs over, the one named last changes fastest.
Arguments:
- tokens: bfloat16 [2048, 1024], P('dp'), may hold values from -6 to 6
- segment_ids: int32 [2048], replicated, may hold values from 0 to 2, as said below
- norm_gain: bfloat16 [2, 2, 1024], replicated, may hold values from 0.25 to 1.75
- norm_bias: bfloat16 [2, 2, 1024], replicated, may hold values from -1.5 to 1.5
- w_qkv: bfloat16 [2, 1024, 3, 1024], P(None, None, None, 'tensor'), may hold values from -0.1875 to 0.1875
- b_qv: bfloat16 [2, 2, 1024], P(None, None, 'tensor'), may hold values from -1.5 to 1.5
- w_out: bfloat16 [2, 1024, 1024], P(None, 'tensor'), may hold values from -2 to 2
- b_out: bfloat16 [2, 1024], replicated, may hold values from -1.5 to 1.5
- w_fc: bfloat16 [2, 1024, 4096], P(None, None, 'tensor'), may hold values from -0.1875 to 0.1875
- b_fc: bfloat16 [2, 4096], P(None, 'tensor'), may hold values from -2.5 to 2.5
- w_proj: bfloat16 [2, 4096, 1024], P(None, 'tensor'), may hold values from -0.09375 to 0.09375
- b_proj: bfloat16 [2, 1024], replicated, may hold values from -1.5 to 1.5
- cotangent: bfloat16 [2048, 1024], P('dp'), may hold values from -6 to 6
Outputs:
- out: float32 [2048, 1024], P('dp')
- grad_input: float32 [2048, 1024], P('dp')
- g_norm_gain: float32 [2, 2, 1024], replicated
- g_norm_bias: float32 [2, 2, 1024], replicated
- g_w_qkv: float32 [2, 1024, 3, 1024], P(None, None, None, 'tensor')
- g_b_qv: float32 [2, 2, 1024], P(None, None, 'tensor')
- g_w_out: float32 [2, 1024, 1024], P(None, 'tensor')
- g_b_out: float32 [2, 1024], replicated
- g_w_fc: float32 [2, 1024, 4096], P(None, None, 'tensor')
- g_b_fc: float32 [2, 4096], P(None, 'tensor')
- g_w_proj: float32 [2, 4096, 1024], P(None, 'tensor')
- g_b_proj: float32 [2, 1024], replicated
Inputs may be any that keep to these rules, and one draw needn't show every extreme that they name: `segment_ids`: never falling along the tokens; segment 1 holds token 127 and token 1920; segments 0 and 2 each hold 1 to 127 tokens.
All inputs are finite; a program needn't handle non-finite values.
Results may differ from a plain program's by a relative error of at most 0.023.
Values may be sent and summed in bfloat16 or wider, within the bound.
No kernel may reach another device: no remote copies, remote signals or barrier semaphores. Data moves between devices by JAX's collectives and lax.ppermute only.
A program may use at most 128 MiB of HBM per device.

v0:
```python
import functools

import jax
import jax.numpy as jnp
from jax import lax
from jax.experimental import pallas as pl
from jax.experimental.pallas import tpu as pltpu
from jax.sharding import PartitionSpec as P

HD = 64
F32 = jnp.float32
BF16 = jnp.bfloat16
ROOT = 0.7978845608028654
CUBE = 0.044715


def dot(left, right):
    return jnp.dot(left, right, preferred_element_type=F32)


def dot_t(left, right):
    return lax.dot_general(left, right, (((1,), (1,)), ((), ())), preferred_element_type=F32)


def norm_parts(value):
    mean = jnp.mean(value, -1, keepdims=True)
    centered = value - mean
    spread = jnp.mean(centered * centered, -1, keepdims=True)
    factor = lax.rsqrt(spread + 1e-05)
    return centered * factor, factor


def tanh_part(value):
    return jnp.tanh(ROOT * (value + CUBE * value * value * value))


def gelu(value):
    return 0.5 * value * (1.0 + tanh_part(value))


def gelu_slope(value):
    bend = tanh_part(value)
    inner = ROOT * (1.0 + 3.0 * CUBE * value * value)
    return 0.5 * (1.0 + bend) + 0.5 * value * (1.0 - bend * bend) * inner


def call(kernel, outs, layered, *args, room=12, blocks={}):
    layer, wide = layered
    near = NEAR.get(kernel, ())
    args = [
        arg if index in near or arg.shape == (1,) else pltpu.with_memory_space_constraint(arg, pltpu.HBM)
        for index, arg in enumerate(args)
    ]

    def spec(index, arg):
        if arg.dtype == jnp.int32 and arg.shape == (1,):
            return pl.BlockSpec(memory_space=pltpu.SMEM)
        if index in blocks:
            return pl.BlockSpec(*blocks[index])
        if index in wide:
            rest = arg.shape[1:]
            return pl.BlockSpec((None,) + rest, lambda i: (layer,) + (0,) * len(rest))
        return pl.BlockSpec(arg.shape, lambda i: (0,) * arg.ndim)

    return pl.pallas_call(
        kernel,
        grid=(1,),
        in_specs=[spec(index, arg) for index, arg in enumerate(args)],
        out_specs=[pl.BlockSpec(out.shape, lambda i, n=len(out.shape): (0,) * n) for out in outs],
        out_shape=[pltpu.HBM(out.shape, out.dtype) for out in outs],
        cost_estimate=pl.CostEstimate(flops=1000, bytes_accessed=1000, transcendentals=0),
        compiler_params=pltpu.CompilerParams(vmem_limit_bytes=room * 1024 * 1024),
    )(*args)


def shape(dims, kind):
    return jax.ShapeDtypeStruct(dims, kind)


def project(a_low, w_ref, bias_ref, q_ref, kv_ref, all_ref):
    q_ref[...] = (dot(a_low, w_ref[0]) + bias_ref[0:1].astype(F32)).astype(BF16)
    k_low = dot(a_low, w_ref[1]).astype(BF16)
    v_low = (dot(a_low, w_ref[2]) + bias_ref[1:2].astype(F32)).astype(BF16)
    local = k_low.shape[1]
    kv_ref[:, :local] = k_low
    kv_ref[:, local:] = v_low
    for index in range(all_ref.shape[0]):
        all_ref[index, :, :local] = k_low
        all_ref[index, :, local:] = v_low


def first_kernel(x_ref, gain_ref, shift_ref, w_ref, bias_ref, a_ref, q_ref, kv_ref, all_ref):
    normed, _ = norm_parts(x_ref[...].astype(F32))
    a_low = (normed * gain_ref[...] + shift_ref[...]).astype(BF16)
    a_ref[...] = a_low
    project(a_low, w_ref, bias_ref, q_ref, kv_ref, all_ref)


def project_kernel(a_ref, w_ref, bias_ref, q_ref, kv_ref, all_ref):
    project(a_ref[...], w_ref, bias_ref, q_ref, kv_ref, all_ref)


def head_masks(rows, local):
    column = lax.broadcasted_iota(jnp.int32, (rows, local), 1)
    return [column < HD, column >= HD]


def only(mask, value):
    return jnp.where(mask, value.astype(F32), 0.0).astype(BF16)


def allowed_of(start_ref, own_ref, all_ref, own_is_query):
    own_spot = start_ref[0] + lax.broadcasted_iota(jnp.int32, own_ref.shape, 0)
    spots = lax.broadcasted_iota(jnp.int32, all_ref.shape, 1)
    order = spots <= own_spot if own_is_query else spots >= own_spot
    return (all_ref[...] == own_ref[...]) & order


def attend_kernel(start_ref, own_ref, all_ref, q_ref, kv_ref, w_ref, o_ref, low_ref, log_ref, part_ref):
    rows, local = q_ref.shape
    total = all_ref.shape[1]
    keys = kv_ref[:, :, :local].reshape(total, local)
    values = kv_ref[:, :, local:].reshape(total, local)
    allowed = allowed_of(start_ref, own_ref, all_ref, True)
    queries = q_ref[...].astype(F32) * HD ** (-0.5)
    masks = head_masks(rows, local)
    outs, logs = [], []
    for mask in masks:
        scores = jnp.where(allowed, dot_t(only(mask, queries), keys), -1e30)
        top = jnp.max(scores, -1, keepdims=True)
        expd = jnp.exp(scores - top)
        denom = jnp.sum(expd, -1, keepdims=True)
        outs.append(dot((expd * (1.0 / denom)).astype(BF16), values))
        logs.append(top + jnp.log(denom))
    attended = jnp.where(masks[0], outs[0], outs[1])
    o_low = attended.astype(BF16)
    o_ref[...] = attended
    low_ref[...] = o_low
    log_ref[...] = jnp.where(masks[0], logs[0], logs[1])
    part_ref[...] = dot(o_low, w_ref[...]).astype(BF16).reshape(part_ref.shape)


def sum_parts(ref, start, rows):
    total = ref[0, start : start + rows].astype(F32)
    for index in range(1, ref.shape[0]):
        total = total + ref[index, start : start + rows].astype(F32)
    return total


def row_kernel(parts_ref, state_ref, bias_ref, gain_ref, shift_ref, state_out, normed_ref, factor_ref, sent_ref):
    state = state_ref[...] + (sum_parts(parts_ref, 0, state_ref.shape[0]) + bias_ref[...])
    normed, factor = norm_parts(state)
    low = (normed * gain_ref[...] + shift_ref[...]).astype(BF16)
    state_out[...] = state
    normed_ref[...] = normed
    factor_ref[...] = jnp.broadcast_to(factor, factor_ref.shape)
    for index in range(sent_ref.shape[0]):
        sent_ref[index] = low


def forward_kernel(b_ref, fc_ref, bias_ref, proj_ref, pre_ref, h_ref, part_ref):
    pre = dot(b_ref[...], fc_ref[...]) + bias_ref[...].astype(F32)
    h_low = gelu(pre).astype(BF16)
    pre_ref[...] = pre
    h_ref[...] = h_low
    part_ref[...] = dot(h_low, proj_ref[...]).astype(BF16).reshape(part_ref.shape)


def turn_kernel(b_ref, fc_ref, bias_ref, proj_ref, g_ref, h_ref, gf_ref, part_ref):
    share = part_ref.shape[1] // 2
    pre = dot(b_ref[...], fc_ref[...]) + bias_ref[...].astype(F32)
    h_low = gelu(pre).astype(BF16)
    h_ref[...] = h_low
    parts = dot(h_low, proj_ref[...]).astype(BF16)
    part_ref[:, :share] = parts.reshape(-1, share, parts.shape[1])
    g_f = (dot_t(g_ref[...], proj_ref[...]) * gelu_slope(pre)).astype(BF16)
    gf_ref[...] = g_f
    parts = dot_t(g_f, fc_ref[...]).astype(BF16)
    part_ref[:, share:] = parts.reshape(-1, share, parts.shape[1])


def backward_kernel(g_ref, pre_ref, fc_ref, proj_ref, gf_ref, part_ref):
    g_f = (dot_t(g_ref[...], proj_ref[...]) * gelu_slope(pre_ref[...])).astype(BF16)
    gf_ref[...] = g_f
    part_ref[...] = dot_t(g_f, fc_ref[...]).astype(BF16).reshape(part_ref.shape)


def norm_back(d_value, normed_ref, factor_ref, gain_ref, grad_ref, sums_ref):
    normed = normed_ref[...]
    scaled = d_value * gain_ref[...]
    back = factor_ref[:, 0:1] * (
        scaled
        - jnp.mean(scaled, -1, keepdims=True)
        - normed * jnp.mean(scaled * normed, -1, keepdims=True)
    )
    sums_ref[0:1] = jnp.sum(d_value * normed, 0, keepdims=True)
    sums_ref[1:2] = jnp.sum(d_value, 0, keepdims=True)
    return grad_ref[...] + back


def back_kernel(parts_ref, normed_ref, factor_ref, gain_ref, grad_ref, grad_out, sums_ref, sent_ref):
    share = normed_ref.shape[0]
    grad = norm_back(sum_parts(parts_ref, 0, share), normed_ref, factor_ref, gain_ref, grad_ref, sums_ref)
    grad_out[...] = grad
    low = grad.astype(BF16)
    for index in range(sent_ref.shape[0]):
        sent_ref[index] = low


def turn_back_kernel(
    parts_ref, state_ref, bias_ref, normed_ref, factor_ref, gain_ref, grad_ref, grad_out, sums_ref, sent_ref
):
    share = normed_ref.shape[0]
    out = (state_ref[...] + (sum_parts(parts_ref, 0, share) + bias_ref[...])).astype(BF16)
    grad = norm_back(sum_parts(parts_ref, share, share), normed_ref, factor_ref, gain_ref, grad_ref, sums_ref)
    grad_out[...] = grad
    low = grad.astype(BF16)
    for index in range(sent_ref.shape[0]):
        sent_ref[index, :share] = low
        sent_ref[index, share:] = out


def two_terms(value):
    high = value.astype(BF16).astype(F32)
    return high, value - high


def output_back_kernel(gy_ref, w_ref, o_ref, log_ref, go_ref, delta_ref, sent_ref):
    rows, local = o_ref.shape
    g_o = dot_t(gy_ref[...].reshape(rows, -1), w_ref[...]).astype(BF16)
    go_ref[...] = g_o
    masks = head_masks(rows, local)
    product = g_o.astype(F32) * o_ref[...]
    deltas = [jnp.sum(jnp.where(mask, product, 0.0), -1, keepdims=True) for mask in masks]
    delta = jnp.where(masks[0], deltas[0], deltas[1])
    delta_ref[...] = delta
    rows_of = []
    for value in (log_ref[...], delta):
        turned = value.T
        high, rest = two_terms(jnp.concatenate((turned[0:1], turned[HD : HD + 1]), 0))
        rows_of += [high, rest]
    rows_of.append(jnp.zeros((8, local), F32))
    extra = jnp.concatenate(rows_of, 0).astype(BF16)
    for index in range(sent_ref.shape[0]):
        sent_ref[index, :rows] = g_o
        sent_ref[index, rows:] = extra


def query_back_kernel(start_ref, own_ref, all_ref, q_ref, kv_ref, go_ref, log_ref, delta_ref, gq_ref):
    rows, local = q_ref.shape
    total = all_ref.shape[1]
    keys = kv_ref[:, :, :local].reshape(total, local)
    values = kv_ref[:, :, local:].reshape(total, local)
    allowed = allowed_of(start_ref, own_ref, all_ref, True)
    queries = q_ref[...].astype(F32) * HD ** (-0.5)
    masks = head_masks(rows, local)
    outs = []
    for head, mask in enumerate(masks):
        at = slice(head * HD, head * HD + 1)
        scores = jnp.where(allowed, dot_t(only(mask, queries), keys), -1e30)
        probs = jnp.exp(scores - log_ref[:, at])
        d_probs = dot_t(only(mask, go_ref[...]), values)
        g_s = (probs * (d_probs - delta_ref[:, at])).astype(BF16)
        outs.append(dot(g_s, keys))
    gq_ref[...] = (jnp.where(masks[0], outs[0], outs[1]) * HD ** (-0.5)).astype(BF16)


def key_back_kernel(start_ref, own_ref, all_ref, kv_ref, q_ref, got_ref, gq_ref, w_ref, gkv_ref, part_ref):
    rows, twice = kv_ref.shape
    local = twice // 2
    total = all_ref.shape[1]
    allowed = allowed_of(start_ref, own_ref, all_ref, False)
    queries = q_ref[...]
    g_o = got_ref[:, :rows].reshape(total, local)
    extra = got_ref[:, rows:].astype(F32)
    keys = kv_ref[:, :local].astype(F32) * HD ** (-0.5)
    values = kv_ref[:, local:]
    masks = head_masks(rows, local)
    d_keys, d_values = [], []
    for head, mask in enumerate(masks):

        def row_of(base):
            row = extra[:, base + head : base + head + 1] + extra[:, base + 2 + head : base + 3 + head]
            return jnp.concatenate([row[index] for index in range(row.shape[0])], 1)

        scores = jnp.where(allowed, dot_t(only(mask, keys), queries), -1e30)
        probs = jnp.exp(scores - row_of(0))
        d_probs = dot_t(only(mask, values), g_o)
        g_s = (probs * (d_probs - row_of(4))).astype(BF16)
        d_keys.append(dot(g_s, queries))
        d_values.append(dot(probs.astype(BF16), g_o))
    g_k = (jnp.where(masks[0], d_keys[0], d_keys[1]) * HD ** (-0.5)).astype(BF16)
    g_v = jnp.where(masks[0], d_values[0], d_values[1]).astype(BF16)
    gkv_ref[:, :local] = g_k
    gkv_ref[:, local:] = g_v
    part = dot_t(gq_ref[...], w_ref[0]) + dot_t(g_k, w_ref[1]) + dot_t(g_v, w_ref[2])
    part_ref[...] = part.astype(BF16).reshape(part_ref.shape)


def end_grads_kernel(h_ref, gm_ref, b_ref, gf_ref, pack_ref, gm_sum, gf_sum):
    g_m, g_f = gm_ref[...], gf_ref[...]
    hidden = g_f.shape[1]
    pack_ref[:hidden] = cross(h_ref[...], g_m).astype(BF16)
    g_w_fc = cross(b_ref[...], g_f).astype(BF16)
    for block in range(g_w_fc.shape[0] // hidden):
        at = slice(block * hidden, (block + 1) * hidden)
        pack_ref[hidden:, at] = g_w_fc[at]
    gm_sum[...] = jnp.sum(g_m.astype(F32), 0, keepdims=True)
    gf_sum[...] = jnp.sum(g_f.astype(F32), 0, keepdims=True)


def attend_grads_kernel(o_ref, gy_ref, a_ref, gq_ref, gkv_ref, pack_ref, gy_sum, gq_sum, gv_sum):
    local = gq_ref.shape[1]
    g_y = gy_ref[...].reshape(-1, gy_ref.shape[-1])
    a_low = a_ref[...]
    g_q, g_k, g_v = gq_ref[...], gkv_ref[:, :local], gkv_ref[:, local:]
    pack_ref[:local] = cross(o_ref[...], g_y).astype(BF16)
    for index, grad in enumerate((g_q, g_k, g_v)):
        product = cross(a_low, grad).astype(BF16)
        for block in range(product.shape[0] // local):
            at = slice(block * local, (block + 1) * local)
            pack_ref[(index + 1) * local : (index + 2) * local, at] = product[at]
    gy_sum[...] = jnp.sum(g_y.astype(F32), 0, keepdims=True)
    gq_sum[...] = jnp.sum(g_q.astype(F32), 0, keepdims=True)
    gv_sum[...] = jnp.sum(g_v.astype(F32), 0, keepdims=True)


def finish_end_kernel(side_ref, p_own, p_got, f_own, f_got, own_ref, got_ref, proj_ref, fc_ref):
    side = side_ref[0]
    half = p_own.shape[0]
    hidden = fc_ref.shape[2]

    def pick(own, got, index):
        return jnp.where(side == index, own[...].astype(F32), got[...].astype(F32))

    for index in range(2):
        rows = slice(index * half, (index + 1) * half)
        proj_ref[0, rows] = pick(p_own, p_got, index)
        packed = pick(f_own, f_got, index)
        for block in range(fc_ref.shape[1] // hidden):
            at = block * hidden + index * half
            fc_ref[0, at : at + half] = packed[:, block * hidden : (block + 1) * hidden]
    proj_ref[1] = pick(own_ref, got_ref, 0)
    packed = pick(own_ref, got_ref, 1)
    for block in range(fc_ref.shape[1] // hidden):
        at = slice(block * hidden, (block + 1) * hidden)
        fc_ref[1, at] = packed[:, at]


def finish_attend_kernel(side_ref, late_own, late_got, own_ref, got_ref, out_ref, qkv_ref):
    side = side_ref[0]
    local, width = out_ref.shape[1:]

    def put(layer, row, value):
        count = value.shape[0]
        if row < local:
            out_ref[layer, row : row + count] = value
        else:
            index, at = row // local - 1, row % local
            for block in range(width // local):
                base = block * local + at
                qkv_ref[layer, index, base : base + count] = value[:, block * local : (block + 1) * local]

    half = own_ref.shape[0]
    for index in range(2):
        picked = jnp.where(side == index, own_ref[...].astype(F32), got_ref[...].astype(F32))
        for row in range(0, half, local):
            put(1, index * half + row, picked[row : row + local])
        for chip in range(late_own.shape[0]):
            picked = jnp.where(side == index, late_own[chip].astype(F32), late_got[chip].astype(F32))
            for group in range(4):
                row = index * half + chip * 32 + group * 8
                put(0, row, picked[:, group * width : (group + 1) * width])


NEAR = {
    project_kernel: (0,),
    attend_kernel: (4,),
    row_kernel: (0,),
    forward_kernel: (0,),
    turn_kernel: (0,),
    turn_back_kernel: (0,),
    back_kernel: (0,),
    backward_kernel: (0,),
    output_back_kernel: (0,),
    query_back_kernel: (4,),
    key_back_kernel: (5,),
    end_grads_kernel: (1, 2),
    attend_grads_kernel: (1, 2),
}


def swap_all(value, axis):
    return lax.all_to_all(value, axis, 0, 0)


def cross(left, right):
    return lax.dot_general(left, right, (((0,), (0,)), ((), ())), preferred_element_type=F32)


CORE, DEPTH = 1, 2


def side_of(flip):
    return (lax.axis_index("dp") // flip) % 2


def swap(value, flip):
    return lax.ppermute(value, "dp", [(i, i ^ flip) for i in range(lax.axis_size("dp"))])


def after(value, event):
    return lax.optimization_barrier((value, event))[0]


def halve(value, flip, event=None, side=None):
    halves = value.reshape((2, value.shape[0] // 2) + value.shape[1:])
    side = side_of(flip) if side is None else side
    mine = lax.dynamic_index_in_dim(halves, side, 0, keepdims=False)
    got = swap(lax.dynamic_index_in_dim(halves, 1 - side, 0, keepdims=False), flip)
    got = got if event is None else after(got, event)
    return (mine.astype(F32) + got.astype(F32)).astype(BF16)


def rejoin(value, flip, side=None, event=None):
    got = swap(value, flip)
    got = got if event is None else after(got, event)
    side = side_of(flip) if side is None else side
    return jnp.concatenate((jnp.where(side, got, value), jnp.where(side, value, got)), 0)


def finish_sums(value, turn, events):
    place = lax.axis_index("dp")
    x_low, x_high = (place // 4) % 2, place // 8
    steps = ((4, x_low ^ x_high), (12, x_high)) if turn else ((12, x_high), (4, x_low ^ x_high))
    for (flip, side), event in zip(steps, events):
        value = halve(value, flip, event, side)
    for flip, side in steps[::-1]:
        value = rejoin(value, flip, side)
    value = rejoin(after(value, events[-1]), DEPTH)
    return value, swap(value, CORE)


def sum_over_x(values):
    groups = [[4 * x + rest for x in range(lax.axis_size("dp") // 4)] for rest in range(4)]
    return lax.psum(values, "dp", axis_index_groups=groups)


def swap_chips(value):
    groups = [[2 * chip + core for chip in range(lax.axis_size("dp") // 2)] for core in range(2)]
    return lax.all_to_all(value, "dp", 0, 0, axis_index_groups=groups)


def body(
    tokens,
    segment_ids,
    norm_gain,
    norm_bias,
    w_qkv,
    b_qv,
    w_out,
    b_out,
    w_fc,
    b_fc,
    w_proj,
    b_proj,
    cotangent,
):
    rows, width = tokens.shape
    total = segment_ids.shape[0]
    layers = w_qkv.shape[0]
    local = w_qkv.shape[3]
    hidden = w_fc.shape[2]
    ranks, slots = lax.axis_size("dp"), lax.axis_size("tensor")
    share = rows // slots
    first = (lax.axis_index("dp") * rows).astype(jnp.int32)
    own = lax.axis_index("tensor") * share
    start = first.reshape(1)
    seg_own = lax.dynamic_slice_in_dim(segment_ids, first, rows).reshape(rows, 1)
    seg_all = segment_ids.reshape(1, total)
    spots = (start, seg_own, seg_all)
    gains = norm_gain.astype(F32).reshape(layers, 2, 1, width)
    shifts = norm_bias.astype(F32).reshape(layers, 2, 1, width)
    out_bias = b_out.astype(F32).reshape(layers, 1, width)
    end_bias = b_proj.astype(F32).reshape(layers, 1, width)
    w_three = w_qkv.transpose(0, 2, 1, 3)
    fc_bias = b_fc.reshape(layers, 1, hidden)
    state = lax.dynamic_slice_in_dim(tokens, own, share).astype(F32)
    a_normed, a_factor = norm_parts(state)
    a_factor = jnp.broadcast_to(a_factor, (share, 128))
    row_block = shape((share, width), F32)
    row_stat = shape((share, 128), F32)
    exchange = shape((slots, share, width), BF16)
    saved = []
    qkv_shapes = [
        shape((rows, local), BF16),
        shape((rows, 2 * local), BF16),
        shape((ranks, rows, 2 * local), BF16),
    ]
    a_low = None
    for layer in range(layers):
        if layer:
            q_low, kv_own, kv_sent = call(project_kernel, qkv_shapes, (layer, (1, 2)), a_low, w_three, b_qv)
        else:
            a_low, q_low, kv_own, kv_sent = call(
                first_kernel,
                [shape((rows, width), BF16)] + qkv_shapes,
                (layer, (3, 4)),
                tokens,
                gains[0, 0],
                shifts[0, 0],
                w_three,
                b_qv,
            )
        kv_all = swap_all(kv_sent, "dp")
        o_full, o_low, logs, attn_parts = call(
            attend_kernel,
            [shape((rows, local), F32), shape((rows, local), BF16), shape((rows, local), F32), exchange],
            (layer, (5,)),
            *spots,
            q_low,
            kv_all,
            w_out,
            room=24,
        )
        middle, b_normed, b_factor, b_sent = call(
            row_kernel,
            [row_block, row_block, row_stat, exchange],
            (layer, ()),
            swap_all(attn_parts, "tensor"),
            state,
            out_bias[layer],
            gains[layer, 1],
            shifts[layer, 1],
        )
        b_low = swap_all(b_sent, "tensor").reshape(rows, width)
        kept = [a_normed, a_factor, a_low, q_low, kv_own, kv_all, o_full, o_low, logs, b_normed, b_factor, b_low]
        if layer < layers - 1:
            pre, h_low, parts = call(
                forward_kernel,
                [shape((rows, hidden), F32), shape((rows, hidden), BF16), exchange],
                (layer, (1, 2, 3)),
                b_low,
                w_fc,
                fc_bias,
                w_proj,
            )
            state, a_normed, a_factor, a_sent = call(
                row_kernel,
                [row_block, row_block, row_stat, exchange],
                (layer, ()),
                swap_all(parts, "tensor"),
                middle,
                end_bias[layer],
                gains[layer + 1, 0],
                shifts[layer + 1, 0],
            )
            a_low = swap_all(a_sent, "tensor").reshape(rows, width)
            kept += [pre, h_low]
        saved.append(kept)
    q_every = lax.all_gather(jnp.concatenate([kept[3] for kept in saved], 1), "dp", axis=0, tiled=True)
    g_m = cotangent
    grad = lax.dynamic_slice_in_dim(cotangent, own, share).astype(F32)
    done = [None] * layers
    smalls, sums = [], []
    two_rows = shape((2, width), F32)
    out = None
    def end_grads(layer, h_low, g_m, b_low, g_f):
        return call(
            end_grads_kernel,
            [shape((2 * hidden, width), BF16), shape((1, width), F32), shape((1, hidden), F32)],
            (layer, ()),
            h_low,
            g_m,
            b_low,
            g_f,
            room=16,
        )

    for layer in reversed(range(layers)):
        a_normed, a_factor, a_low, q_low, kv_own, kv_all, o_full, o_low, logs, b_normed, b_factor, b_low = (
            saved[layer][:12]
        )
        if layer == layers - 1:
            double = shape((slots, 2 * share, width), BF16)
            h_low, g_f, parts = call(
                turn_kernel,
                [shape((rows, hidden), BF16), shape((rows, hidden), BF16), double],
                (layer, (1, 2, 3)),
                b_low,
                w_fc,
                fc_bias,
                w_proj,
                g_m,
            )
            grad, sums_b, sent = call(
                turn_back_kernel,
                [row_block, two_rows, double],
                (layer, ()),
                swap_all(parts, "tensor"),
                middle,
                end_bias[layer],
                b_normed,
                b_factor,
                gains[layer, 1],
                grad,
            )
            got = swap_all(sent, "tensor")
            g_y = got
            out = got[:, share:].reshape(rows, width).astype(F32)
        else:
            pre, h_low = saved[layer][12:]
            g_f, parts = call(
                backward_kernel,
                [shape((rows, hidden), BF16), exchange],
                (layer, (2, 3)),
                g_m,
                pre,
                w_fc,
                w_proj,
            )
            end_pack, gm_sum, gf_sum = end_grads(layer, h_low, g_m, b_low, g_f)
            grad, sums_b, sent = call(
                back_kernel,
                [row_block, two_rows, exchange],
                (layer, ()),
                swap_all(parts, "tensor"),
                b_normed,
                b_factor,
                gains[layer, 1],
                grad,
            )
            g_y = swap_all(sent, "tensor")
        grad_b = grad
        g_o, delta, sent = call(
            output_back_kernel,
            [shape((rows, local), BF16), shape((rows, local), F32), shape((ranks, rows + 16, local), BF16)],
            (layer, (1,)),
            g_y,
            w_out,
            o_full,
            logs,
            blocks={0: ((slots, share, width), lambda i: (0, 0, 0))},
        )
        if not layer:
            starts = [
                halve(halve(part, CORE), DEPTH) for part in (end_pack[:hidden], end_pack[hidden:])
            ]
            sent, starts = lax.optimization_barrier((sent, starts))
        go_all = swap_all(sent, "dp")
        (g_q,) = call(
            query_back_kernel,
            [shape((rows, local), BF16)],
            (layer, ()),
            *spots,
            q_low,
            kv_all,
            g_o,
            logs,
            delta,
            room=24,
        )
        g_kv, parts = call(
            key_back_kernel,
            [shape((rows, 2 * local), BF16), exchange],
            (layer, (7,)),
            *spots,
            kv_own,
            q_every,
            go_all,
            g_q,
            w_three,
            room=24,
            blocks={4: ((total, local), lambda i: (0, layer))},
        )
        grad, sums_a, sent = call(
            back_kernel,
            [row_block, two_rows, exchange],
            (layer, ()),
            swap_all(parts, "tensor"),
            a_normed,
            a_factor,
            gains[layer, 0],
            grad,
        )
        sums = [sums_a, sums_b] + sums
        if layer:
            end_pack, gm_sum, gf_sum = end_grads(layer, h_low, g_m, b_low, g_f)
        attend_pack, gy_sum, gq_sum, gv_sum = call(
            attend_grads_kernel,
            [
                shape((4 * local, width), BF16),
                shape((1, width), F32),
                shape((1, local), F32),
                shape((1, local), F32),
            ],
            (layer, ()),
            o_low,
            g_y,
            a_low,
            g_q,
            g_kv,
            room=16,
            blocks={1: ((slots, share, width), lambda i: (0, 0, 0))},
        )
        smalls = [gy_sum, gm_sum, gq_sum, gv_sum, gf_sum] + smalls
        if layer:
            g_m = swap_all(sent, "tensor").reshape(rows, width)
            end_part = halve(halve(end_pack, CORE, go_all), DEPTH, grad)
            attend_part = halve(halve(attend_pack, CORE), DEPTH, g_m)
            done[layer] = sum_over_x((end_part, attend_part))
    tail = jnp.concatenate([sent, jnp.broadcast_to(jnp.concatenate(sums, 0).astype(BF16), (slots, 8, width))], 1)
    tail_got = got = swap_all(tail, "tensor")
    grad_input = got[:, :share].reshape(rows, width).astype(F32)
    norm_sums = jnp.sum(got[:, share:].astype(F32), 0)
    small = jnp.concatenate([norm_sums.reshape(-1)] + [part.reshape(-1) for part in smalls])
    each = small.size // (8 * ranks)
    wide = 4 * width
    packed = jnp.concatenate(
        (
            attend_pack.reshape(ranks, 4, 8, width).transpose(0, 2, 1, 3).reshape(ranks, 8, wide),
            jnp.pad(small.astype(BF16).reshape(ranks, 8, each), ((0, 0), (0, 0), (0, 128 - each))),
        ),
        2,
    )
    half = halve(packed, CORE)
    arrived = swap_chips(half)
    mine = jnp.sum(arrived.astype(F32), 0).astype(BF16)
    late = swap_chips(jnp.broadcast_to(mine, (ranks // 2,) + mine.shape))
    late_got = swap(late, CORE)
    events = (g_kv, grad, half)
    end_parts = [part for turn, value in enumerate(starts) for part in finish_sums(value, turn, events)]
    end_last, attend_last = [rejoin(after(part, grad), DEPTH, None, half) for part in done[1]]
    side = side_of(CORE)
    sides = side.astype(jnp.int32).reshape(1)
    g_w_proj, g_w_fc = call(
        finish_end_kernel,
        [shape((layers, hidden, width), F32), shape((layers, width, hidden), F32)],
        (0, ()),
        sides,
        *end_parts,
        end_last,
        swap(end_last, CORE),
        room=40,
    )
    g_w_out, g_w_qkv = call(
        finish_attend_kernel,
        [shape((layers, local, width), F32), shape((layers, 3, width, local), F32)],
        (0, ()),
        sides,
        late,
        late_got,
        attend_last,
        swap(attend_last, CORE),
        room=24,
    )
    ours, theirs = late[:, :, wide : wide + each], late_got[:, :, wide : wide + each]
    small = jnp.concatenate((jnp.where(side, theirs, ours), jnp.where(side, ours, theirs)), 0)
    small = small.reshape(-1).astype(F32)
    norm_grads = small[: 8 * width].reshape(layers, 2, 2, width)
    per_layer = small[8 * width :].reshape(layers, -1)
    cut = 2 * width

    return (
        out,
        grad_input,
        norm_grads[:, :, 0],
        norm_grads[:, :, 1],
        g_w_qkv.transpose(0, 2, 1, 3),
        per_layer[:, cut : cut + 2 * local].reshape(layers, 2, local),
        g_w_out,
        per_layer[:, :width],
        g_w_fc,
        per_layer[:, cut + 2 * local :],
        g_w_proj,
        per_layer[:, width:cut],
    )


def solution(mesh):
    in_specs = (
        P("dp", None),
        P(),
        P(),
        P(),
        P(None, None, None, "tensor"),
        P(None, None, "tensor"),
        P(None, "tensor", None),
        P(),
        P(None, None, "tensor"),
        P(None, "tensor"),
        P(None, "tensor", None),
        P(),
        P("dp", None),
    )
    out_specs = (
        P("dp", None),
        P("dp", None),
        P(),
        P(),
        P(None, None, None, "tensor"),
        P(None, None, "tensor"),
        P(None, "tensor", None),
        P(),
        P(None, None, "tensor"),
        P(None, "tensor"),
        P(None, "tensor", None),
        P(),
    )
    return jax.shard_map(body, mesh=mesh, in_specs=in_specs, out_specs=out_specs, check_vma=False)
```

profile of v0, /device:TPU:1, one launch (start us, length us, event | category | flops | bytes accessed | tf_op | source)
XLA Modules:
  0.0 421.0 jit_solution(4071000829075161680)
XLA Ops:
  9.2 2.9 shard_map.220
  12.1 9.3 %all-to-all-start = ((bf16[16,128,256]{2,1,0:T(8,128)(2,1)}), bf16[16,128,256]{2,1,0:T(8,128)(2,1)S(1)}, u32[]{:S(2)}, u32[]{:S(2)}) async-start(bf16[16,128,256]{2,1,0:T(8,128)(2,1)} %get-tuple-element.104), calls=%async_computation | async-start | bytes 2097152 | tf_op jit(solution)/shard_map/all_to_all | solution.py:394
  22.9 15.7 %all-to-all-done.kv_ref = bf16[16,128,256]{2,1,0:T(8,128)(2,1)S(1)} async-done(((bf16[16,128,256]{2,1,0:T(8,128)(2,1)}), bf16[16,128,256]{2,1,0:T(8,128)(2,1)S(1)}, u32[]{:S(2)}, u32[]{:S(2)}) %all-to-all-start) | async-done | bytes 1048608 | tf_op jit(solution)/shard_map/all_to_all | solution.py:394
  38.6 3.6 shard_map.221
  42.2 4.7 %all-to-all-start.1 = ((bf16[8,16,1024]{2,1,0:T(8,128)(2,1)}), bf16[8,16,1024]{2,1,0:T(8,128)(2,1)S(1)}, u32[]{:S(2)}, u32[]{:S(2)}) async-start(bf16[8,16,1024]{2,1,0:T(8,128)(2,1)} %get-tuple-element.105), calls=%async_computation.1 | async-start | bytes 524288 | tf_op jit(solution)/shard_map/all_to_all | solution.py:394
  48.1 5.2 %all-to-all-done.1.parts_ref = bf16[8,16,1024]{2,1,0:T(8,128)(2,1)S(1)} async-done(((bf16[8,16,1024]{2,1,0:T(8,128)(2,1)}), bf16[8,16,1024]{2,1,0:T(8,128)(2,1)S(1)}, u32[]{:S(2)}, u32[]{:S(2)}) %all-to-all-start.1) | async-done | bytes 262176 | tf_op jit(solution)/shard_map/all_to_all | solution.py:394
  55.1 3.4 all-to-all-start.2
  59.2 5.5 %all-to-all-done.2 = bf16[8,16,1024]{2,1,0:T(8,128)(2,1)S(1)} async-done(((bf16[8,16,1024]{2,1,0:T(8,128)(2,1)}), bf16[8,16,1024]{2,1,0:T(8,128)(2,1)S(1)}, u32[]{:S(2)}, u32[]{:S(2)}) %all-to-all-start.2) | async-done | bytes 262176 | tf_op jit(solution)/shard_map/all_to_all | solution.py:394
  67.5 3.4 all-to-all-start.3
  71.5 5.5 %all-to-all-done.3.parts_ref = bf16[8,16,1024]{2,1,0:T(8,128)(2,1)S(1)} async-done(((bf16[8,16,1024]{2,1,0:T(8,128)(2,1)}), bf16[8,16,1024]{2,1,0:T(8,128)(2,1)S(1)}, u32[]{:S(2)}, u32[]{:S(2)}) %all-to-all-start.3) | async-done | bytes 262176 | tf_op jit(solution)/shard_map/all_to_all | solution.py:394
  78.8 9.5 %all_to_all.100 = bf16[8,16,1024]{2,1,0:T(8,128)(2,1)S(1)} all-to-all(bf16[8,16,1024]{2,1,0:T(8,128)(2,1)} %get-tuple-element.109), channel_id=1, replica_groups=mesh['tensor'=8,'dp'=16] {'tensor'}, dimensions={0} | all-to-all | bytes 524288 | tf_op jit(solution)/shard_map/all_to_all | solution.py:394
  90.9 26.5 %all_to_all.101.kv_ref = bf16[16,128,256]{2,1,0:T(8,128)(2,1)S(1)} all-to-all(bf16[16,128,256]{2,1,0:T(8,128)(2,1)} %get-tuple-element.111), channel_id=1, replica_groups=mesh['tensor'=8,'dp'=16] {'dp'}, dimensions={0} | all-to-all | bytes 2097152 | tf_op jit(solution)/shard_map/all_to_all | solution.py:394
  117.4 3.6 shard_map.226
  121.0 9.8 %all_to_all.102.parts_ref = bf16[8,16,1024]{2,1,0:T(8,128)(2,1)S(1)} all-to-all(bf16[8,16,1024]{2,1,0:T(8,128)(2,1)} %get-tuple-element.112), channel_id=1, replica_groups=mesh['tensor'=8,'dp'=16] {'tensor'}, dimensions={0} | all-to-all | bytes 524288 | tf_op jit(solution)/shard_map/all_to_all | solution.py:394
  132.6 9.5 %all_to_all.103 = bf16[8,16,1024]{2,1,0:T(8,128)(2,1)S(1)} all-to-all(bf16[8,16,1024]{2,1,0:T(8,128)(2,1)} %get-tuple-element.114), channel_id=1, replica_groups=mesh['tensor'=8,'dp'=16] {'tensor'}, dimensions={0} | all-to-all | bytes 524288 | tf_op jit(solution)/shard_map/all_to_all | solution.py:394
  142.2 3.8 shard_map.228
  146.0 4.1 all-to-all-start.8
  151.6 3.0 shard_map.243
  156.9 3.2 collective-permute-start.22
  162.2 5.4 %all-to-all-start.9 = ((bf16[8,32,1024]{2,1,0:T(8,128)(2,1)}), bf16[8,32,1024]{2,1,0:T(8,128)(2,1)S(1)}, u32[]{:S(2)}, u32[]{:S(2)}) async-start(bf16[8,32,1024]{2,1,0:T(8,128)(2,1)} %get-tuple-element.119), calls=%async_computation.9 | async-start | bytes 1048576 | tf_op jit(solution)/shard_map/all_to_all | solution.py:394
  167.9 10.1 %all-to-all-done.9.gy_ref = bf16[8,32,1024]{2,1,0:T(8,128)(2,1)S(1)} async-done(((bf16[8,32,1024]{2,1,0:T(8,128)(2,1)}), bf16[8,32,1024]{2,1,0:T(8,128)(2,1)S(1)}, u32[]{:S(2)}, u32[]{:S(2)}) %all-to-all-start.9) | async-done | bytes 524320 | tf_op jit(solution)/shard_map/all_to_all | solution.py:394
  180.1 4.7 %all-to-all-start.10 = ((bf16[16,144,128]{2,1,0:T(8,128)(2,1)}), bf16[16,144,128]{2,1,0:T(8,128)(2,1)}, u32[]{:S(2)}, u32[]{:S(2)}) async-start(bf16[16,144,128]{2,1,0:T(8,128)(2,1)} %get-tuple-element.124), calls=%async_computation.10 | async-start | bytes 1179648 | tf_op jit(solution)/shard_map/all_to_all | solution.py:394
  185.7 2.9 shard_map.231.gq_ref
  189.4 8.0 %all-to-all-done.10.got_ref = bf16[16,144,128]{2,1,0:T(8,128)(2,1)} async-done(((bf16[16,144,128]{2,1,0:T(8,128)(2,1)}), bf16[16,144,128]{2,1,0:T(8,128)(2,1)}, u32[]{:S(2)}, u32[]{:S(2)}) %all-to-all-start.10) | async-done | bytes 589856 | tf_op jit(solution)/shard_map/all_to_all | solution.py:394
  201.7 5.9 %all-gather.2.cloned.1.call-done.q_ref = bf16[2048,256]{1,0:T(8,128)(2,1)} async-done(((bf16[128,256]{1,0:T(8,128)(2,1)}), bf16[2048,256]{1,0:T(8,128)(2,1)}) %all-gather.2.cloned.1.call-update) | async-done | bytes 1048592 | tf_op jit(solution)/shard_map/all_gather | solution.py:561
  207.5 4.0 shard_map.232
  211.5 3.4 all-to-all-start.11
  224.1 3.4 all-to-all-start.12
  229.6 4.2 %all-to-all-done.12 = bf16[8,16,1024]{2,1,0:T(8,128)(2,1)S(1)} async-done(((bf16[8,16,1024]{2,1,0:T(8,128)(2,1)}), bf16[8,16,1024]{2,1,0:T(8,128)(2,1)S(1)}, u32[]{:S(2)}, u32[]{:S(2)}) %all-to-all-start.12) | async-done | bytes 262176 | tf_op jit(solution)/shard_map/all_to_all | solution.py:394
  233.9 3.2 shard_map.234
  237.1 3.4 all-to-all-start.13
  240.5 3.0 shard_map.237
  251.9 5.4 %all-to-all-start.14 = ((bf16[8,16,1024]{2,1,0:T(8,128)(2,1)}), bf16[8,16,1024]{2,1,0:T(8,128)(2,1)S(1)}, u32[]{:S(2)}, u32[]{:S(2)}) async-start(bf16[8,16,1024]{2,1,0:T(8,128)(2,1)} %get-tuple-element.137), calls=%async_computation.14 | async-start | bytes 524288 | tf_op jit(solution)/shard_map/all_to_all | solution.py:394
  270.9 3.7 collective-permute-done.1
  276.4 6.6 %all-to-all-start.15 = ((bf16[16,144,128]{2,1,0:T(8,128)(2,1)}), bf16[16,144,128]{2,1,0:T(8,128)(2,1)S(1)}, u32[]{:S(2)}, u32[]{:S(2)}) async-start(bf16[16,144,128]{2,1,0:T(8,128)(2,1)} %get-tuple-element.144), calls=%async_computation.15 | async-start | bytes 1179648 | tf_op jit(solution)/shard_map/all_to_all | solution.py:394
  294.7 3.9 shard_map.239
  298.6 4.5 %all-to-all-start.16 = ((bf16[8,16,1024]{2,1,0:T(8,128)(2,1)}), bf16[8,16,1024]{2,1,0:T(8,128)(2,1)S(1)}, u32[]{:S(2)}, u32[]{:S(2)}) async-start(bf16[8,16,1024]{2,1,0:T(8,128)(2,1)} %get-tuple-element.147), calls=%async_computation.16 | async-start | bytes 524288 | tf_op jit(solution)/shard_map/all_to_all | solution.py:394
  311.8 22.1 %all-reduce.4.cloned.1.call-done = (bf16[128,1024]{1,0:T(8,128)(2,1)}, bf16[256,1024]{1,0:T(8,128)(2,1)}) async-done(((bf16[128,1024]{1,0:T(8,128)(2,1)}, bf16[256,1024]{1,0:T(8,128)(2,1)}), (bf16[128,1024]{1,0:T(8,128)(2,1)}, bf16[256,1024]{1,0:T(8,128)(2,1)})) %all-reduce.4.cloned.1.call-update) | async-done | bytes 786448 | tf_op jit(solution)/shard_map/psum | solution.py:446
  334.0 2.9 collective-permute-start.24
  339.3 4.1 all-to-all-start.17
  352.5 5.9 %collective-permute-start.4 = (bf16[8,8,4224]{2,1,0:T(8,128)(2,1)S(1)}, bf16[8,8,4224]{2,1,0:T(8,128)(2,1)S(1)}, u32[]{:S(2)}, u32[]{:S(2)}) collective-permute-start(bf16[8,8,4224]{2,1,0:T(8,128)(2,1)S(1)} %fusion.7), channel_id=1, source_target_pairs={{0,1},{1,0},{2,3},{3,2},{4,5},{5,4},{6,7},{7,6},{8,9},{9,8},{10,11... | collective-permute-start | bytes 1622024 | tf_op jit(solution)/shard_map/ppermute | solution.py:409
  360.9 4.3 %all-to-all-start.18 = ((bf16[8,8,4224]{2,1,0:T(8,128)(2,1)}), bf16[8,8,4224]{2,1,0:T(8,128)(2,1)S(1)}, u32[]{:S(2)}, u32[]{:S(2)}) async-start(bf16[8,8,4224]{2,1,0:T(8,128)(2,1)} %fusion.1), calls=%async_computation.18 | async-start | bytes 1081344 | tf_op jit(solution)/shard_map/all_to_all | solution.py:451
  365.2 3.0 collective-permute-start.20
  370.7 9.2 %collective-permute-done.20 = bf16[128,1024]{1,0:T(8,128)(2,1)S(1)} collective-permute-done((bf16[128,1024]{1,0:T(8,128)(2,1)S(1)}, bf16[128,1024]{1,0:T(8,128)(2,1)S(1)}, u32[]{:S(2)}, u32[]{:S(2)}) %collective-permute-start.20) | collective-permute-done | bytes 262176 | tf_op jit(solution)/shard_map/ppermute | solution.py:409
  380.9 5.1 %all-to-all-start.19 = ((bf16[8,8,4224]{2,1,0:T(8,128)(2,1)}), bf16[8,8,4224]{2,1,0:T(8,128)(2,1)S(1)}, u32[]{:S(2)}, u32[]{:S(2)}) async-start(bf16[8,8,4224]{2,1,0:T(8,128)(2,1)} %broadcast_in_dim.15), calls=%async_computation.19 | async-start | bytes 1081344 | tf_op jit(solution)/shard_map/all_to_all | solution.py:451
  388.7 7.4 %all-to-all-done.19.late_own = bf16[8,8,4224]{2,1,0:T(8,128)(2,1)S(1)} async-done(((bf16[8,8,4224]{2,1,0:T(8,128)(2,1)}), bf16[8,8,4224]{2,1,0:T(8,128)(2,1)S(1)}, u32[]{:S(2)}, u32[]{:S(2)}) %all-to-all-start.19) | async-done | bytes 540704 | tf_op jit(solution)/shard_map/all_to_all | solution.py:451
  400.2 6.2 %shard_map.245 = (f32[2,512,1024]{2,1,0:T(8,128)}, f32[2,1024,512]{2,1,0:T(8,128)}) custom-call(s32[1]{0:T(128)} %bitcast.45.side_ref, bf16[256,1024]{1,0:T(8,128)(2,1)} %copy-done.10, bf16[256,1024]{1,0:T(8,128)(2,1)} %collective-permute-done.15.p_got, bf16[256,1024]{1,0:T(8,128)(2,1)} %copy-done.9, bf16[256,1024]{1,0:T(8,128)(2,1)} %collective-permute-done.21.f_got, ...), custom_call_target="tpu_custom_call" | custom-call | flops 1000 | bytes 1000 | tf_op jit(solution)/shard_map/pallas_call | solution.py:65
  410.5 3.7 shard_map.244
  (246 shorter events, 114.2 us)
Async XLA Ops:
  12.1 34.8 %copy-start.17 = (bf16[128,1024]{1,0:T(8,128)(2,1)S(1)}, bf16[128,1024]{1,0:T(8,128)(2,1)}, u32[]{:S(2)}) copy-start(bf16[128,1024]{1,0:T(8,128)(2,1)} %x_ref.1) | copy-start | bytes 786436
  12.1 35.4 %copy-start.22 = (bf16[2,1024]{1,0:T(2,128)(2,1)S(1)}, bf16[2,1024]{1,0:T(2,128)(2,1)}, u32[]{:S(2)}) copy-start(bf16[2,1024]{1,0:T(2,128)(2,1)} %param.20) | copy-start | bytes 12292
  12.1 26.5 %all-to-all-start = ((bf16[16,128,256]{2,1,0:T(8,128)(2,1)}), bf16[16,128,256]{2,1,0:T(8,128)(2,1)S(1)}, u32[]{:S(2)}, u32[]{:S(2)}) async-start(bf16[16,128,256]{2,1,0:T(8,128)(2,1)} %get-tuple-element.104), calls=%async_computation | async-start | bytes 2097152 | tf_op jit(solution)/shard_map/all_to_all | solution.py:394
  21.4 37.2 %copy-start.28 = (bf16[2,512]{1,0:T(2,128)(2,1)S(1)}, bf16[2,512]{1,0:T(2,128)(2,1)}, u32[]{:S(2)}) copy-start(bf16[2,512]{1,0:T(2,128)(2,1)} %param.22) | copy-start | bytes 6148
  42.2 11.1 %all-to-all-start.1 = ((bf16[8,16,1024]{2,1,0:T(8,128)(2,1)}), bf16[8,16,1024]{2,1,0:T(8,128)(2,1)S(1)}, u32[]{:S(2)}, u32[]{:S(2)}) async-start(bf16[8,16,1024]{2,1,0:T(8,128)(2,1)} %get-tuple-element.105), calls=%async_computation.1 | async-start | bytes 524288 | tf_op jit(solution)/shard_map/all_to_all | solution.py:394
  55.1 9.5 %all-to-all-start.2 = ((bf16[8,16,1024]{2,1,0:T(8,128)(2,1)}), bf16[8,16,1024]{2,1,0:T(8,128)(2,1)S(1)}, u32[]{:S(2)}, u32[]{:S(2)}) async-start(bf16[8,16,1024]{2,1,0:T(8,128)(2,1)} %get-tuple-element.106), calls=%async_computation.2 | async-start | bytes 524288 | tf_op jit(solution)/shard_map/all_to_all | solution.py:394
  67.5 9.5 %all-to-all-start.3 = ((bf16[8,16,1024]{2,1,0:T(8,128)(2,1)}), bf16[8,16,1024]{2,1,0:T(8,128)(2,1)S(1)}, u32[]{:S(2)}, u32[]{:S(2)}) async-start(bf16[8,16,1024]{2,1,0:T(8,128)(2,1)} %get-tuple-element.107), calls=%async_computation.3 | async-start | bytes 524288 | tf_op jit(solution)/shard_map/all_to_all | solution.py:394
  146.0 14.2 %all-to-all-start.8 = ((bf16[8,32,1024]{2,1,0:T(8,128)(2,1)}), bf16[8,32,1024]{2,1,0:T(8,128)(2,1)}, u32[]{:S(2)}, u32[]{:S(2)}) async-start(bf16[8,32,1024]{2,1,0:T(8,128)(2,1)} %get-tuple-element.115), calls=%async_computation.8 | async-start | bytes 1048576 | tf_op jit(solution)/shard_map/all_to_all | solution.py:394
  150.1 57.4 %all-gather.2.cloned.1.call-start = ((), (), s32[]{:S(2)}) async-start(), calls=%async_computation.20 | async-start | bytes 1114112 | tf_op jit(solution)/shard_map/all_gather | solution.py:561
  156.9 32.5 %collective-permute-start.22 = (bf16[512,1024]{1,0:T(8,128)(2,1)}, bf16[512,1024]{1,0:T(8,128)(2,1)}, u32[]{:S(2)}, u32[]{:S(2)}) collective-permute-start(bf16[512,1024]{1,0:T(8,128)(2,1)} %dynamic-slice_bitcast_fusion), channel_id=1, source_target_pairs={{0,1},{1,0},{2,3},{3,2},{4,5},{5,4},{6,7},{7,6},{8,9},{9,8},{10,11... | collective-permute-start | bytes 3145736 | tf_op jit(solution)/shard_map/ppermute | solution.py:409
  162.2 15.7 %all-to-all-start.9 = ((bf16[8,32,1024]{2,1,0:T(8,128)(2,1)}), bf16[8,32,1024]{2,1,0:T(8,128)(2,1)S(1)}, u32[]{:S(2)}, u32[]{:S(2)}) async-start(bf16[8,32,1024]{2,1,0:T(8,128)(2,1)} %get-tuple-element.119), calls=%async_computation.9 | async-start | bytes 1048576 | tf_op jit(solution)/shard_map/all_to_all | solution.py:394
  180.1 17.3 %all-to-all-start.10 = ((bf16[16,144,128]{2,1,0:T(8,128)(2,1)}), bf16[16,144,128]{2,1,0:T(8,128)(2,1)}, u32[]{:S(2)}, u32[]{:S(2)}) async-start(bf16[16,144,128]{2,1,0:T(8,128)(2,1)} %get-tuple-element.124), calls=%async_computation.10 | async-start | bytes 1179648 | tf_op jit(solution)/shard_map/all_to_all | solution.py:394
  200.3 64.2 %collective-permute-start.23 = (bf16[256,1024]{1,0:T(8,128)(2,1)}, bf16[256,1024]{1,0:T(8,128)(2,1)}, u32[]{:S(2)}, u32[]{:S(2)}) collective-permute-start(bf16[256,1024]{1,0:T(8,128)(2,1)} %dynamic-slice_bitcast_fusion.1), channel_id=1, source_target_pairs={{0,2},{1,3},{2,0},{3,1},{4,6},{5,7},{6,4},{7,5},{8,10},{9,11},{10,... | collective-permute-start | bytes 1572872 | tf_op jit(solution)/shard_map/ppermute | solution.py:409
  211.5 10.8 %all-to-all-start.11 = ((bf16[8,16,1024]{2,1,0:T(8,128)(2,1)}), bf16[8,16,1024]{2,1,0:T(8,128)(2,1)S(1)}, u32[]{:S(2)}, u32[]{:S(2)}) async-start(bf16[8,16,1024]{2,1,0:T(8,128)(2,1)} %get-tuple-element.127), calls=%async_computation.11 | async-start | bytes 524288 | tf_op jit(solution)/shard_map/all_to_all | solution.py:394
  219.2 29.7 %collective-permute-start.6 = (bf16[256,1024]{1,0:T(8,128)(2,1)}, bf16[256,1024]{1,0:T(8,128)(2,1)}, u32[]{:S(2)}, u32[]{:S(2)}) collective-permute-start(bf16[256,1024]{1,0:T(8,128)(2,1)} %dynamic-slice_bitcast_fusion.2), channel_id=1, source_target_pairs={{0,1},{1,0},{2,3},{3,2},{4,5},{5,4},{6,7},{7,6},{8,9},{9,8},{10,11... | collective-permute-start | bytes 1572872 | tf_op jit(solution)/shard_map/ppermute | solution.py:409
  224.1 9.7 %all-to-all-start.12 = ((bf16[8,16,1024]{2,1,0:T(8,128)(2,1)}), bf16[8,16,1024]{2,1,0:T(8,128)(2,1)S(1)}, u32[]{:S(2)}, u32[]{:S(2)}) async-start(bf16[8,16,1024]{2,1,0:T(8,128)(2,1)} %get-tuple-element.131), calls=%async_computation.12 | async-start | bytes 524288 | tf_op jit(solution)/shard_map/all_to_all | solution.py:394
  237.1 13.1 %all-to-all-start.13 = ((bf16[8,16,1024]{2,1,0:T(8,128)(2,1)}), bf16[8,16,1024]{2,1,0:T(8,128)(2,1)S(1)}, u32[]{:S(2)}, u32[]{:S(2)}) async-start(bf16[8,16,1024]{2,1,0:T(8,128)(2,1)} %get-tuple-element.133), calls=%async_computation.13 | async-start | bytes 524288 | tf_op jit(solution)/shard_map/all_to_all | solution.py:394
  246.1 11.1 %collective-permute-start.2 = (bf16[256,1024]{1,0:T(8,128)(2,1)}, bf16[256,1024]{1,0:T(8,128)(2,1)}, u32[]{:S(2)}, u32[]{:S(2)}) collective-permute-start(bf16[256,1024]{1,0:T(8,128)(2,1)} %dynamic-slice_bitcast_fusion.3), channel_id=1, source_target_pairs={{0,1},{1,0},{2,3},{3,2},{4,5},{5,4},{6,7},{7,6},{8,9},{9,8},{10,11... | collective-permute-start | bytes 1572872 | tf_op jit(solution)/shard_map/ppermute | solution.py:409
  248.8 11.0 %collective-permute-start = (bf16[256,1024]{1,0:T(8,128)(2,1)}, bf16[256,1024]{1,0:T(8,128)(2,1)}, u32[]{:S(2)}, u32[]{:S(2)}) collective-permute-start(bf16[256,1024]{1,0:T(8,128)(2,1)} %dynamic-slice_bitcast_fusion.4), channel_id=1, source_target_pairs={{0,1},{1,0},{2,3},{3,2},{4,5},{5,4},{6,7},{7,6},{8,9},{9,8},{10,11... | collective-permute-start | bytes 1572872 | tf_op jit(solution)/shard_map/ppermute | solution.py:409
  251.9 13.1 %all-to-all-start.14 = ((bf16[8,16,1024]{2,1,0:T(8,128)(2,1)}), bf16[8,16,1024]{2,1,0:T(8,128)(2,1)S(1)}, u32[]{:S(2)}, u32[]{:S(2)}) async-start(bf16[8,16,1024]{2,1,0:T(8,128)(2,1)} %get-tuple-element.137), calls=%async_computation.14 | async-start | bytes 524288 | tf_op jit(solution)/shard_map/all_to_all | solution.py:394
  259.4 9.7 %collective-permute-start.3 = (bf16[128,1024]{1,0:T(8,128)(2,1)}, bf16[128,1024]{1,0:T(8,128)(2,1)}, u32[]{:S(2)}, u32[]{:S(2)}) collective-permute-start(bf16[128,1024]{1,0:T(8,128)(2,1)} %dynamic-slice_bitcast_fusion.6), channel_id=1, source_target_pairs={{0,2},{1,3},{2,0},{3,1},{4,6},{5,7},{6,4},{7,5},{8,10},{9,11},{10,... | collective-permute-start | bytes 786440 | tf_op jit(solution)/shard_map/ppermute | solution.py:409
  261.1 13.5 %collective-permute-start.1 = (bf16[128,1024]{1,0:T(8,128)(2,1)S(1)}, bf16[128,1024]{1,0:T(8,128)(2,1)S(1)}, u32[]{:S(2)}, u32[]{:S(2)}) collective-permute-start(bf16[128,1024]{1,0:T(8,128)(2,1)S(1)} %dynamic-slice_bitcast_fusion.7), channel_id=1, source_target_pairs={{0,2},{1,3},{2,0},{3,1},{4,6},{5,7},{6,4},{7,5},{8,10},{9,11},{10,... | collective-permute-start | bytes 786440 | tf_op jit(solution)/shard_map/ppermute | solution.py:409
  264.5 20.6 %collective-permute-start.7 = (bf16[128,1024]{1,0:T(8,128)(2,1)}, bf16[128,1024]{1,0:T(8,128)(2,1)}, u32[]{:S(2)}, u32[]{:S(2)}) collective-permute-start(bf16[128,1024]{1,0:T(8,128)(2,1)} %dynamic-slice_bitcast_fusion.5), channel_id=1, source_target_pairs={{0,2},{1,3},{2,0},{3,1},{4,6},{5,7},{6,4},{7,5},{8,10},{9,11},{10,... | collective-permute-start | bytes 786440 | tf_op jit(solution)/shard_map/ppermute | solution.py:409
  276.4 18.3 %all-to-all-start.15 = ((bf16[16,144,128]{2,1,0:T(8,128)(2,1)}), bf16[16,144,128]{2,1,0:T(8,128)(2,1)S(1)}, u32[]{:S(2)}, u32[]{:S(2)}) async-start(bf16[16,144,128]{2,1,0:T(8,128)(2,1)} %get-tuple-element.144), calls=%async_computation.15 | async-start | bytes 1179648 | tf_op jit(solution)/shard_map/all_to_all | solution.py:394
  283.0 51.0 %all-reduce.4.cloned.1.call-start = ((), (), s32[]{:S(2)}) async-start(), calls=%async_computation.21 | async-start | bytes 1572864 | tf_op jit(solution)/shard_map/psum | solution.py:446
  286.1 17.0 %collective-permute-start.16 = (bf16[64,1024]{1,0:T(8,128)(2,1)S(1)}, bf16[64,1024]{1,0:T(8,128)(2,1)S(1)}, u32[]{:S(2)}, u32[]{:S(2)}) collective-permute-start(bf16[64,1024]{1,0:T(8,128)(2,1)S(1)} %dynamic-slice_bitcast_fusion.8), channel_id=1, source_target_pairs={{0,4},{1,5},{2,6},{3,7},{4,0},{5,1},{6,2},{7,3},{8,12},{9,13},{10,... | collective-permute-start | bytes 393224 | tf_op jit(solution)/shard_map/ppermute | solution.py:409
  292.2 15.3 %collective-permute-start.10 = (bf16[64,1024]{1,0:T(8,128)(2,1)S(1)}, bf16[64,1024]{1,0:T(8,128)(2,1)S(1)}, u32[]{:S(2)}, u32[]{:S(2)}) collective-permute-start(bf16[64,1024]{1,0:T(8,128)(2,1)S(1)} %dynamic-slice_bitcast_fusion.9), channel_id=1, source_target_pairs={{0,12},{1,13},{2,14},{3,15},{4,8},{5,9},{6,10},{7,11},{8,4},{9,5},... | collective-permute-start | bytes 393224 | tf_op jit(solution)/shard_map/ppermute | solution.py:409
  298.6 10.8 %all-to-all-start.16 = ((bf16[8,16,1024]{2,1,0:T(8,128)(2,1)}), bf16[8,16,1024]{2,1,0:T(8,128)(2,1)S(1)}, u32[]{:S(2)}, u32[]{:S(2)}) async-start(bf16[8,16,1024]{2,1,0:T(8,128)(2,1)} %get-tuple-element.147), calls=%async_computation.16 | async-start | bytes 524288 | tf_op jit(solution)/shard_map/all_to_all | solution.py:394
  303.2 40.2 %collective-permute-start.17 = (bf16[32,1024]{1,0:T(8,128)(2,1)S(1)}, bf16[32,1024]{1,0:T(8,128)(2,1)S(1)}, u32[]{:S(2)}, u32[]{:S(2)}) collective-permute-start(bf16[32,1024]{1,0:T(8,128)(2,1)S(1)} %dynamic-slice_bitcast_fusion.10), channel_id=1, source_target_pairs={{0,12},{1,13},{2,14},{3,15},{4,8},{5,9},{6,10},{7,11},{8,4},{9,5},... | collective-permute-start | bytes 196616 | tf_op jit(solution)/shard_map/ppermute | solution.py:409
  308.1 44.3 %copy-start.2 = (bf16[512,1024]{1,0:T(8,128)(2,1)S(1)}, bf16[512,1024]{1,0:T(8,128)(2,1)}, u32[]{:S(2)}) copy-start(bf16[512,1024]{1,0:T(8,128)(2,1)} %get-tuple-element.157) | copy-start | bytes 3145732
  308.2 37.2 %collective-permute-start.11 = (bf16[32,1024]{1,0:T(8,128)(2,1)S(1)}, bf16[32,1024]{1,0:T(8,128)(2,1)S(1)}, u32[]{:S(2)}, u32[]{:S(2)}) collective-permute-start(bf16[32,1024]{1,0:T(8,128)(2,1)S(1)} %dynamic-slice_bitcast_fusion.11), channel_id=1, source_target_pairs={{0,4},{1,5},{2,6},{3,7},{4,0},{5,1},{6,2},{7,3},{8,12},{9,13},{10,... | collective-permute-start | bytes 196616 | tf_op jit(solution)/shard_map/ppermute | solution.py:409
  334.0 31.2 %collective-permute-start.24 = (bf16[256,1024]{1,0:T(8,128)(2,1)}, bf16[256,1024]{1,0:T(8,128)(2,1)}, u32[]{:S(2)}, u32[]{:S(2)}) collective-permute-start(bf16[256,1024]{1,0:T(8,128)(2,1)} %get-tuple-element.190), channel_id=1, source_target_pairs={{0,2},{1,3},{2,0},{3,1},{4,6},{5,7},{6,4},{7,5},{8,10},{9,11},{10,... | collective-permute-start | bytes 1572872 | tf_op jit(solution)/shard_map/ppermute | solution.py:409
  339.3 11.3 %all-to-all-start.17 = ((bf16[8,24,1024]{2,1,0:T(8,128)(2,1)}), bf16[8,24,1024]{2,1,0:T(8,128)(2,1)S(1)}, u32[]{:S(2)}, u32[]{:S(2)}) async-start(bf16[8,24,1024]{2,1,0:T(8,128)(2,1)} %pad_maximum_fusion.4), calls=%async_computation.17 | async-start | bytes 786432 | tf_op jit(solution)/shard_map/all_to_all | solution.py:394
  343.5 4.8 %collective-permute-start.18 = (bf16[32,1024]{1,0:T(8,128)(2,1)S(1)}, bf16[32,1024]{1,0:T(8,128)(2,1)S(1)}, u32[]{:S(2)}, u32[]{:S(2)}) collective-permute-start(bf16[32,1024]{1,0:T(8,128)(2,1)S(1)} %fusion.15), channel_id=1, source_target_pairs={{0,12},{1,13},{2,14},{3,15},{4,8},{5,9},{6,10},{7,11},{8,4},{9,5},... | collective-permute-start | bytes 196616 | tf_op jit(solution)/shard_map/ppermute | solution.py:409
  345.3 3.6 collective-permute-start.12
  345.4 53.4 %collective-permute-start.8 = (bf16[128,1024]{1,0:T(8,128)(2,1)}, bf16[128,1024]{1,0:T(8,128)(2,1)}, u32[]{:S(2)}, u32[]{:S(2)}) collective-permute-start(bf16[128,1024]{1,0:T(8,128)(2,1)} %get-tuple-element.175), channel_id=1, source_target_pairs={{0,2},{1,3},{2,0},{3,1},{4,6},{5,7},{6,4},{7,5},{8,10},{9,11},{10,... | collective-permute-start | bytes 786440 | tf_op jit(solution)/shard_map/ppermute | solution.py:409
  348.3 10.1 %collective-permute-start.19 = (bf16[64,1024]{1,0:T(8,128)(2,1)S(1)}, bf16[64,1024]{1,0:T(8,128)(2,1)S(1)}, u32[]{:S(2)}, u32[]{:S(2)}) collective-permute-start(bf16[64,1024]{1,0:T(8,128)(2,1)S(1)} %pad_maximum_fusion.8), channel_id=1, source_target_pairs={{0,4},{1,5},{2,6},{3,7},{4,0},{5,1},{6,2},{7,3},{8,12},{9,13},{10,... | collective-permute-start | bytes 393224 | tf_op jit(solution)/shard_map/ppermute | solution.py:409
  349.0 9.5 %collective-permute-start.13 = (bf16[64,1024]{1,0:T(8,128)(2,1)S(1)}, bf16[64,1024]{1,0:T(8,128)(2,1)S(1)}, u32[]{:S(2)}, u32[]{:S(2)}) collective-permute-start(bf16[64,1024]{1,0:T(8,128)(2,1)S(1)} %pad_maximum_fusion.7), channel_id=1, source_target_pairs={{0,12},{1,13},{2,14},{3,15},{4,8},{5,9},{6,10},{7,11},{8,4},{9,5},... | collective-permute-start | bytes 393224 | tf_op jit(solution)/shard_map/ppermute | solution.py:409
  352.5 7.5 %collective-permute-start.4 = (bf16[8,8,4224]{2,1,0:T(8,128)(2,1)S(1)}, bf16[8,8,4224]{2,1,0:T(8,128)(2,1)S(1)}, u32[]{:S(2)}, u32[]{:S(2)}) collective-permute-start(bf16[8,8,4224]{2,1,0:T(8,128)(2,1)S(1)} %fusion.7), channel_id=1, source_target_pairs={{0,1},{1,0},{2,3},{3,2},{4,5},{5,4},{6,7},{7,6},{8,9},{9,8},{10,11... | collective-permute-start | bytes 1622024 | tf_op jit(solution)/shard_map/ppermute | solution.py:409
  360.9 19.1 %all-to-all-start.18 = ((bf16[8,8,4224]{2,1,0:T(8,128)(2,1)}), bf16[8,8,4224]{2,1,0:T(8,128)(2,1)S(1)}, u32[]{:S(2)}, u32[]{:S(2)}) async-start(bf16[8,8,4224]{2,1,0:T(8,128)(2,1)} %fusion.1), calls=%async_computation.18 | async-start | bytes 1081344 | tf_op jit(solution)/shard_map/all_to_all | solution.py:451
  365.2 14.7 %collective-permute-start.20 = (bf16[128,1024]{1,0:T(8,128)(2,1)S(1)}, bf16[128,1024]{1,0:T(8,128)(2,1)S(1)}, u32[]{:S(2)}, u32[]{:S(2)}) collective-permute-start(bf16[128,1024]{1,0:T(8,128)(2,1)S(1)} %pad_maximum_fusion.6), channel_id=1, source_target_pairs={{0,2},{1,3},{2,0},{3,1},{4,6},{5,7},{6,4},{7,5},{8,10},{9,11},{10,... | collective-permute-start | bytes 786440 | tf_op jit(solution)/shard_map/ppermute | solution.py:409
  369.4 30.8 %collective-permute-start.25 = (bf16[512,1024]{1,0:T(8,128)(2,1)S(1)}, bf16[512,1024]{1,0:T(8,128)(2,1)}, u32[]{:S(2)}, u32[]{:S(2)}) collective-permute-start(bf16[512,1024]{1,0:T(8,128)(2,1)S(1)} %pad_maximum_fusion.own_ref), channel_id=1, source_target_pairs={{0,1},{1,0},{2,3},{3,2},{4,5},{5,4},{6,7},{7,6},{8,9},{9,8},{10,11... | collective-permute-start | bytes 3145736 | tf_op jit(solution)/shard_map/ppermute | solution.py:409
  370.7 16.8 %collective-permute-start.14 = (bf16[128,1024]{1,0:T(8,128)(2,1)S(1)}, bf16[128,1024]{1,0:T(8,128)(2,1)}, u32[]{:S(2)}, u32[]{:S(2)}) collective-permute-start(bf16[128,1024]{1,0:T(8,128)(2,1)S(1)} %pad_maximum_fusion.5), channel_id=1, source_target_pairs={{0,2},{1,3},{2,0},{3,1},{4,6},{5,7},{6,4},{7,5},{8,10},{9,11},{10,... | collective-permute-start | bytes 786440 | tf_op jit(solution)/shard_map/ppermute | solution.py:409
  380.9 15.3 %all-to-all-start.19 = ((bf16[8,8,4224]{2,1,0:T(8,128)(2,1)}), bf16[8,8,4224]{2,1,0:T(8,128)(2,1)S(1)}, u32[]{:S(2)}, u32[]{:S(2)}) async-start(bf16[8,8,4224]{2,1,0:T(8,128)(2,1)} %broadcast_in_dim.15), calls=%async_computation.19 | async-start | bytes 1081344 | tf_op jit(solution)/shard_map/all_to_all | solution.py:451
  386.1 14.1 %collective-permute-start.21 = (bf16[256,1024]{1,0:T(8,128)(2,1)S(1)}, bf16[256,1024]{1,0:T(8,128)(2,1)}, u32[]{:S(2)}, u32[]{:S(2)}) collective-permute-start(bf16[256,1024]{1,0:T(8,128)(2,1)S(1)} %pad_maximum_fusion.3.f_own), channel_id=1, source_target_pairs={{0,1},{1,0},{2,3},{3,2},{4,5},{5,4},{6,7},{7,6},{8,9},{9,8},{10,11... | collective-permute-start | bytes 1572872 | tf_op jit(solution)/shard_map/ppermute | solution.py:409
  388.5 11.7 %collective-permute-start.15 = (bf16[256,1024]{1,0:T(8,128)(2,1)S(1)}, bf16[256,1024]{1,0:T(8,128)(2,1)}, u32[]{:S(2)}, u32[]{:S(2)}) collective-permute-start(bf16[256,1024]{1,0:T(8,128)(2,1)S(1)} %pad_maximum_fusion.2.p_own), channel_id=1, source_target_pairs={{0,1},{1,0},{2,3},{3,2},{4,5},{5,4},{6,7},{7,6},{8,9},{9,8},{10,11... | collective-permute-start | bytes 1572872 | tf_op jit(solution)/shard_map/ppermute | solution.py:409
  396.1 10.3 %collective-permute-start.5 = (bf16[8,8,4224]{2,1,0:T(8,128)(2,1)S(1)}, bf16[8,8,4224]{2,1,0:T(8,128)(2,1)S(1)}, u32[]{:S(2)}, u32[]{:S(2)}) collective-permute-start(bf16[8,8,4224]{2,1,0:T(8,128)(2,1)S(1)} %all-to-all-done.19.late_own), channel_id=1, source_target_pairs={{0,1},{1,0},{2,3},{3,2},{4,5},{5,4},{6,7},{7,6},{8,9},{9,8},{10,11... | collective-permute-start | bytes 1622024 | tf_op jit(solution)/shard_map/ppermute | solution.py:409
  400.0 10.5 %collective-permute-start.9 = (bf16[256,1024]{1,0:T(8,128)(2,1)S(1)}, bf16[256,1024]{1,0:T(8,128)(2,1)}, u32[]{:S(2)}, u32[]{:S(2)}) collective-permute-start(bf16[256,1024]{1,0:T(8,128)(2,1)S(1)} %pad_maximum_fusion.1.own_ref), channel_id=1, source_target_pairs={{0,1},{1,0},{2,3},{3,2},{4,5},{5,4},{6,7},{7,6},{8,9},{9,8},{10,11... | collective-permute-start | bytes 1572872 | tf_op jit(solution)/shard_map/ppermute | solution.py:409
  (28 other events, 300.8 us)
Sparse Core Ops, SparseCore 0:
  153.3 54.1 all-gather.1
  289.4 44.5 all-reduce.3
where the time goes:
time: 425 us; the launch traced here: 421 us
  starting transfers between devices  113 us (27%)
  waiting for transfers between devices  111 us (26%)
  Pallas kernels  74 us (17%)
  blocking collectives  55.3 us (13%)
  other arithmetic  31.2 us (7%)
  local copies, waits for them, and re-layouts  22.2 us (5%)
  between operations  14.8 us (3%)
    pallas_call x26, Pallas kernels, call(): pl.pallas_call(kernel, grid=(1,), in_specs=[spec(index, arg) for index, a...  74 us
    all_to_all x14, starting transfers between devices, swap_all(): return lax.all_to_all(value, axis, 0, 0)  65.9 us
    all_to_all x14, waiting for transfers between devices, swap_all(): return lax.all_to_all(value, axis, 0, 0)  57.4 us
    all_to_all x4, blocking collectives, swap_all(): return lax.all_to_all(value, axis, 0, 0)  55.3 us
    ppermute x26, starting transfers between devices, swap(): lax.ppermute(value, 'dp', [(i, i ^ flip) for i in range(lax.axis_size('dp...  37.3 us
    psum x1, waiting for transfers between devices, sum_over_x(): return lax.psum(values, 'dp', axis_index_groups=groups)  22.1 us
    ppermute x26, waiting for transfers between devices, swap(): lax.ppermute(value, 'dp', [(i, i ^ flip) for i in range(lax.axis_size('dp...  17.8 us
    convert_element_type x13, other arithmetic, halve(): return (mine.astype(F32) + got.astype(F32)).astype(BF16)  14.1 us
  transfers between devices with their start and end apart: 44, of which 19 were waited for; matrix products, arithmetic and copies ran while one was open for 12% of the time, Pallas kernels for 11%

commit v1 on v0

--- a/solution.py
+++ b/solution.py
@@ -630,6 +630,8 @@
                 gains[layer, 1],
                 grad,
             )
+            sent, quarters = lax.optimization_barrier((sent, quarters))
+            done[1] = sum_over_x(quarters)
             g_y = swap_all(sent, "tensor")
         grad_b = grad
         g_o, delta, sent = call(
@@ -642,7 +644,9 @@
             logs,
             blocks={0: ((slots, share, width), lambda i: (0, 0, 0))},
         )
-        if not layer:
+        if layer:
+            sent, q_every = lax.optimization_barrier((sent, q_every))
+        else:
             starts = [
                 halve(halve(part, CORE), DEPTH) for part in (end_pack[:hidden], end_pack[hidden:])
             ]
@@ -673,6 +677,8 @@
             room=24,
             blocks={4: ((total, local), lambda i: (0, layer))},
         )
+        if not layer:
+            parts, done[1] = lax.optimization_barrier((parts, done[1]))
         grad, sums_a, sent = call(
             back_kernel,
             [row_block, two_rows, exchange],
@@ -708,7 +714,7 @@
             g_m = swap_all(sent, "tensor").reshape(rows, width)
             end_part = halve(halve(end_pack, CORE, go_all), DEPTH, grad)
             attend_part = halve(halve(attend_pack, CORE), DEPTH, g_m)
-            done[layer] = sum_over_x((end_part, attend_part))
+            quarters = (end_part, attend_part)
     tail = jnp.concatenate([sent, jnp.broadcast_to(jnp.concatenate(sums, 0).astype(BF16), (slots, 8, width))], 1)
     tail_got = got = swap_all(tail, "tensor")
     grad_input = got[:, :share].reshape(rows, width).astype(F32)
@@ -727,10 +733,9 @@
     arrived = swap_chips(half)
     mine = jnp.sum(arrived.astype(F32), 0).astype(BF16)
     late = swap_chips(jnp.broadcast_to(mine, (ranks // 2,) + mine.shape))
-    late_got = swap(late, CORE)
     events = (g_kv, grad, half)
     end_parts = [part for turn, value in enumerate(starts) for part in finish_sums(value, turn, events)]
-    end_last, attend_last = [rejoin(after(part, grad), DEPTH, None, half) for part in done[1]]
+    end_last, attend_last = [rejoin(part, DEPTH, None, half) for part in done[1]]
     side = side_of(CORE)
     sides = side.astype(jnp.int32).reshape(1)
     g_w_proj, g_w_fc = call(
@@ -743,6 +748,8 @@
         swap(end_last, CORE),
         room=40,
     )
+    late, g_w_proj, g_w_fc = lax.optimization_barrier((late, g_w_proj, g_w_fc))
+    late_got = swap(late, CORE)
     g_w_out, g_w_qkv = call(
         finish_attend_kernel,
         [shape((layers, local, width), F32), shape((layers, 3, width, local), F32)],

time: 425 us -> 420 us (0.988)
  blocking collectives: 55.3 us -> 28.5 us
  starting transfers between devices: 113 us -> 132 us
    all_to_all x4 -> x3, blocking collectives: 55.3 us -> 28.5 us  [swap_all(): return lax.all_to_all(value, axis, 0, 0)]
    all_to_all x14 -> x15, waiting for transfers between devices: 57.4 us -> 75.9 us  [swap_all(): return lax.all_to_all(value, axis, 0, 0)]
    all_to_all x14 -> x15, starting transfers between devices: 65.9 us -> 79.3 us  [swap_all(): return lax.all_to_all(value, axis, 0, 0)]
    psum x1, waiting for transfers between devices: 22.1 us -> 11.7 us  [sum_over_x(): return lax.psum(values, 'dp', axis_index_groups=groups)]
    ppermute x26, waiting for transfers between devices: 17.8 us -> 26.4 us  [swap(): lax.ppermute(value, 'dp', [(i, i ^ flip) for i in range(lax.axis_size('dp...]
    all_to_all x2, waiting for transfers between devices: 7.45 us -> 0.41 us  [swap_chips(): return lax.all_to_all(value, 'dp', 0, 0, axis_index_groups=groups)]
    ppermute x26, starting transfers between devices: 37.3 us -> 44 us  [swap(): lax.ppermute(value, 'dp', [(i, i ^ flip) for i in range(lax.axis_size('dp...]
    all_gather x1, waiting for transfers between devices: 5.88 us -> 0.01 us  [body(): lax.all_gather(jnp.concatenate([kept[3] for kept in saved], 1), 'dp', axi...]
  transfers between devices with their start and end apart: 44 -> 45, of which waited for: 19 -> 22; matrix products, arithmetic and copies ran while one was open for 12% -> 12% of each run, Pallas kernels for 11% -> 13%
where the time goes in v1:
time: 420 us; the launch traced here: 417 us
  starting transfers between devices  132 us (31%)
  waiting for transfers between devices  114 us (27%)
  Pallas kernels  74.1 us (18%)
  other arithmetic  30.6 us (7%)
  blocking collectives  28.5 us (7%)
  local copies, waits for them, and re-layouts  22.4 us (5%)
  between operations  15 us (4%)
    all_to_all x15, starting transfers between devices, swap_all(): return lax.all_to_all(value, axis, 0, 0)  79.3 us
    all_to_all x15, waiting for transfers between devices, swap_all(): return lax.all_to_all(value, axis, 0, 0)  75.9 us
    pallas_call x26, Pallas kernels, call(): pl.pallas_call(kernel, grid=(1,), in_specs=[spec(index, arg) for index, a...  74.1 us
    ppermute x26, starting transfers between devices, swap(): lax.ppermute(value, 'dp', [(i, i ^ flip) for i in range(lax.axis_size('dp...  44 us
    all_to_all x3, blocking collectives, swap_all(): return lax.all_to_all(value, axis, 0, 0)  28.5 us
    ppermute x26, waiting for transfers between devices, swap(): lax.ppermute(value, 'dp', [(i, i ^ flip) for i in range(lax.axis_size('dp...  26.4 us
    convert_element_type x13, other arithmetic, halve(): return (mine.astype(F32) + got.astype(F32)).astype(BF16)  13.3 us
    psum x1, waiting for transfers between devices, sum_over_x(): return lax.psum(values, 'dp', axis_index_groups=groups)  11.7 us
  transfers between devices with their start and end apart: 45, of which 22 were waited for; matrix products, arithmetic and copies ran while one was open for 12% of the time, Pallas kernels for 13%

profile of v1, /device:TPU:1, one launch (start us, length us, event | category | flops | bytes accessed | tf_op | source)
XLA Modules:
  0.0 416.8 jit_solution(12161145826301792990)
XLA Ops:
  12.1 9.3 %all-to-all-start = ((bf16[16,128,256]{2,1,0:T(8,128)(2,1)}), bf16[16,128,256]{2,1,0:T(8,128)(2,1)S(1)}, u32[]{:S(2)}, u32[]{:S(2)}) async-start(bf16[16,128,256]{2,1,0:T(8,128)(2,1)} %get-tuple-element.113), calls=%async_computation | async-start | bytes 2097152 | tf_op jit(solution)/shard_map/all_to_all | solution.py:394
  22.9 15.7 %all-to-all-done.kv_ref = bf16[16,128,256]{2,1,0:T(8,128)(2,1)S(1)} async-done(((bf16[16,128,256]{2,1,0:T(8,128)(2,1)}), bf16[16,128,256]{2,1,0:T(8,128)(2,1)S(1)}, u32[]{:S(2)}, u32[]{:S(2)}) %all-to-all-start) | async-done | bytes 1048608 | tf_op jit(solution)/shard_map/all_to_all | solution.py:394
  38.6 3.6 shard_map.221
  42.2 4.6 %all-to-all-start.1 = ((bf16[8,16,1024]{2,1,0:T(8,128)(2,1)}), bf16[8,16,1024]{2,1,0:T(8,128)(2,1)S(1)}, u32[]{:S(2)}, u32[]{:S(2)}) async-start(bf16[8,16,1024]{2,1,0:T(8,128)(2,1)} %get-tuple-element.114), calls=%async_computation.1 | async-start | bytes 524288 | tf_op jit(solution)/shard_map/all_to_all | solution.py:394
  48.1 5.2 %all-to-all-done.1.parts_ref = bf16[8,16,1024]{2,1,0:T(8,128)(2,1)S(1)} async-done(((bf16[8,16,1024]{2,1,0:T(8,128)(2,1)}), bf16[8,16,1024]{2,1,0:T(8,128)(2,1)S(1)}, u32[]{:S(2)}, u32[]{:S(2)}) %all-to-all-start.1) | async-done | bytes 262176 | tf_op jit(solution)/shard_map/all_to_all | solution.py:394
  55.1 3.4 all-to-all-start.2
  59.2 5.5 %all-to-all-done.2 = bf16[8,16,1024]{2,1,0:T(8,128)(2,1)S(1)} async-done(((bf16[8,16,1024]{2,1,0:T(8,128)(2,1)}), bf16[8,16,1024]{2,1,0:T(8,128)(2,1)S(1)}, u32[]{:S(2)}, u32[]{:S(2)}) %all-to-all-start.2) | async-done | bytes 262176 | tf_op jit(solution)/shard_map/all_to_all | solution.py:394
  67.5 3.4 all-to-all-start.3
  71.5 5.5 %all-to-all-done.3.parts_ref = bf16[8,16,1024]{2,1,0:T(8,128)(2,1)S(1)} async-done(((bf16[8,16,1024]{2,1,0:T(8,128)(2,1)}), bf16[8,16,1024]{2,1,0:T(8,128)(2,1)S(1)}, u32[]{:S(2)}, u32[]{:S(2)}) %all-to-all-start.3) | async-done | bytes 262176 | tf_op jit(solution)/shard_map/all_to_all | solution.py:394
  78.8 9.5 %all_to_all.100 = bf16[8,16,1024]{2,1,0:T(8,128)(2,1)S(1)} all-to-all(bf16[8,16,1024]{2,1,0:T(8,128)(2,1)} %get-tuple-element.118), channel_id=1, replica_groups=mesh['tensor'=8,'dp'=16] {'tensor'}, dimensions={0} | all-to-all | bytes 524288 | tf_op jit(solution)/shard_map/all_to_all | solution.py:394
  90.9 9.9 %all-to-all-start.5 = ((bf16[16,128,256]{2,1,0:T(8,128)(2,1)}), bf16[16,128,256]{2,1,0:T(8,128)(2,1)S(1)}, u32[]{:S(2)}, u32[]{:S(2)}) async-start(bf16[16,128,256]{2,1,0:T(8,128)(2,1)} %get-tuple-element.120), calls=%async_computation.5 | async-start | bytes 2097152 | tf_op jit(solution)/shard_map/all_to_all | solution.py:394
  101.5 16.5 %all-to-all-done.5.kv_ref = bf16[16,128,256]{2,1,0:T(8,128)(2,1)S(1)} async-done(((bf16[16,128,256]{2,1,0:T(8,128)(2,1)}), bf16[16,128,256]{2,1,0:T(8,128)(2,1)S(1)}, u32[]{:S(2)}, u32[]{:S(2)}) %all-to-all-start.5) | async-done | bytes 1048608 | tf_op jit(solution)/shard_map/all_to_all | solution.py:394
  118.0 3.6 shard_map.226
  121.6 9.6 %all_to_all.101.parts_ref = bf16[8,16,1024]{2,1,0:T(8,128)(2,1)S(1)} all-to-all(bf16[8,16,1024]{2,1,0:T(8,128)(2,1)} %get-tuple-element.121), channel_id=1, replica_groups=mesh['tensor'=8,'dp'=16] {'tensor'}, dimensions={0} | all-to-all | bytes 524288 | tf_op jit(solution)/shard_map/all_to_all | solution.py:394
  133.0 9.5 %all_to_all.102 = bf16[8,16,1024]{2,1,0:T(8,128)(2,1)S(1)} all-to-all(bf16[8,16,1024]{2,1,0:T(8,128)(2,1)} %get-tuple-element.123), channel_id=1, replica_groups=mesh['tensor'=8,'dp'=16] {'tensor'}, dimensions={0} | all-to-all | bytes 524288 | tf_op jit(solution)/shard_map/all_to_all | solution.py:394
  142.5 3.8 shard_map.228
  146.3 4.1 all-to-all-start.8
  151.2 3.0 shard_map.236
  154.3 3.8 all-to-all-done.8.parts_ref
  160.1 3.5 all-to-all-start.9
  166.0 4.2 %collective-permute-start = (bf16[512,1024]{1,0:T(8,128)(2,1)}, bf16[512,1024]{1,0:T(8,128)(2,1)}, u32[]{:S(2)}, u32[]{:S(2)}) collective-permute-start(bf16[512,1024]{1,0:T(8,128)(2,1)} %dynamic-slice_bitcast_fusion), channel_id=1, source_target_pairs={{0,1},{1,0},{2,3},{3,2},{4,5},{5,4},{6,7},{7,6},{8,9},{9,8},{10,11... | collective-permute-start | bytes 3145736 | tf_op jit(solution)/shard_map/ppermute | solution.py:409
  173.3 10.8 %all-to-all-start.10 = ((bf16[16,144,128]{2,1,0:T(8,128)(2,1)}), bf16[16,144,128]{2,1,0:T(8,128)(2,1)}, u32[]{:S(2)}, u32[]{:S(2)}) async-start(bf16[16,144,128]{2,1,0:T(8,128)(2,1)} %get-tuple-element.135), calls=%async_computation.10 | async-start | bytes 1179648 | tf_op jit(solution)/shard_map/all_to_all | solution.py:394
  189.1 6.9 %all-to-all-done.10.got_ref = bf16[16,144,128]{2,1,0:T(8,128)(2,1)} async-done(((bf16[16,144,128]{2,1,0:T(8,128)(2,1)}), bf16[16,144,128]{2,1,0:T(8,128)(2,1)}, u32[]{:S(2)}, u32[]{:S(2)}) %all-to-all-start.10) | async-done | bytes 589856 | tf_op jit(solution)/shard_map/all_to_all | solution.py:394
  195.9 4.0 shard_map.232
  205.6 3.4 all-to-all-start.11
  211.0 5.5 %all-to-all-done.11.parts_ref = bf16[8,16,1024]{2,1,0:T(8,128)(2,1)S(1)} async-done(((bf16[8,16,1024]{2,1,0:T(8,128)(2,1)}), bf16[8,16,1024]{2,1,0:T(8,128)(2,1)S(1)}, u32[]{:S(2)}, u32[]{:S(2)}) %all-to-all-start.11) | async-done | bytes 262176 | tf_op jit(solution)/shard_map/all_to_all | solution.py:394
  218.3 3.4 all-to-all-start.12
  223.1 5.5 %all-to-all-done.12 = bf16[8,16,1024]{2,1,0:T(8,128)(2,1)S(1)} async-done(((bf16[8,16,1024]{2,1,0:T(8,128)(2,1)}), bf16[8,16,1024]{2,1,0:T(8,128)(2,1)S(1)}, u32[]{:S(2)}, u32[]{:S(2)}) %all-to-all-start.12) | async-done | bytes 262176 | tf_op jit(solution)/shard_map/all_to_all | solution.py:394
  228.5 3.2 shard_map.234
  231.7 3.4 all-to-all-start.13
  235.1 3.0 shard_map.239
  248.7 4.3 %collective-permute-done.3 = bf16[128,1024]{1,0:T(8,128)(2,1)S(1)} collective-permute-done((bf16[128,1024]{1,0:T(8,128)(2,1)S(1)}, bf16[128,1024]{1,0:T(8,128)(2,1)S(1)}, u32[]{:S(2)}, u32[]{:S(2)}) %collective-permute-start.3) | collective-permute-done | bytes 262176 | tf_op jit(solution)/shard_map/ppermute | solution.py:409
  254.8 5.3 %all-to-all-start.14 = ((bf16[8,16,1024]{2,1,0:T(8,128)(2,1)}), bf16[8,16,1024]{2,1,0:T(8,128)(2,1)S(1)}, u32[]{:S(2)}, u32[]{:S(2)}) async-start(bf16[8,16,1024]{2,1,0:T(8,128)(2,1)} %get-tuple-element.158), calls=%async_computation.14 | async-start | bytes 524288 | tf_op jit(solution)/shard_map/all_to_all | solution.py:394
  274.0 3.9 collective-permute-done.5
  278.9 5.1 %all-to-all-start.15 = ((bf16[16,144,128]{2,1,0:T(8,128)(2,1)}), bf16[16,144,128]{2,1,0:T(8,128)(2,1)S(1)}, u32[]{:S(2)}, u32[]{:S(2)}) async-start(bf16[16,144,128]{2,1,0:T(8,128)(2,1)} %get-tuple-element.165), calls=%async_computation.15 | async-start | bytes 1179648 | tf_op jit(solution)/shard_map/all_to_all | solution.py:394
  291.8 5.0 %all-to-all-done.15.got_ref = bf16[16,144,128]{2,1,0:T(8,128)(2,1)S(1)} async-done(((bf16[16,144,128]{2,1,0:T(8,128)(2,1)}), bf16[16,144,128]{2,1,0:T(8,128)(2,1)S(1)}, u32[]{:S(2)}, u32[]{:S(2)}) %all-to-all-start.15) | async-done | bytes 589856 | tf_op jit(solution)/shard_map/all_to_all | solution.py:394
  296.8 3.9 shard_map.241
  300.7 11.7 %all-reduce.4.cloned.1.call-done = (bf16[256,1024]{1,0:T(8,128)(2,1)}, bf16[128,1024]{1,0:T(8,128)(2,1)}) async-done(((bf16[256,1024]{1,0:T(8,128)(2,1)}, bf16[128,1024]{1,0:T(8,128)(2,1)}), (bf16[256,1024]{1,0:T(8,128)(2,1)}, bf16[128,1024]{1,0:T(8,128)(2,1)})) %all-reduce.4.cloned.1.call-update) | async-done | bytes 786448 | tf_op jit(solution)/shard_map/psum | solution.py:446
  312.4 5.0 %all-to-all-start.16 = ((bf16[8,16,1024]{2,1,0:T(8,128)(2,1)}), bf16[8,16,1024]{2,1,0:T(8,128)(2,1)S(1)}, u32[]{:S(2)}, u32[]{:S(2)}) async-start(bf16[8,16,1024]{2,1,0:T(8,128)(2,1)} %get-tuple-element.171), calls=%async_computation.16 | async-start | bytes 524288 | tf_op jit(solution)/shard_map/all_to_all | solution.py:394
  331.5 4.5 %all-to-all-start.17 = ((bf16[8,24,1024]{2,1,0:T(8,128)(2,1)}), bf16[8,24,1024]{2,1,0:T(8,128)(2,1)S(1)}, u32[]{:S(2)}, u32[]{:S(2)}) async-start(bf16[8,24,1024]{2,1,0:T(8,128)(2,1)} %pad_maximum_fusion.4), calls=%async_computation.17 | async-start | bytes 786432 | tf_op jit(solution)/shard_map/all_to_all | solution.py:394
  344.7 5.8 %collective-permute-start.8 = (bf16[8,8,4224]{2,1,0:T(8,128)(2,1)S(1)}, bf16[8,8,4224]{2,1,0:T(8,128)(2,1)S(1)}, u32[]{:S(2)}, u32[]{:S(2)}) collective-permute-start(bf16[8,8,4224]{2,1,0:T(8,128)(2,1)S(1)} %fusion.7), channel_id=1, source_target_pairs={{0,1},{1,0},{2,3},{3,2},{4,5},{5,4},{6,7},{7,6},{8,9},{9,8},{10,11... | collective-permute-start | bytes 1622024 | tf_op jit(solution)/shard_map/ppermute | solution.py:409
  353.0 4.4 %all-to-all-start.18 = ((bf16[8,8,4224]{2,1,0:T(8,128)(2,1)}), bf16[8,8,4224]{2,1,0:T(8,128)(2,1)S(1)}, u32[]{:S(2)}, u32[]{:S(2)}) async-start(bf16[8,8,4224]{2,1,0:T(8,128)(2,1)} %fusion.1), calls=%async_computation.18 | async-start | bytes 1081344 | tf_op jit(solution)/shard_map/all_to_all | solution.py:451
  363.5 8.0 %collective-permute-done.19 = bf16[128,1024]{1,0:T(8,128)(2,1)S(1)} collective-permute-done((bf16[128,1024]{1,0:T(8,128)(2,1)S(1)}, bf16[128,1024]{1,0:T(8,128)(2,1)S(1)}, u32[]{:S(2)}, u32[]{:S(2)}) %collective-permute-start.19) | collective-permute-done | bytes 262176 | tf_op jit(solution)/shard_map/ppermute | solution.py:409
  371.6 3.9 collective-permute-start.20
  381.8 4.0 all-to-all-start.19
  385.8 3.0 collective-permute-start.24
  389.8 6.2 %shard_map.244 = (f32[2,512,1024]{2,1,0:T(8,128)}, f32[2,1024,512]{2,1,0:T(8,128)}) custom-call(s32[1]{0:T(128)} %bitcast.57.side_ref, bf16[256,1024]{1,0:T(8,128)(2,1)} %copy-done.10, bf16[256,1024]{1,0:T(8,128)(2,1)} %collective-permute-done.14.p_got, bf16[256,1024]{1,0:T(8,128)(2,1)} %copy-done.8, bf16[256,1024]{1,0:T(8,128)(2,1)} %collective-permute-done.20.f_got, ...), custom_call_target="tpu_custom_call" | custom-call | flops 1000 | bytes 1000 | tf_op jit(solution)/shard_map/pallas_call | solution.py:65
  406.3 3.7 shard_map.245
  (269 shorter events, 127.8 us)
Async XLA Ops:
  12.1 35.4 %copy-start.23 = (bf16[2,1024]{1,0:T(2,128)(2,1)S(1)}, bf16[2,1024]{1,0:T(2,128)(2,1)}, u32[]{:S(2)}) copy-start(bf16[2,1024]{1,0:T(2,128)(2,1)} %param.20) | copy-start | bytes 12292
  12.1 26.5 %all-to-all-start = ((bf16[16,128,256]{2,1,0:T(8,128)(2,1)}), bf16[16,128,256]{2,1,0:T(8,128)(2,1)S(1)}, u32[]{:S(2)}, u32[]{:S(2)}) async-start(bf16[16,128,256]{2,1,0:T(8,128)(2,1)} %get-tuple-element.113), calls=%async_computation | async-start | bytes 2097152 | tf_op jit(solution)/shard_map/all_to_all | solution.py:394
  21.4 37.2 %copy-start.35 = (bf16[2,512]{1,0:T(2,128)(2,1)S(1)}, bf16[2,512]{1,0:T(2,128)(2,1)}, u32[]{:S(2)}) copy-start(bf16[2,512]{1,0:T(2,128)(2,1)} %param.22) | copy-start | bytes 6148
  42.2 11.1 %all-to-all-start.1 = ((bf16[8,16,1024]{2,1,0:T(8,128)(2,1)}), bf16[8,16,1024]{2,1,0:T(8,128)(2,1)S(1)}, u32[]{:S(2)}, u32[]{:S(2)}) async-start(bf16[8,16,1024]{2,1,0:T(8,128)(2,1)} %get-tuple-element.114), calls=%async_computation.1 | async-start | bytes 524288 | tf_op jit(solution)/shard_map/all_to_all | solution.py:394
  55.1 9.5 %all-to-all-start.2 = ((bf16[8,16,1024]{2,1,0:T(8,128)(2,1)}), bf16[8,16,1024]{2,1,0:T(8,128)(2,1)S(1)}, u32[]{:S(2)}, u32[]{:S(2)}) async-start(bf16[8,16,1024]{2,1,0:T(8,128)(2,1)} %get-tuple-element.115), calls=%async_computation.2 | async-start | bytes 524288 | tf_op jit(solution)/shard_map/all_to_all | solution.py:394
  67.5 9.5 %all-to-all-start.3 = ((bf16[8,16,1024]{2,1,0:T(8,128)(2,1)}), bf16[8,16,1024]{2,1,0:T(8,128)(2,1)S(1)}, u32[]{:S(2)}, u32[]{:S(2)}) async-start(bf16[8,16,1024]{2,1,0:T(8,128)(2,1)} %get-tuple-element.116), calls=%async_computation.3 | async-start | bytes 524288 | tf_op jit(solution)/shard_map/all_to_all | solution.py:394
  90.9 27.1 %all-to-all-start.5 = ((bf16[16,128,256]{2,1,0:T(8,128)(2,1)}), bf16[16,128,256]{2,1,0:T(8,128)(2,1)S(1)}, u32[]{:S(2)}, u32[]{:S(2)}) async-start(bf16[16,128,256]{2,1,0:T(8,128)(2,1)} %get-tuple-element.120), calls=%async_computation.5 | async-start | bytes 2097152 | tf_op jit(solution)/shard_map/all_to_all | solution.py:394
  100.8 72.6 %all-gather.2.cloned.1.call-start = ((), (), s32[]{:S(2)}) async-start(), calls=%async_computation.20 | async-start | bytes 1114112 | tf_op jit(solution)/shard_map/all_gather | solution.py:561
  146.3 11.8 %all-to-all-start.8 = ((bf16[8,32,1024]{2,1,0:T(8,128)(2,1)}), bf16[8,32,1024]{2,1,0:T(8,128)(2,1)}, u32[]{:S(2)}, u32[]{:S(2)}) async-start(bf16[8,32,1024]{2,1,0:T(8,128)(2,1)} %get-tuple-element.124), calls=%async_computation.8 | async-start | bytes 1048576 | tf_op jit(solution)/shard_map/all_to_all | solution.py:394
  160.1 11.0 %all-to-all-start.9 = ((bf16[8,32,1024]{2,1,0:T(8,128)(2,1)}), bf16[8,32,1024]{2,1,0:T(8,128)(2,1)S(1)}, u32[]{:S(2)}, u32[]{:S(2)}) async-start(bf16[8,32,1024]{2,1,0:T(8,128)(2,1)} %get-tuple-element.128), calls=%async_computation.9 | async-start | bytes 1048576 | tf_op jit(solution)/shard_map/all_to_all | solution.py:394
  166.0 43.1 %collective-permute-start = (bf16[512,1024]{1,0:T(8,128)(2,1)}, bf16[512,1024]{1,0:T(8,128)(2,1)}, u32[]{:S(2)}, u32[]{:S(2)}) collective-permute-start(bf16[512,1024]{1,0:T(8,128)(2,1)} %dynamic-slice_bitcast_fusion), channel_id=1, source_target_pairs={{0,1},{1,0},{2,3},{3,2},{4,5},{5,4},{6,7},{7,6},{8,9},{9,8},{10,11... | collective-permute-start | bytes 3145736 | tf_op jit(solution)/shard_map/ppermute | solution.py:409
  173.3 22.6 %all-to-all-start.10 = ((bf16[16,144,128]{2,1,0:T(8,128)(2,1)}), bf16[16,144,128]{2,1,0:T(8,128)(2,1)}, u32[]{:S(2)}, u32[]{:S(2)}) async-start(bf16[16,144,128]{2,1,0:T(8,128)(2,1)} %get-tuple-element.135), calls=%async_computation.10 | async-start | bytes 1179648 | tf_op jit(solution)/shard_map/all_to_all | solution.py:394
  204.2 38.1 %collective-permute-start.2 = (bf16[256,1024]{1,0:T(8,128)(2,1)}, bf16[256,1024]{1,0:T(8,128)(2,1)}, u32[]{:S(2)}, u32[]{:S(2)}) collective-permute-start(bf16[256,1024]{1,0:T(8,128)(2,1)} %dynamic-slice_bitcast_fusion.3), channel_id=1, source_target_pairs={{0,1},{1,0},{2,3},{3,2},{4,5},{5,4},{6,7},{7,6},{8,9},{9,8},{10,11... | collective-permute-start | bytes 1572872 | tf_op jit(solution)/shard_map/ppermute | solution.py:409
  205.6 10.9 %all-to-all-start.11 = ((bf16[8,16,1024]{2,1,0:T(8,128)(2,1)}), bf16[8,16,1024]{2,1,0:T(8,128)(2,1)S(1)}, u32[]{:S(2)}, u32[]{:S(2)}) async-start(bf16[8,16,1024]{2,1,0:T(8,128)(2,1)} %get-tuple-element.138), calls=%async_computation.11 | async-start | bytes 524288 | tf_op jit(solution)/shard_map/all_to_all | solution.py:394
  218.3 10.2 %all-to-all-start.12 = ((bf16[8,16,1024]{2,1,0:T(8,128)(2,1)}), bf16[8,16,1024]{2,1,0:T(8,128)(2,1)S(1)}, u32[]{:S(2)}, u32[]{:S(2)}) async-start(bf16[8,16,1024]{2,1,0:T(8,128)(2,1)} %get-tuple-element.142), calls=%async_computation.12 | async-start | bytes 524288 | tf_op jit(solution)/shard_map/all_to_all | solution.py:394
  222.5 22.3 %collective-permute-start.1 = (bf16[256,1024]{1,0:T(8,128)(2,1)}, bf16[256,1024]{1,0:T(8,128)(2,1)}, u32[]{:S(2)}, u32[]{:S(2)}) collective-permute-start(bf16[256,1024]{1,0:T(8,128)(2,1)} %dynamic-slice_bitcast_fusion.4), channel_id=1, source_target_pairs={{0,2},{1,3},{2,0},{3,1},{4,6},{5,7},{6,4},{7,5},{8,10},{9,11},{10,... | collective-permute-start | bytes 1572872 | tf_op jit(solution)/shard_map/ppermute | solution.py:409
  231.7 15.2 %all-to-all-start.13 = ((bf16[8,16,1024]{2,1,0:T(8,128)(2,1)}), bf16[8,16,1024]{2,1,0:T(8,128)(2,1)S(1)}, u32[]{:S(2)}, u32[]{:S(2)}) async-start(bf16[8,16,1024]{2,1,0:T(8,128)(2,1)} %get-tuple-element.144), calls=%async_computation.13 | async-start | bytes 524288 | tf_op jit(solution)/shard_map/all_to_all | solution.py:394
  240.9 19.3 %collective-permute-start.6 = (bf16[256,1024]{1,0:T(8,128)(2,1)}, bf16[256,1024]{1,0:T(8,128)(2,1)}, u32[]{:S(2)}, u32[]{:S(2)}) collective-permute-start(bf16[256,1024]{1,0:T(8,128)(2,1)} %dynamic-slice_bitcast_fusion.1), channel_id=1, source_target_pairs={{0,1},{1,0},{2,3},{3,2},{4,5},{5,4},{6,7},{7,6},{8,9},{9,8},{10,11... | collective-permute-start | bytes 1572872 | tf_op jit(solution)/shard_map/ppermute | solution.py:409
  243.5 9.5 %collective-permute-start.3 = (bf16[128,1024]{1,0:T(8,128)(2,1)S(1)}, bf16[128,1024]{1,0:T(8,128)(2,1)S(1)}, u32[]{:S(2)}, u32[]{:S(2)}) collective-permute-start(bf16[128,1024]{1,0:T(8,128)(2,1)S(1)} %dynamic-slice_bitcast_fusion.7), channel_id=1, source_target_pairs={{0,2},{1,3},{2,0},{3,1},{4,6},{5,7},{6,4},{7,5},{8,10},{9,11},{10,... | collective-permute-start | bytes 786440 | tf_op jit(solution)/shard_map/ppermute | solution.py:409
  244.5 18.6 %collective-permute-start.4 = (bf16[256,1024]{1,0:T(8,128)(2,1)}, bf16[256,1024]{1,0:T(8,128)(2,1)}, u32[]{:S(2)}, u32[]{:S(2)}) collective-permute-start(bf16[256,1024]{1,0:T(8,128)(2,1)} %dynamic-slice_bitcast_fusion.2), channel_id=1, source_target_pairs={{0,1},{1,0},{2,3},{3,2},{4,5},{5,4},{6,7},{7,6},{8,9},{9,8},{10,11... | collective-permute-start | bytes 1572872 | tf_op jit(solution)/shard_map/ppermute | solution.py:409
  254.8 13.2 %all-to-all-start.14 = ((bf16[8,16,1024]{2,1,0:T(8,128)(2,1)}), bf16[8,16,1024]{2,1,0:T(8,128)(2,1)S(1)}, u32[]{:S(2)}, u32[]{:S(2)}) async-start(bf16[8,16,1024]{2,1,0:T(8,128)(2,1)} %get-tuple-element.158), calls=%async_computation.14 | async-start | bytes 524288 | tf_op jit(solution)/shard_map/all_to_all | solution.py:394
  260.1 52.2 %all-reduce.4.cloned.1.call-start = ((), (), s32[]{:S(2)}) async-start(), calls=%async_computation.21 | async-start | bytes 1572864 | tf_op jit(solution)/shard_map/psum | solution.py:446
  262.3 10.0 %collective-permute-start.7 = (bf16[128,1024]{1,0:T(8,128)(2,1)}, bf16[128,1024]{1,0:T(8,128)(2,1)}, u32[]{:S(2)}, u32[]{:S(2)}) collective-permute-start(bf16[128,1024]{1,0:T(8,128)(2,1)} %dynamic-slice_bitcast_fusion.5), channel_id=1, source_target_pairs={{0,2},{1,3},{2,0},{3,1},{4,6},{5,7},{6,4},{7,5},{8,10},{9,11},{10,... | collective-permute-start | bytes 786440 | tf_op jit(solution)/shard_map/ppermute | solution.py:409
  265.2 12.7 %collective-permute-start.5 = (bf16[128,1024]{1,0:T(8,128)(2,1)S(1)}, bf16[128,1024]{1,0:T(8,128)(2,1)}, u32[]{:S(2)}, u32[]{:S(2)}) collective-permute-start(bf16[128,1024]{1,0:T(8,128)(2,1)S(1)} %dynamic-slice_bitcast_fusion.6), channel_id=1, source_target_pairs={{0,2},{1,3},{2,0},{3,1},{4,6},{5,7},{6,4},{7,5},{8,10},{9,11},{10,... | collective-permute-start | bytes 786440 | tf_op jit(solution)/shard_map/ppermute | solution.py:409
  278.9 17.9 %all-to-all-start.15 = ((bf16[16,144,128]{2,1,0:T(8,128)(2,1)}), bf16[16,144,128]{2,1,0:T(8,128)(2,1)S(1)}, u32[]{:S(2)}, u32[]{:S(2)}) async-start(bf16[16,144,128]{2,1,0:T(8,128)(2,1)} %get-tuple-element.165), calls=%async_computation.15 | async-start | bytes 1179648 | tf_op jit(solution)/shard_map/all_to_all | solution.py:394
  288.2 34.7 %collective-permute-start.15 = (bf16[64,1024]{1,0:T(8,128)(2,1)S(1)}, bf16[64,1024]{1,0:T(8,128)(2,1)S(1)}, u32[]{:S(2)}, u32[]{:S(2)}) collective-permute-start(bf16[64,1024]{1,0:T(8,128)(2,1)S(1)} %dynamic-slice_bitcast_fusion.8), channel_id=1, source_target_pairs={{0,4},{1,5},{2,6},{3,7},{4,0},{5,1},{6,2},{7,3},{8,12},{9,13},{10,... | collective-permute-start | bytes 393224 | tf_op jit(solution)/shard_map/ppermute | solution.py:409
  289.7 35.9 %collective-permute-start.9 = (bf16[64,1024]{1,0:T(8,128)(2,1)S(1)}, bf16[64,1024]{1,0:T(8,128)(2,1)S(1)}, u32[]{:S(2)}, u32[]{:S(2)}) collective-permute-start(bf16[64,1024]{1,0:T(8,128)(2,1)S(1)} %dynamic-slice_bitcast_fusion.9), channel_id=1, source_target_pairs={{0,12},{1,13},{2,14},{3,15},{4,8},{5,9},{6,10},{7,11},{8,4},{9,5},... | collective-permute-start | bytes 393224 | tf_op jit(solution)/shard_map/ppermute | solution.py:409
  312.4 14.2 %all-to-all-start.16 = ((bf16[8,16,1024]{2,1,0:T(8,128)(2,1)}), bf16[8,16,1024]{2,1,0:T(8,128)(2,1)S(1)}, u32[]{:S(2)}, u32[]{:S(2)}) async-start(bf16[8,16,1024]{2,1,0:T(8,128)(2,1)} %get-tuple-element.171), calls=%async_computation.16 | async-start | bytes 524288 | tf_op jit(solution)/shard_map/all_to_all | solution.py:394
  317.4 40.0 %collective-permute-start.21 = (bf16[256,1024]{1,0:T(8,128)(2,1)}, bf16[256,1024]{1,0:T(8,128)(2,1)}, u32[]{:S(2)}, u32[]{:S(2)}) collective-permute-start(bf16[256,1024]{1,0:T(8,128)(2,1)} %get-tuple-element.201), channel_id=1, source_target_pairs={{0,2},{1,3},{2,0},{3,1},{4,6},{5,7},{6,4},{7,5},{8,10},{9,11},{10,... | collective-permute-start | bytes 1572872 | tf_op jit(solution)/shard_map/ppermute | solution.py:409
  323.0 13.0 %collective-permute-start.16 = (bf16[32,1024]{1,0:T(8,128)(2,1)S(1)}, bf16[32,1024]{1,0:T(8,128)(2,1)S(1)}, u32[]{:S(2)}, u32[]{:S(2)}) collective-permute-start(bf16[32,1024]{1,0:T(8,128)(2,1)S(1)} %dynamic-slice_bitcast_fusion.10), channel_id=1, source_target_pairs={{0,12},{1,13},{2,14},{3,15},{4,8},{5,9},{6,10},{7,11},{8,4},{9,5},... | collective-permute-start | bytes 196616 | tf_op jit(solution)/shard_map/ppermute | solution.py:409
  325.7 11.4 %collective-permute-start.10 = (bf16[32,1024]{1,0:T(8,128)(2,1)S(1)}, bf16[32,1024]{1,0:T(8,128)(2,1)S(1)}, u32[]{:S(2)}, u32[]{:S(2)}) collective-permute-start(bf16[32,1024]{1,0:T(8,128)(2,1)S(1)} %dynamic-slice_bitcast_fusion.11), channel_id=1, source_target_pairs={{0,4},{1,5},{2,6},{3,7},{4,0},{5,1},{6,2},{7,3},{8,12},{9,13},{10,... | collective-permute-start | bytes 196616 | tf_op jit(solution)/shard_map/ppermute | solution.py:409
  331.5 11.4 %all-to-all-start.17 = ((bf16[8,24,1024]{2,1,0:T(8,128)(2,1)}), bf16[8,24,1024]{2,1,0:T(8,128)(2,1)S(1)}, u32[]{:S(2)}, u32[]{:S(2)}) async-start(bf16[8,24,1024]{2,1,0:T(8,128)(2,1)} %pad_maximum_fusion.4), calls=%async_computation.17 | async-start | bytes 786432 | tf_op jit(solution)/shard_map/all_to_all | solution.py:394
  336.0 4.4 %collective-permute-start.17 = (bf16[32,1024]{1,0:T(8,128)(2,1)S(1)}, bf16[32,1024]{1,0:T(8,128)(2,1)S(1)}, u32[]{:S(2)}, u32[]{:S(2)}) collective-permute-start(bf16[32,1024]{1,0:T(8,128)(2,1)S(1)} %fusion.15), channel_id=1, source_target_pairs={{0,12},{1,13},{2,14},{3,15},{4,8},{5,9},{6,10},{7,11},{8,4},{9,5},... | collective-permute-start | bytes 196616 | tf_op jit(solution)/shard_map/ppermute | solution.py:409
  337.2 3.6 collective-permute-start.11
  340.5 10.0 %collective-permute-start.18 = (bf16[64,1024]{1,0:T(8,128)(2,1)S(1)}, bf16[64,1024]{1,0:T(8,128)(2,1)S(1)}, u32[]{:S(2)}, u32[]{:S(2)}) collective-permute-start(bf16[64,1024]{1,0:T(8,128)(2,1)S(1)} %pad_maximum_fusion.8), channel_id=1, source_target_pairs={{0,4},{1,5},{2,6},{3,7},{4,0},{5,1},{6,2},{7,3},{8,12},{9,13},{10,... | collective-permute-start | bytes 393224 | tf_op jit(solution)/shard_map/ppermute | solution.py:409
  341.4 9.1 %collective-permute-start.12 = (bf16[64,1024]{1,0:T(8,128)(2,1)}, bf16[64,1024]{1,0:T(8,128)(2,1)S(1)}, u32[]{:S(2)}, u32[]{:S(2)}) collective-permute-start(bf16[64,1024]{1,0:T(8,128)(2,1)} %pad_maximum_fusion.7), channel_id=1, source_target_pairs={{0,12},{1,13},{2,14},{3,15},{4,8},{5,9},{6,10},{7,11},{8,4},{9,5},... | collective-permute-start | bytes 393224 | tf_op jit(solution)/shard_map/ppermute | solution.py:409
  342.8 46.9 %copy-start.14 = (bf16[8,24,1024]{2,1,0:T(8,128)(2,1)}, bf16[8,24,1024]{2,1,0:T(8,128)(2,1)S(1)}, u32[]{:S(2)}) copy-start(bf16[8,24,1024]{2,1,0:T(8,128)(2,1)S(1)} %all-to-all-done.17) | copy-start | bytes 1179652
  344.7 7.3 %collective-permute-start.8 = (bf16[8,8,4224]{2,1,0:T(8,128)(2,1)S(1)}, bf16[8,8,4224]{2,1,0:T(8,128)(2,1)S(1)}, u32[]{:S(2)}, u32[]{:S(2)}) collective-permute-start(bf16[8,8,4224]{2,1,0:T(8,128)(2,1)S(1)} %fusion.7), channel_id=1, source_target_pairs={{0,1},{1,0},{2,3},{3,2},{4,5},{5,4},{6,7},{7,6},{8,9},{9,8},{10,11... | collective-permute-start | bytes 1622024 | tf_op jit(solution)/shard_map/ppermute | solution.py:409
  353.0 26.4 %all-to-all-start.18 = ((bf16[8,8,4224]{2,1,0:T(8,128)(2,1)}), bf16[8,8,4224]{2,1,0:T(8,128)(2,1)S(1)}, u32[]{:S(2)}, u32[]{:S(2)}) async-start(bf16[8,8,4224]{2,1,0:T(8,128)(2,1)} %fusion.1), calls=%async_computation.18 | async-start | bytes 1081344 | tf_op jit(solution)/shard_map/all_to_all | solution.py:451
  357.4 14.1 %collective-permute-start.19 = (bf16[128,1024]{1,0:T(8,128)(2,1)S(1)}, bf16[128,1024]{1,0:T(8,128)(2,1)S(1)}, u32[]{:S(2)}, u32[]{:S(2)}) collective-permute-start(bf16[128,1024]{1,0:T(8,128)(2,1)S(1)} %pad_maximum_fusion.6), channel_id=1, source_target_pairs={{0,2},{1,3},{2,0},{3,1},{4,6},{5,7},{6,4},{7,5},{8,10},{9,11},{10,... | collective-permute-start | bytes 786440 | tf_op jit(solution)/shard_map/ppermute | solution.py:409
  361.7 28.0 %collective-permute-start.22 = (bf16[512,1024]{1,0:T(8,128)(2,1)S(1)}, bf16[512,1024]{1,0:T(8,128)(2,1)}, u32[]{:S(2)}, u32[]{:S(2)}) collective-permute-start(bf16[512,1024]{1,0:T(8,128)(2,1)S(1)} %pad_maximum_fusion.own_ref), channel_id=1, source_target_pairs={{0,1},{1,0},{2,3},{3,2},{4,5},{5,4},{6,7},{7,6},{8,9},{9,8},{10,11... | collective-permute-start | bytes 3145736 | tf_op jit(solution)/shard_map/ppermute | solution.py:409
  363.5 13.6 %collective-permute-start.13 = (bf16[128,1024]{1,0:T(8,128)(2,1)S(1)}, bf16[128,1024]{1,0:T(8,128)(2,1)S(1)}, u32[]{:S(2)}, u32[]{:S(2)}) collective-permute-start(bf16[128,1024]{1,0:T(8,128)(2,1)S(1)} %pad_maximum_fusion.5), channel_id=1, source_target_pairs={{0,2},{1,3},{2,0},{3,1},{4,6},{5,7},{6,4},{7,5},{8,10},{9,11},{10,... | collective-permute-start | bytes 786440 | tf_op jit(solution)/shard_map/ppermute | solution.py:409
  371.6 18.1 %collective-permute-start.20 = (bf16[256,1024]{1,0:T(8,128)(2,1)S(1)}, bf16[256,1024]{1,0:T(8,128)(2,1)}, u32[]{:S(2)}, u32[]{:S(2)}) collective-permute-start(bf16[256,1024]{1,0:T(8,128)(2,1)S(1)} %pad_maximum_fusion.2.f_own), channel_id=1, source_target_pairs={{0,1},{1,0},{2,3},{3,2},{4,5},{5,4},{6,7},{7,6},{8,9},{9,8},{10,11... | collective-permute-start | bytes 1572872 | tf_op jit(solution)/shard_map/ppermute | solution.py:409
  377.2 12.5 %collective-permute-start.14 = (bf16[256,1024]{1,0:T(8,128)(2,1)S(1)}, bf16[256,1024]{1,0:T(8,128)(2,1)}, u32[]{:S(2)}, u32[]{:S(2)}) collective-permute-start(bf16[256,1024]{1,0:T(8,128)(2,1)S(1)} %pad_maximum_fusion.1.p_own), channel_id=1, source_target_pairs={{0,1},{1,0},{2,3},{3,2},{4,5},{5,4},{6,7},{7,6},{8,9},{9,8},{10,11... | collective-permute-start | bytes 1572872 | tf_op jit(solution)/shard_map/ppermute | solution.py:409
  381.8 14.6 %all-to-all-start.19 = ((bf16[8,8,4224]{2,1,0:T(8,128)(2,1)}), bf16[8,8,4224]{2,1,0:T(8,128)(2,1)S(1)}, u32[]{:S(2)}, u32[]{:S(2)}) async-start(bf16[8,8,4224]{2,1,0:T(8,128)(2,1)} %broadcast_in_dim.15), calls=%async_computation.19 | async-start | bytes 1081344 | tf_op jit(solution)/shard_map/all_to_all | solution.py:451
  385.8 15.1 %collective-permute-start.24 = (bf16[128,1024]{1,0:T(8,128)(2,1)}, bf16[128,1024]{1,0:T(8,128)(2,1)S(1)}, u32[]{:S(2)}, u32[]{:S(2)}) collective-permute-start(bf16[128,1024]{1,0:T(8,128)(2,1)} %get-tuple-element.206), channel_id=1, source_target_pairs={{0,2},{1,3},{2,0},{3,1},{4,6},{5,7},{6,4},{7,5},{8,10},{9,11},{10,... | collective-permute-start | bytes 786440 | tf_op jit(solution)/shard_map/ppermute | solution.py:409
  396.4 5.8 %collective-permute-start.23 = (bf16[8,8,4224]{2,1,0:T(8,128)(2,1)S(1)}, bf16[8,8,4224]{2,1,0:T(8,128)(2,1)S(1)}, u32[]{:S(2)}, u32[]{:S(2)}) collective-permute-start(bf16[8,8,4224]{2,1,0:T(8,128)(2,1)S(1)} %all-to-all-done.19.late_own), channel_id=1, source_target_pairs={{0,1},{1,0},{2,3},{3,2},{4,5},{5,4},{6,7},{7,6},{8,9},{9,8},{10,11... | collective-permute-start | bytes 1622024 | tf_op jit(solution)/shard_map/ppermute | solution.py:409
  401.0 4.5 %collective-permute-start.25 = (bf16[256,1024]{1,0:T(8,128)(2,1)S(1)}, bf16[256,1024]{1,0:T(8,128)(2,1)S(1)}, u32[]{:S(2)}, u32[]{:S(2)}) collective-permute-start(bf16[256,1024]{1,0:T(8,128)(2,1)S(1)} %pad_maximum_fusion.3.own_ref), channel_id=1, source_target_pairs={{0,1},{1,0},{2,3},{3,2},{4,5},{5,4},{6,7},{7,6},{8,9},{9,8},{10,11... | collective-permute-start | bytes 1572872 | tf_op jit(solution)/shard_map/ppermute | solution.py:409
  (40 other events, 535.8 us)
Sparse Core Ops, SparseCore 0:
  104.0 44.8 all-gather.1
  268.1 44.1 all-reduce.3

commit v2 on v0

--- a/solution.py
+++ b/solution.py
@@ -642,11 +642,8 @@
             logs,
             blocks={0: ((slots, share, width), lambda i: (0, 0, 0))},
         )
-        if not layer:
-            starts = [
-                halve(halve(part, CORE), DEPTH) for part in (end_pack[:hidden], end_pack[hidden:])
-            ]
-            sent, starts = lax.optimization_barrier((sent, starts))
+        if layer:
+            sent, q_every = lax.optimization_barrier((sent, q_every))
         go_all = swap_all(sent, "dp")
         (g_q,) = call(
             query_back_kernel,
@@ -727,7 +724,7 @@
     arrived = swap_chips(half)
     mine = jnp.sum(arrived.astype(F32), 0).astype(BF16)
     late = swap_chips(jnp.broadcast_to(mine, (ranks // 2,) + mine.shape))
-    late_got = swap(late, CORE)
+    starts = [halve(halve(part, CORE, grad_b), DEPTH, g_o) for part in (end_pack[:hidden], end_pack[hidden:])]
     events = (g_kv, grad, half)
     end_parts = [part for turn, value in enumerate(starts) for part in finish_sums(value, turn, events)]
     end_last, attend_last = [rejoin(after(part, grad), DEPTH, None, half) for part in done[1]]
@@ -743,6 +740,9 @@
         swap(end_last, CORE),
         room=40,
     )
+    attend_got = swap(attend_last, CORE)
+    late, attend_got, g_w_proj, g_w_fc = lax.optimization_barrier((late, attend_got, g_w_proj, g_w_fc))
+    late_got = swap(late, CORE)
     g_w_out, g_w_qkv = call(
         finish_attend_kernel,
         [shape((layers, local, width), F32), shape((layers, 3, width, local), F32)],
@@ -751,7 +751,7 @@
         late,
         late_got,
         attend_last,
-        swap(attend_last, CORE),
+        attend_got,
         room=24,
     )
     ours, theirs = late[:, :, wide : wide + each], late_got[:, :, wide : wide + each]

time: 425 us -> 405 us (0.953)
  blocking collectives: 55.3 us -> 28.5 us
  starting transfers between devices: 113 us -> 128 us
  waiting for transfers between devices: 111 us -> 101 us
    all_to_all x4 -> x3, blocking collectives: 55.3 us -> 28.5 us  [swap_all(): return lax.all_to_all(value, axis, 0, 0)]
    psum x1, waiting for transfers between devices: 22.1 us -> 0.01 us  [sum_over_x(): return lax.psum(values, 'dp', axis_index_groups=groups)]
    all_to_all x14 -> x15, waiting for transfers between devices: 57.4 us -> 68.7 us  [swap_all(): return lax.all_to_all(value, axis, 0, 0)]
    all_to_all x14 -> x15, starting transfers between devices: 65.9 us -> 76.9 us  [swap_all(): return lax.all_to_all(value, axis, 0, 0)]
    ppermute x26, waiting for transfers between devices: 17.8 us -> 27.3 us  [swap(): lax.ppermute(value, 'dp', [(i, i ^ flip) for i in range(lax.axis_size('dp...]
    all_gather x1, waiting for transfers between devices: 5.88 us -> 0.01 us  [body(): lax.all_gather(jnp.concatenate([kept[3] for kept in saved], 1), 'dp', axi...]
    another operation x10, other arithmetic: 2.91 us -> 8.16 us
  transfers between devices with their start and end apart: 44 -> 45, of which waited for: 19 -> 17; matrix products, arithmetic and copies ran while one was open for 12% -> 12% of each run, Pallas kernels for 11% -> 14%
where the time goes in v2:
time: 405 us; the launch traced here: 401 us
  starting transfers between devices  128 us (32%)
  waiting for transfers between devices  101 us (25%)
  Pallas kernels  74.1 us (18%)
  other arithmetic  34.8 us (9%)
  blocking collectives  28.5 us (7%)
  local copies, waits for them, and re-layouts  20.1 us (5%)
  between operations  15 us (4%)
    all_to_all x15, starting transfers between devices, swap_all(): return lax.all_to_all(value, axis, 0, 0)  76.9 us
    pallas_call x26, Pallas kernels, call(): pl.pallas_call(kernel, grid=(1,), in_specs=[spec(index, arg) for index, a...  74.1 us
    all_to_all x15, waiting for transfers between devices, swap_all(): return lax.all_to_all(value, axis, 0, 0)  68.7 us
    ppermute x26, starting transfers between devices, swap(): lax.ppermute(value, 'dp', [(i, i ^ flip) for i in range(lax.axis_size('dp...  40.6 us
    all_to_all x3, blocking collectives, swap_all(): return lax.all_to_all(value, axis, 0, 0)  28.5 us
    ppermute x26, waiting for transfers between devices, swap(): lax.ppermute(value, 'dp', [(i, i ^ flip) for i in range(lax.axis_size('dp...  27.3 us
    convert_element_type x13, other arithmetic, halve(): return (mine.astype(F32) + got.astype(F32)).astype(BF16)  10.7 us
    all_to_all x2, starting transfers between devices, swap_chips(): return lax.all_to_all(value, 'dp', 0, 0, axis_index_groups=groups)  10.5 us
  transfers between devices with their start and end apart: 45, of which 17 were waited for; matrix products, arithmetic and copies ran while one was open for 12% of the time, Pallas kernels for 14%

profile of v2, /device:TPU:1, one launch (start us, length us, event | category | flops | bytes accessed | tf_op | source)
XLA Modules:
  0.0 401.3 jit_solution(17096624561095724149)
XLA Ops:
  12.1 9.3 %all-to-all-start = ((bf16[16,128,256]{2,1,0:T(8,128)(2,1)}), bf16[16,128,256]{2,1,0:T(8,128)(2,1)S(1)}, u32[]{:S(2)}, u32[]{:S(2)}) async-start(bf16[16,128,256]{2,1,0:T(8,128)(2,1)} %get-tuple-element.111), calls=%async_computation | async-start | bytes 2097152 | tf_op jit(solution)/shard_map/all_to_all | solution.py:394
  22.9 15.7 %all-to-all-done.kv_ref = bf16[16,128,256]{2,1,0:T(8,128)(2,1)S(1)} async-done(((bf16[16,128,256]{2,1,0:T(8,128)(2,1)}), bf16[16,128,256]{2,1,0:T(8,128)(2,1)S(1)}, u32[]{:S(2)}, u32[]{:S(2)}) %all-to-all-start) | async-done | bytes 1048608 | tf_op jit(solution)/shard_map/all_to_all | solution.py:394
  38.6 3.6 shard_map.221
  42.2 4.6 %all-to-all-start.1 = ((bf16[8,16,1024]{2,1,0:T(8,128)(2,1)}), bf16[8,16,1024]{2,1,0:T(8,128)(2,1)S(1)}, u32[]{:S(2)}, u32[]{:S(2)}) async-start(bf16[8,16,1024]{2,1,0:T(8,128)(2,1)} %get-tuple-element.112), calls=%async_computation.1 | async-start | bytes 524288 | tf_op jit(solution)/shard_map/all_to_all | solution.py:394
  48.1 5.2 %all-to-all-done.1.parts_ref = bf16[8,16,1024]{2,1,0:T(8,128)(2,1)S(1)} async-done(((bf16[8,16,1024]{2,1,0:T(8,128)(2,1)}), bf16[8,16,1024]{2,1,0:T(8,128)(2,1)S(1)}, u32[]{:S(2)}, u32[]{:S(2)}) %all-to-all-start.1) | async-done | bytes 262176 | tf_op jit(solution)/shard_map/all_to_all | solution.py:394
  55.1 3.4 all-to-all-start.2
  59.2 5.5 %all-to-all-done.2 = bf16[8,16,1024]{2,1,0:T(8,128)(2,1)S(1)} async-done(((bf16[8,16,1024]{2,1,0:T(8,128)(2,1)}), bf16[8,16,1024]{2,1,0:T(8,128)(2,1)S(1)}, u32[]{:S(2)}, u32[]{:S(2)}) %all-to-all-start.2) | async-done | bytes 262176 | tf_op jit(solution)/shard_map/all_to_all | solution.py:394
  67.5 3.4 all-to-all-start.3
  71.5 5.5 %all-to-all-done.3.parts_ref = bf16[8,16,1024]{2,1,0:T(8,128)(2,1)S(1)} async-done(((bf16[8,16,1024]{2,1,0:T(8,128)(2,1)}), bf16[8,16,1024]{2,1,0:T(8,128)(2,1)S(1)}, u32[]{:S(2)}, u32[]{:S(2)}) %all-to-all-start.3) | async-done | bytes 262176 | tf_op jit(solution)/shard_map/all_to_all | solution.py:394
  78.8 9.5 %all_to_all.100 = bf16[8,16,1024]{2,1,0:T(8,128)(2,1)S(1)} all-to-all(bf16[8,16,1024]{2,1,0:T(8,128)(2,1)} %get-tuple-element.116), channel_id=1, replica_groups=mesh['tensor'=8,'dp'=16] {'tensor'}, dimensions={0} | all-to-all | bytes 524288 | tf_op jit(solution)/shard_map/all_to_all | solution.py:394
  90.9 9.9 %all-to-all-start.5 = ((bf16[16,128,256]{2,1,0:T(8,128)(2,1)}), bf16[16,128,256]{2,1,0:T(8,128)(2,1)S(1)}, u32[]{:S(2)}, u32[]{:S(2)}) async-start(bf16[16,128,256]{2,1,0:T(8,128)(2,1)} %get-tuple-element.118), calls=%async_computation.5 | async-start | bytes 2097152 | tf_op jit(solution)/shard_map/all_to_all | solution.py:394
  101.5 16.5 %all-to-all-done.5.kv_ref = bf16[16,128,256]{2,1,0:T(8,128)(2,1)S(1)} async-done(((bf16[16,128,256]{2,1,0:T(8,128)(2,1)}), bf16[16,128,256]{2,1,0:T(8,128)(2,1)S(1)}, u32[]{:S(2)}, u32[]{:S(2)}) %all-to-all-start.5) | async-done | bytes 1048608 | tf_op jit(solution)/shard_map/all_to_all | solution.py:394
  118.0 3.6 shard_map.226
  121.6 9.6 %all_to_all.101.parts_ref = bf16[8,16,1024]{2,1,0:T(8,128)(2,1)S(1)} all-to-all(bf16[8,16,1024]{2,1,0:T(8,128)(2,1)} %get-tuple-element.119), channel_id=1, replica_groups=mesh['tensor'=8,'dp'=16] {'tensor'}, dimensions={0} | all-to-all | bytes 524288 | tf_op jit(solution)/shard_map/all_to_all | solution.py:394
  133.0 9.5 %all_to_all.102 = bf16[8,16,1024]{2,1,0:T(8,128)(2,1)S(1)} all-to-all(bf16[8,16,1024]{2,1,0:T(8,128)(2,1)} %get-tuple-element.121), channel_id=1, replica_groups=mesh['tensor'=8,'dp'=16] {'tensor'}, dimensions={0} | all-to-all | bytes 524288 | tf_op jit(solution)/shard_map/all_to_all | solution.py:394
  142.5 3.8 shard_map.228
  146.3 4.1 %all-to-all-start.8 = ((bf16[8,32,1024]{2,1,0:T(8,128)(2,1)}), bf16[8,32,1024]{2,1,0:T(8,128)(2,1)}, u32[]{:S(2)}, u32[]{:S(2)}) async-start(bf16[8,32,1024]{2,1,0:T(8,128)(2,1)} %get-tuple-element.122), calls=%async_computation.8 | async-start | bytes 1048576 | tf_op jit(solution)/shard_map/all_to_all | solution.py:394
  151.1 3.0 shard_map.243
  154.2 3.9 all-to-all-done.8.parts_ref
  160.1 3.5 all-to-all-start.9
  166.0 4.2 %collective-permute-start.21 = (bf16[512,1024]{1,0:T(8,128)(2,1)}, bf16[512,1024]{1,0:T(8,128)(2,1)}, u32[]{:S(2)}, u32[]{:S(2)}) collective-permute-start(bf16[512,1024]{1,0:T(8,128)(2,1)} %dynamic-slice_bitcast_fusion), channel_id=1, source_target_pairs={{0,1},{1,0},{2,3},{3,2},{4,5},{5,4},{6,7},{7,6},{8,9},{9,8},{10,11... | collective-permute-start | bytes 3145736 | tf_op jit(solution)/shard_map/ppermute | solution.py:409
  173.3 10.8 %all-to-all-start.10 = ((bf16[16,144,128]{2,1,0:T(8,128)(2,1)}), bf16[16,144,128]{2,1,0:T(8,128)(2,1)}, u32[]{:S(2)}, u32[]{:S(2)}) async-start(bf16[16,144,128]{2,1,0:T(8,128)(2,1)} %get-tuple-element.133), calls=%async_computation.10 | async-start | bytes 1179648 | tf_op jit(solution)/shard_map/all_to_all | solution.py:394
  189.6 6.3 %all-to-all-done.10.got_ref = bf16[16,144,128]{2,1,0:T(8,128)(2,1)} async-done(((bf16[16,144,128]{2,1,0:T(8,128)(2,1)}), bf16[16,144,128]{2,1,0:T(8,128)(2,1)}, u32[]{:S(2)}, u32[]{:S(2)}) %all-to-all-start.10) | async-done | bytes 589856 | tf_op jit(solution)/shard_map/all_to_all | solution.py:394
  200.2 4.0 shard_map.232
  204.2 3.4 all-to-all-start.11
  216.9 3.8 all-to-all-start.12
  224.4 3.6 all-to-all-done.12
  228.1 3.2 shard_map.234
  231.3 3.4 all-to-all-start.13
  234.7 3.0 shard_map.241
  251.5 4.7 %all-to-all-start.14 = ((bf16[8,16,1024]{2,1,0:T(8,128)(2,1)}), bf16[8,16,1024]{2,1,0:T(8,128)(2,1)S(1)}, u32[]{:S(2)}, u32[]{:S(2)}) async-start(bf16[8,16,1024]{2,1,0:T(8,128)(2,1)} %get-tuple-element.146), calls=%async_computation.14 | async-start | bytes 524288 | tf_op jit(solution)/shard_map/all_to_all | solution.py:394
  259.4 4.3 %all-to-all-done.14.gy_ref = bf16[8,16,1024]{2,1,0:T(8,128)(2,1)S(1)} async-done(((bf16[8,16,1024]{2,1,0:T(8,128)(2,1)}), bf16[8,16,1024]{2,1,0:T(8,128)(2,1)S(1)}, u32[]{:S(2)}, u32[]{:S(2)}) %all-to-all-start.14) | async-done | bytes 262176 | tf_op jit(solution)/shard_map/all_to_all | solution.py:394
  265.8 4.5 %all-to-all-start.15 = ((bf16[16,144,128]{2,1,0:T(8,128)(2,1)}), bf16[16,144,128]{2,1,0:T(8,128)(2,1)S(1)}, u32[]{:S(2)}, u32[]{:S(2)}) async-start(bf16[16,144,128]{2,1,0:T(8,128)(2,1)} %get-tuple-element.149), calls=%async_computation.15 | async-start | bytes 1179648 | tf_op jit(solution)/shard_map/all_to_all | solution.py:394
  270.4 3.0 shard_map.237.gq_ref
  274.6 3.0 collective-permute-start.14
  279.1 9.5 %collective-permute-done.14 = bf16[128,1024]{1,0:T(8,128)(2,1)S(1)} collective-permute-done((bf16[128,1024]{1,0:T(8,128)(2,1)S(1)}, bf16[128,1024]{1,0:T(8,128)(2,1)S(1)}, u32[]{:S(2)}, u32[]{:S(2)}) %collective-permute-start.14) | collective-permute-done | bytes 262176 | tf_op jit(solution)/shard_map/ppermute | solution.py:409
  288.8 5.4 %collective-permute-done.6 = bf16[128,1024]{1,0:T(8,128)(2,1)S(1)} collective-permute-done((bf16[128,1024]{1,0:T(8,128)(2,1)S(1)}, bf16[128,1024]{1,0:T(8,128)(2,1)S(1)}, u32[]{:S(2)}, u32[]{:S(2)}) %collective-permute-start.6) | collective-permute-done | bytes 262176 | tf_op jit(solution)/shard_map/ppermute | solution.py:409
  295.6 3.9 shard_map.238
  299.5 3.6 all-to-all-start.16
  315.9 4.4 %all-to-all-start.17 = ((bf16[8,24,1024]{2,1,0:T(8,128)(2,1)}), bf16[8,24,1024]{2,1,0:T(8,128)(2,1)S(1)}, u32[]{:S(2)}, u32[]{:S(2)}) async-start(bf16[8,24,1024]{2,1,0:T(8,128)(2,1)} %pad_maximum_fusion.4), calls=%async_computation.17 | async-start | bytes 786432 | tf_op jit(solution)/shard_map/all_to_all | solution.py:394
  329.7 5.7 %collective-permute-start = (bf16[8,8,4224]{2,1,0:T(8,128)(2,1)S(1)}, bf16[8,8,4224]{2,1,0:T(8,128)(2,1)S(1)}, u32[]{:S(2)}, u32[]{:S(2)}) collective-permute-start(bf16[8,8,4224]{2,1,0:T(8,128)(2,1)S(1)} %fusion.7), channel_id=1, source_target_pairs={{0,1},{1,0},{2,3},{3,2},{4,5},{5,4},{6,7},{7,6},{8,9},{9,8},{10,11... | collective-permute-start | bytes 1622024 | tf_op jit(solution)/shard_map/ppermute | solution.py:409
  337.8 6.5 %all-to-all-start.18 = ((bf16[8,8,4224]{2,1,0:T(8,128)(2,1)}), bf16[8,8,4224]{2,1,0:T(8,128)(2,1)S(1)}, u32[]{:S(2)}, u32[]{:S(2)}) async-start(bf16[8,8,4224]{2,1,0:T(8,128)(2,1)} %fusion.1), calls=%async_computation.18 | async-start | bytes 1081344 | tf_op jit(solution)/shard_map/all_to_all | solution.py:451
  344.4 3.0 collective-permute-start.19
  351.0 8.1 %collective-permute-done.19 = bf16[128,1024]{1,0:T(8,128)(2,1)S(1)} collective-permute-done((bf16[128,1024]{1,0:T(8,128)(2,1)S(1)}, bf16[128,1024]{1,0:T(8,128)(2,1)S(1)}, u32[]{:S(2)}, u32[]{:S(2)}) %collective-permute-start.19) | collective-permute-done | bytes 262176 | tf_op jit(solution)/shard_map/ppermute | solution.py:409
  369.7 4.0 all-to-all-start.19
  373.7 6.2 %shard_map.244 = (f32[2,512,1024]{2,1,0:T(8,128)}, f32[2,1024,512]{2,1,0:T(8,128)}) custom-call(s32[1]{0:T(128)} %bitcast.39.side_ref, bf16[256,1024]{1,0:T(8,128)(2,1)} %pad_maximum_fusion.2.p_own, bf16[256,1024]{1,0:T(8,128)(2,1)} %collective-permute-done.12.p_got, bf16[256,1024]{1,0:T(8,128)(2,1)} %copy-done.10, ...), custom_call_target="tpu_custom_call" | custom-call | flops 1000 | bytes 1000 | tf_op jit(solution)/shard_map/pallas_call | solution.py:65
  379.9 4.6 %all-to-all-done.19.late_own = bf16[8,8,4224]{2,1,0:T(8,128)(2,1)S(1)} async-done(((bf16[8,8,4224]{2,1,0:T(8,128)(2,1)}), bf16[8,8,4224]{2,1,0:T(8,128)(2,1)S(1)}, u32[]{:S(2)}, u32[]{:S(2)}) %all-to-all-start.19) | async-done | bytes 540704 | tf_op jit(solution)/shard_map/all_to_all | solution.py:451
  390.7 3.7 shard_map.245
  (256 shorter events, 119.4 us)
Async XLA Ops:
  12.1 34.8 %copy-start.13 = (bf16[128,1024]{1,0:T(8,128)(2,1)S(1)}, bf16[128,1024]{1,0:T(8,128)(2,1)}, u32[]{:S(2)}) copy-start(bf16[128,1024]{1,0:T(8,128)(2,1)} %x_ref.1) | copy-start | bytes 786436
  12.1 35.4 %copy-start.18 = (bf16[2,1024]{1,0:T(2,128)(2,1)S(1)}, bf16[2,1024]{1,0:T(2,128)(2,1)}, u32[]{:S(2)}) copy-start(bf16[2,1024]{1,0:T(2,128)(2,1)} %param.20) | copy-start | bytes 12292
  12.1 26.5 %all-to-all-start = ((bf16[16,128,256]{2,1,0:T(8,128)(2,1)}), bf16[16,128,256]{2,1,0:T(8,128)(2,1)S(1)}, u32[]{:S(2)}, u32[]{:S(2)}) async-start(bf16[16,128,256]{2,1,0:T(8,128)(2,1)} %get-tuple-element.111), calls=%async_computation | async-start | bytes 2097152 | tf_op jit(solution)/shard_map/all_to_all | solution.py:394
  21.4 37.2 %copy-start.31 = (bf16[2,512]{1,0:T(2,128)(2,1)S(1)}, bf16[2,512]{1,0:T(2,128)(2,1)}, u32[]{:S(2)}) copy-start(bf16[2,512]{1,0:T(2,128)(2,1)} %param.22) | copy-start | bytes 6148
  42.2 11.1 %all-to-all-start.1 = ((bf16[8,16,1024]{2,1,0:T(8,128)(2,1)}), bf16[8,16,1024]{2,1,0:T(8,128)(2,1)S(1)}, u32[]{:S(2)}, u32[]{:S(2)}) async-start(bf16[8,16,1024]{2,1,0:T(8,128)(2,1)} %get-tuple-element.112), calls=%async_computation.1 | async-start | bytes 524288 | tf_op jit(solution)/shard_map/all_to_all | solution.py:394
  55.1 9.5 %all-to-all-start.2 = ((bf16[8,16,1024]{2,1,0:T(8,128)(2,1)}), bf16[8,16,1024]{2,1,0:T(8,128)(2,1)S(1)}, u32[]{:S(2)}, u32[]{:S(2)}) async-start(bf16[8,16,1024]{2,1,0:T(8,128)(2,1)} %get-tuple-element.113), calls=%async_computation.2 | async-start | bytes 524288 | tf_op jit(solution)/shard_map/all_to_all | solution.py:394
  67.5 9.5 %all-to-all-start.3 = ((bf16[8,16,1024]{2,1,0:T(8,128)(2,1)}), bf16[8,16,1024]{2,1,0:T(8,128)(2,1)S(1)}, u32[]{:S(2)}, u32[]{:S(2)}) async-start(bf16[8,16,1024]{2,1,0:T(8,128)(2,1)} %get-tuple-element.114), calls=%async_computation.3 | async-start | bytes 524288 | tf_op jit(solution)/shard_map/all_to_all | solution.py:394
  90.9 27.1 %all-to-all-start.5 = ((bf16[16,128,256]{2,1,0:T(8,128)(2,1)}), bf16[16,128,256]{2,1,0:T(8,128)(2,1)S(1)}, u32[]{:S(2)}, u32[]{:S(2)}) async-start(bf16[16,128,256]{2,1,0:T(8,128)(2,1)} %get-tuple-element.118), calls=%async_computation.5 | async-start | bytes 2097152 | tf_op jit(solution)/shard_map/all_to_all | solution.py:394
  100.8 72.6 %all-gather.2.cloned.1.call-start = ((), (), s32[]{:S(2)}) async-start(), calls=%async_computation.20 | async-start | bytes 1114112 | tf_op jit(solution)/shard_map/all_gather | solution.py:561
  146.3 11.8 %all-to-all-start.8 = ((bf16[8,32,1024]{2,1,0:T(8,128)(2,1)}), bf16[8,32,1024]{2,1,0:T(8,128)(2,1)}, u32[]{:S(2)}, u32[]{:S(2)}) async-start(bf16[8,32,1024]{2,1,0:T(8,128)(2,1)} %get-tuple-element.122), calls=%async_computation.8 | async-start | bytes 1048576 | tf_op jit(solution)/shard_map/all_to_all | solution.py:394
  160.1 11.0 %all-to-all-start.9 = ((bf16[8,32,1024]{2,1,0:T(8,128)(2,1)}), bf16[8,32,1024]{2,1,0:T(8,128)(2,1)S(1)}, u32[]{:S(2)}, u32[]{:S(2)}) async-start(bf16[8,32,1024]{2,1,0:T(8,128)(2,1)} %get-tuple-element.126), calls=%async_computation.9 | async-start | bytes 1048576 | tf_op jit(solution)/shard_map/all_to_all | solution.py:394
  166.0 23.6 %collective-permute-start.21 = (bf16[512,1024]{1,0:T(8,128)(2,1)}, bf16[512,1024]{1,0:T(8,128)(2,1)}, u32[]{:S(2)}, u32[]{:S(2)}) collective-permute-start(bf16[512,1024]{1,0:T(8,128)(2,1)} %dynamic-slice_bitcast_fusion), channel_id=1, source_target_pairs={{0,1},{1,0},{2,3},{3,2},{4,5},{5,4},{6,7},{7,6},{8,9},{9,8},{10,11... | collective-permute-start | bytes 3145736 | tf_op jit(solution)/shard_map/ppermute | solution.py:409
  173.3 22.6 %all-to-all-start.10 = ((bf16[16,144,128]{2,1,0:T(8,128)(2,1)}), bf16[16,144,128]{2,1,0:T(8,128)(2,1)}, u32[]{:S(2)}, u32[]{:S(2)}) async-start(bf16[16,144,128]{2,1,0:T(8,128)(2,1)} %get-tuple-element.133), calls=%async_computation.10 | async-start | bytes 1179648 | tf_op jit(solution)/shard_map/all_to_all | solution.py:394
  198.8 48.9 %collective-permute-start.22 = (bf16[256,1024]{1,0:T(8,128)(2,1)}, bf16[256,1024]{1,0:T(8,128)(2,1)}, u32[]{:S(2)}, u32[]{:S(2)}) collective-permute-start(bf16[256,1024]{1,0:T(8,128)(2,1)} %dynamic-slice_bitcast_fusion.1), channel_id=1, source_target_pairs={{0,2},{1,3},{2,0},{3,1},{4,6},{5,7},{6,4},{7,5},{8,10},{9,11},{10,... | collective-permute-start | bytes 1572872 | tf_op jit(solution)/shard_map/ppermute | solution.py:409
  204.2 10.9 %all-to-all-start.11 = ((bf16[8,16,1024]{2,1,0:T(8,128)(2,1)}), bf16[8,16,1024]{2,1,0:T(8,128)(2,1)S(1)}, u32[]{:S(2)}, u32[]{:S(2)}) async-start(bf16[8,16,1024]{2,1,0:T(8,128)(2,1)} %get-tuple-element.136), calls=%async_computation.11 | async-start | bytes 524288 | tf_op jit(solution)/shard_map/all_to_all | solution.py:394
  211.8 30.7 %collective-permute-start.1 = (bf16[256,1024]{1,0:T(8,128)(2,1)}, bf16[256,1024]{1,0:T(8,128)(2,1)}, u32[]{:S(2)}, u32[]{:S(2)}) collective-permute-start(bf16[256,1024]{1,0:T(8,128)(2,1)} %dynamic-slice_bitcast_fusion.4), channel_id=1, source_target_pairs={{0,1},{1,0},{2,3},{3,2},{4,5},{5,4},{6,7},{7,6},{8,9},{9,8},{10,11... | collective-permute-start | bytes 1572872 | tf_op jit(solution)/shard_map/ppermute | solution.py:409
  216.9 11.2 %all-to-all-start.12 = ((bf16[8,16,1024]{2,1,0:T(8,128)(2,1)}), bf16[8,16,1024]{2,1,0:T(8,128)(2,1)S(1)}, u32[]{:S(2)}, u32[]{:S(2)}) async-start(bf16[8,16,1024]{2,1,0:T(8,128)(2,1)} %get-tuple-element.140), calls=%async_computation.12 | async-start | bytes 524288 | tf_op jit(solution)/shard_map/all_to_all | solution.py:394
  231.3 18.5 %all-to-all-start.13 = ((bf16[8,16,1024]{2,1,0:T(8,128)(2,1)}), bf16[8,16,1024]{2,1,0:T(8,128)(2,1)S(1)}, u32[]{:S(2)}, u32[]{:S(2)}) async-start(bf16[8,16,1024]{2,1,0:T(8,128)(2,1)} %get-tuple-element.142), calls=%async_computation.13 | async-start | bytes 524288 | tf_op jit(solution)/shard_map/all_to_all | solution.py:394
  241.7 31.6 %collective-permute-start.13 = (bf16[256,1024]{1,0:T(8,128)(2,1)}, bf16[256,1024]{1,0:T(8,128)(2,1)}, u32[]{:S(2)}, u32[]{:S(2)}) collective-permute-start(bf16[256,1024]{1,0:T(8,128)(2,1)} %dynamic-slice_bitcast_fusion.2), channel_id=1, source_target_pairs={{0,1},{1,0},{2,3},{3,2},{4,5},{5,4},{6,7},{7,6},{8,9},{9,8},{10,11... | collective-permute-start | bytes 1572872 | tf_op jit(solution)/shard_map/ppermute | solution.py:409
  243.8 13.7 %collective-permute-start.2 = (bf16[128,1024]{1,0:T(8,128)(2,1)S(1)}, bf16[128,1024]{1,0:T(8,128)(2,1)}, u32[]{:S(2)}, u32[]{:S(2)}) collective-permute-start(bf16[128,1024]{1,0:T(8,128)(2,1)S(1)} %dynamic-slice_bitcast_fusion.7), channel_id=1, source_target_pairs={{0,2},{1,3},{2,0},{3,1},{4,6},{5,7},{6,4},{7,5},{8,10},{9,11},{10,... | collective-permute-start | bytes 786440 | tf_op jit(solution)/shard_map/ppermute | solution.py:409
  247.4 30.2 %collective-permute-start.5 = (bf16[256,1024]{1,0:T(8,128)(2,1)}, bf16[256,1024]{1,0:T(8,128)(2,1)}, u32[]{:S(2)}, u32[]{:S(2)}) collective-permute-start(bf16[256,1024]{1,0:T(8,128)(2,1)} %dynamic-slice_bitcast_fusion.3), channel_id=1, source_target_pairs={{0,1},{1,0},{2,3},{3,2},{4,5},{5,4},{6,7},{7,6},{8,9},{9,8},{10,11... | collective-permute-start | bytes 1572872 | tf_op jit(solution)/shard_map/ppermute | solution.py:409
  251.5 12.2 %all-to-all-start.14 = ((bf16[8,16,1024]{2,1,0:T(8,128)(2,1)}), bf16[8,16,1024]{2,1,0:T(8,128)(2,1)S(1)}, u32[]{:S(2)}, u32[]{:S(2)}) async-start(bf16[8,16,1024]{2,1,0:T(8,128)(2,1)} %get-tuple-element.146), calls=%async_computation.14 | async-start | bytes 524288 | tf_op jit(solution)/shard_map/all_to_all | solution.py:394
  256.2 55.8 %all-reduce.4.cloned.1.call-start = ((), (), s32[]{:S(2)}) async-start(), calls=%async_computation.21 | async-start | bytes 1572864 | tf_op jit(solution)/shard_map/psum | solution.py:446
  265.8 29.7 %all-to-all-start.15 = ((bf16[16,144,128]{2,1,0:T(8,128)(2,1)}), bf16[16,144,128]{2,1,0:T(8,128)(2,1)S(1)}, u32[]{:S(2)}, u32[]{:S(2)}) async-start(bf16[16,144,128]{2,1,0:T(8,128)(2,1)} %get-tuple-element.149), calls=%async_computation.15 | async-start | bytes 1179648 | tf_op jit(solution)/shard_map/all_to_all | solution.py:394
  274.6 14.0 %collective-permute-start.14 = (bf16[128,1024]{1,0:T(8,128)(2,1)S(1)}, bf16[128,1024]{1,0:T(8,128)(2,1)S(1)}, u32[]{:S(2)}, u32[]{:S(2)}) collective-permute-start(bf16[128,1024]{1,0:T(8,128)(2,1)S(1)} %dynamic-slice_bitcast_fusion.5), channel_id=1, source_target_pairs={{0,2},{1,3},{2,0},{3,1},{4,6},{5,7},{6,4},{7,5},{8,10},{9,11},{10,... | collective-permute-start | bytes 786440 | tf_op jit(solution)/shard_map/ppermute | solution.py:409
  278.9 15.3 %collective-permute-start.6 = (bf16[128,1024]{1,0:T(8,128)(2,1)S(1)}, bf16[128,1024]{1,0:T(8,128)(2,1)S(1)}, u32[]{:S(2)}, u32[]{:S(2)}) collective-permute-start(bf16[128,1024]{1,0:T(8,128)(2,1)S(1)} %dynamic-slice_bitcast_fusion.6), channel_id=1, source_target_pairs={{0,2},{1,3},{2,0},{3,1},{4,6},{5,7},{6,4},{7,5},{8,10},{9,11},{10,... | collective-permute-start | bytes 786440 | tf_op jit(solution)/shard_map/ppermute | solution.py:409
  288.7 14.4 %collective-permute-start.15 = (bf16[64,1024]{1,0:T(8,128)(2,1)S(1)}, bf16[64,1024]{1,0:T(8,128)(2,1)S(1)}, u32[]{:S(2)}, u32[]{:S(2)}) collective-permute-start(bf16[64,1024]{1,0:T(8,128)(2,1)S(1)} %dynamic-slice_bitcast_fusion.8), channel_id=1, source_target_pairs={{0,4},{1,5},{2,6},{3,7},{4,0},{5,1},{6,2},{7,3},{8,12},{9,13},{10,... | collective-permute-start | bytes 393224 | tf_op jit(solution)/shard_map/ppermute | solution.py:409
  294.3 13.7 %collective-permute-start.7 = (bf16[64,1024]{1,0:T(8,128)(2,1)S(1)}, bf16[64,1024]{1,0:T(8,128)(2,1)S(1)}, u32[]{:S(2)}, u32[]{:S(2)}) collective-permute-start(bf16[64,1024]{1,0:T(8,128)(2,1)S(1)} %dynamic-slice_bitcast_fusion.9), channel_id=1, source_target_pairs={{0,12},{1,13},{2,14},{3,15},{4,8},{5,9},{6,10},{7,11},{8,4},{9,5},... | collective-permute-start | bytes 393224 | tf_op jit(solution)/shard_map/ppermute | solution.py:409
  299.5 10.1 %all-to-all-start.16 = ((bf16[8,16,1024]{2,1,0:T(8,128)(2,1)}), bf16[8,16,1024]{2,1,0:T(8,128)(2,1)S(1)}, u32[]{:S(2)}, u32[]{:S(2)}) async-start(bf16[8,16,1024]{2,1,0:T(8,128)(2,1)} %get-tuple-element.152), calls=%async_computation.16 | async-start | bytes 524288 | tf_op jit(solution)/shard_map/all_to_all | solution.py:394
  303.1 17.2 %collective-permute-start.16 = (bf16[32,1024]{1,0:T(8,128)(2,1)S(1)}, bf16[32,1024]{1,0:T(8,128)(2,1)S(1)}, u32[]{:S(2)}, u32[]{:S(2)}) collective-permute-start(bf16[32,1024]{1,0:T(8,128)(2,1)S(1)} %dynamic-slice_bitcast_fusion.10), channel_id=1, source_target_pairs={{0,12},{1,13},{2,14},{3,15},{4,8},{5,9},{6,10},{7,11},{8,4},{9,5},... | collective-permute-start | bytes 196616 | tf_op jit(solution)/shard_map/ppermute | solution.py:409
  308.8 13.0 %collective-permute-start.8 = (bf16[32,1024]{1,0:T(8,128)(2,1)S(1)}, bf16[32,1024]{1,0:T(8,128)(2,1)S(1)}, u32[]{:S(2)}, u32[]{:S(2)}) collective-permute-start(bf16[32,1024]{1,0:T(8,128)(2,1)S(1)} %dynamic-slice_bitcast_fusion.11), channel_id=1, source_target_pairs={{0,4},{1,5},{2,6},{3,7},{4,0},{5,1},{6,2},{7,3},{8,12},{9,13},{10,... | collective-permute-start | bytes 196616 | tf_op jit(solution)/shard_map/ppermute | solution.py:409
  312.1 32.3 %collective-permute-start.23 = (bf16[256,1024]{1,0:T(8,128)(2,1)}, bf16[256,1024]{1,0:T(8,128)(2,1)}, u32[]{:S(2)}, u32[]{:S(2)}) collective-permute-start(bf16[256,1024]{1,0:T(8,128)(2,1)} %get-tuple-element.198), channel_id=1, source_target_pairs={{0,2},{1,3},{2,0},{3,1},{4,6},{5,7},{6,4},{7,5},{8,10},{9,11},{10,... | collective-permute-start | bytes 1572872 | tf_op jit(solution)/shard_map/ppermute | solution.py:409
  315.9 11.9 %all-to-all-start.17 = ((bf16[8,24,1024]{2,1,0:T(8,128)(2,1)}), bf16[8,24,1024]{2,1,0:T(8,128)(2,1)S(1)}, u32[]{:S(2)}, u32[]{:S(2)}) async-start(bf16[8,24,1024]{2,1,0:T(8,128)(2,1)} %pad_maximum_fusion.4), calls=%async_computation.17 | async-start | bytes 786432 | tf_op jit(solution)/shard_map/all_to_all | solution.py:394
  320.4 4.9 %collective-permute-start.17 = (bf16[32,1024]{1,0:T(8,128)(2,1)S(1)}, bf16[32,1024]{1,0:T(8,128)(2,1)S(1)}, u32[]{:S(2)}, u32[]{:S(2)}) collective-permute-start(bf16[32,1024]{1,0:T(8,128)(2,1)S(1)} %fusion.15), channel_id=1, source_target_pairs={{0,12},{1,13},{2,14},{3,15},{4,8},{5,9},{6,10},{7,11},{8,4},{9,5},... | collective-permute-start | bytes 196616 | tf_op jit(solution)/shard_map/ppermute | solution.py:409
  321.8 4.3 %collective-permute-start.9 = (bf16[32,1024]{1,0:T(8,128)(2,1)S(1)}, bf16[32,1024]{1,0:T(8,128)(2,1)S(1)}, u32[]{:S(2)}, u32[]{:S(2)}) collective-permute-start(bf16[32,1024]{1,0:T(8,128)(2,1)S(1)} %fusion.16), channel_id=1, source_target_pairs={{0,4},{1,5},{2,6},{3,7},{4,0},{5,1},{6,2},{7,3},{8,12},{9,13},{10,... | collective-permute-start | bytes 196616 | tf_op jit(solution)/shard_map/ppermute | solution.py:409
  322.7 27.3 %collective-permute-start.3 = (bf16[128,1024]{1,0:T(8,128)(2,1)S(1)}, bf16[128,1024]{1,0:T(8,128)(2,1)}, u32[]{:S(2)}, u32[]{:S(2)}) collective-permute-start(bf16[128,1024]{1,0:T(8,128)(2,1)S(1)} %copy-done.17), channel_id=1, source_target_pairs={{0,2},{1,3},{2,0},{3,1},{4,6},{5,7},{6,4},{7,5},{8,10},{9,11},{10,... | collective-permute-start | bytes 786440 | tf_op jit(solution)/shard_map/ppermute | solution.py:409
  325.4 10.0 %collective-permute-start.18 = (bf16[64,1024]{1,0:T(8,128)(2,1)S(1)}, bf16[64,1024]{1,0:T(8,128)(2,1)S(1)}, u32[]{:S(2)}, u32[]{:S(2)}) collective-permute-start(bf16[64,1024]{1,0:T(8,128)(2,1)S(1)} %pad_maximum_fusion.8), channel_id=1, source_target_pairs={{0,4},{1,5},{2,6},{3,7},{4,0},{5,1},{6,2},{7,3},{8,12},{9,13},{10,... | collective-permute-start | bytes 393224 | tf_op jit(solution)/shard_map/ppermute | solution.py:409
  326.2 9.2 %collective-permute-start.10 = (bf16[64,1024]{1,0:T(8,128)(2,1)S(1)}, bf16[64,1024]{1,0:T(8,128)(2,1)S(1)}, u32[]{:S(2)}, u32[]{:S(2)}) collective-permute-start(bf16[64,1024]{1,0:T(8,128)(2,1)S(1)} %pad_maximum_fusion.7), channel_id=1, source_target_pairs={{0,12},{1,13},{2,14},{3,15},{4,8},{5,9},{6,10},{7,11},{8,4},{9,5},... | collective-permute-start | bytes 393224 | tf_op jit(solution)/shard_map/ppermute | solution.py:409
  329.7 7.2 %collective-permute-start = (bf16[8,8,4224]{2,1,0:T(8,128)(2,1)S(1)}, bf16[8,8,4224]{2,1,0:T(8,128)(2,1)S(1)}, u32[]{:S(2)}, u32[]{:S(2)}) collective-permute-start(bf16[8,8,4224]{2,1,0:T(8,128)(2,1)S(1)} %fusion.7), channel_id=1, source_target_pairs={{0,1},{1,0},{2,3},{3,2},{4,5},{5,4},{6,7},{7,6},{8,9},{9,8},{10,11... | collective-permute-start | bytes 1622024 | tf_op jit(solution)/shard_map/ppermute | solution.py:409
  337.8 29.4 %all-to-all-start.18 = ((bf16[8,8,4224]{2,1,0:T(8,128)(2,1)}), bf16[8,8,4224]{2,1,0:T(8,128)(2,1)S(1)}, u32[]{:S(2)}, u32[]{:S(2)}) async-start(bf16[8,8,4224]{2,1,0:T(8,128)(2,1)} %fusion.1), calls=%async_computation.18 | async-start | bytes 1081344 | tf_op jit(solution)/shard_map/all_to_all | solution.py:451
  344.4 14.7 %collective-permute-start.19 = (bf16[128,1024]{1,0:T(8,128)(2,1)S(1)}, bf16[128,1024]{1,0:T(8,128)(2,1)S(1)}, u32[]{:S(2)}, u32[]{:S(2)}) collective-permute-start(bf16[128,1024]{1,0:T(8,128)(2,1)S(1)} %pad_maximum_fusion.6), channel_id=1, source_target_pairs={{0,2},{1,3},{2,0},{3,1},{4,6},{5,7},{6,4},{7,5},{8,10},{9,11},{10,... | collective-permute-start | bytes 786440 | tf_op jit(solution)/shard_map/ppermute | solution.py:409
  348.7 25.0 %collective-permute-start.24 = (bf16[512,1024]{1,0:T(8,128)(2,1)S(1)}, bf16[512,1024]{1,0:T(8,128)(2,1)}, u32[]{:S(2)}, u32[]{:S(2)}) collective-permute-start(bf16[512,1024]{1,0:T(8,128)(2,1)S(1)} %pad_maximum_fusion.own_ref), channel_id=1, source_target_pairs={{0,1},{1,0},{2,3},{3,2},{4,5},{5,4},{6,7},{7,6},{8,9},{9,8},{10,11... | collective-permute-start | bytes 3145736 | tf_op jit(solution)/shard_map/ppermute | solution.py:409
  350.0 14.7 %collective-permute-start.11 = (bf16[128,1024]{1,0:T(8,128)(2,1)S(1)}, bf16[128,1024]{1,0:T(8,128)(2,1)S(1)}, u32[]{:S(2)}, u32[]{:S(2)}) collective-permute-start(bf16[128,1024]{1,0:T(8,128)(2,1)S(1)} %pad_maximum_fusion.5), channel_id=1, source_target_pairs={{0,2},{1,3},{2,0},{3,1},{4,6},{5,7},{6,4},{7,5},{8,10},{9,11},{10,... | collective-permute-start | bytes 786440 | tf_op jit(solution)/shard_map/ppermute | solution.py:409
  359.2 14.5 %collective-permute-start.20 = (bf16[256,1024]{1,0:T(8,128)(2,1)S(1)}, bf16[256,1024]{1,0:T(8,128)(2,1)}, u32[]{:S(2)}, u32[]{:S(2)}) collective-permute-start(bf16[256,1024]{1,0:T(8,128)(2,1)S(1)} %pad_maximum_fusion.3.f_own), channel_id=1, source_target_pairs={{0,1},{1,0},{2,3},{3,2},{4,5},{5,4},{6,7},{7,6},{8,9},{9,8},{10,11... | collective-permute-start | bytes 1572872 | tf_op jit(solution)/shard_map/ppermute | solution.py:409
  365.6 8.1 %collective-permute-start.12 = (bf16[256,1024]{1,0:T(8,128)(2,1)}, bf16[256,1024]{1,0:T(8,128)(2,1)}, u32[]{:S(2)}, u32[]{:S(2)}) collective-permute-start(bf16[256,1024]{1,0:T(8,128)(2,1)} %pad_maximum_fusion.2.p_own), channel_id=1, source_target_pairs={{0,1},{1,0},{2,3},{3,2},{4,5},{5,4},{6,7},{7,6},{8,9},{9,8},{10,11... | collective-permute-start | bytes 1572872 | tf_op jit(solution)/shard_map/ppermute | solution.py:409
  367.2 12.7 %collective-permute-start.4 = (bf16[256,1024]{1,0:T(8,128)(2,1)S(1)}, bf16[256,1024]{1,0:T(8,128)(2,1)}, u32[]{:S(2)}, u32[]{:S(2)}) collective-permute-start(bf16[256,1024]{1,0:T(8,128)(2,1)S(1)} %pad_maximum_fusion.1.own_ref), channel_id=1, source_target_pairs={{0,1},{1,0},{2,3},{3,2},{4,5},{5,4},{6,7},{7,6},{8,9},{9,8},{10,11... | collective-permute-start | bytes 1572872 | tf_op jit(solution)/shard_map/ppermute | solution.py:409
  369.7 14.8 %all-to-all-start.19 = ((bf16[8,8,4224]{2,1,0:T(8,128)(2,1)}), bf16[8,8,4224]{2,1,0:T(8,128)(2,1)S(1)}, u32[]{:S(2)}, u32[]{:S(2)}) async-start(bf16[8,8,4224]{2,1,0:T(8,128)(2,1)} %broadcast_in_dim.15), calls=%async_computation.19 | async-start | bytes 1081344 | tf_op jit(solution)/shard_map/all_to_all | solution.py:451
  384.5 3.0 collective-permute-start.25
  (33 other events, 418.4 us)
Sparse Core Ops, SparseCore 0:
  104.0 44.8 all-gather.1
  260.6 45.6 all-reduce.3

commit v3 on v2

--- a/solution.py
+++ b/solution.py
@@ -437,7 +437,7 @@
         value = halve(value, flip, event, side)
     for flip, side in steps[::-1]:
         value = rejoin(value, flip, side)
-    value = rejoin(after(value, events[-1]), DEPTH)
+    value = rejoin(value, DEPTH, None, events[-1])
     return value, swap(value, CORE)
 
 
@@ -724,8 +724,8 @@
     arrived = swap_chips(half)
     mine = jnp.sum(arrived.astype(F32), 0).astype(BF16)
     late = swap_chips(jnp.broadcast_to(mine, (ranks // 2,) + mine.shape))
-    starts = [halve(halve(part, CORE, grad_b), DEPTH, g_o) for part in (end_pack[:hidden], end_pack[hidden:])]
-    events = (g_kv, grad, half)
+    starts = [halve(halve(part, CORE, grad_b), DEPTH, g_kv) for part in (end_pack[:hidden], end_pack[hidden:])]
+    events = (grad, half, mine)
     end_parts = [part for turn, value in enumerate(starts) for part in finish_sums(value, turn, events)]
     end_last, attend_last = [rejoin(after(part, grad), DEPTH, None, half) for part in done[1]]
     side = side_of(CORE)
@@ -741,7 +741,7 @@
         room=40,
     )
     attend_got = swap(attend_last, CORE)
-    late, attend_got, g_w_proj, g_w_fc = lax.optimization_barrier((late, attend_got, g_w_proj, g_w_fc))
+    late, attend_got = lax.optimization_barrier((late, attend_got))
     late_got = swap(late, CORE)
     g_w_out, g_w_qkv = call(
         finish_attend_kernel,

time: 405 us -> 405 us (level)
  waiting for transfers between devices: 101 us -> 87.8 us
  starting transfers between devices: 128 us -> 135 us
  local copies, waits for them, and re-layouts: 20.1 us -> 24.2 us
    ppermute x26, waiting for transfers between devices: 27.3 us -> 6.15 us  [swap(): lax.ppermute(value, 'dp', [(i, i ^ flip) for i in range(lax.axis_size('dp...]
    all_to_all x15, waiting for transfers between devices: 68.7 us -> 81.3 us  [swap_all(): return lax.all_to_all(value, axis, 0, 0)]
    ppermute x26, starting transfers between devices: 40.6 us -> 46.9 us  [swap(): lax.ppermute(value, 'dp', [(i, i ^ flip) for i in range(lax.axis_size('dp...]
    all_to_all x2, waiting for transfers between devices: 4.57 us -> 0.35 us  [swap_chips(): return lax.all_to_all(value, 'dp', 0, 0, axis_index_groups=groups)]
  transfers between devices with their start and end apart: 45 -> 45, of which waited for: 17 -> 19; matrix products, arithmetic and copies ran while one was open for 12% -> 13% of each run, Pallas kernels for 14% -> 14%
where the time goes in v3:
time: 405 us; the launch traced here: 401 us
  starting transfers between devices  135 us (33%)
  waiting for transfers between devices  87.8 us (22%)
  Pallas kernels  74.1 us (18%)
  other arithmetic  36.7 us (9%)
  blocking collectives  28.5 us (7%)
  local copies, waits for them, and re-layouts  24.2 us (6%)
  between operations  14.9 us (4%)
    all_to_all x15, waiting for transfers between devices, swap_all(): return lax.all_to_all(value, axis, 0, 0)  81.3 us
    all_to_all x15, starting transfers between devices, swap_all(): return lax.all_to_all(value, axis, 0, 0)  76.6 us
    pallas_call x26, Pallas kernels, call(): pl.pallas_call(kernel, grid=(1,), in_specs=[spec(index, arg) for index, a...  74.1 us
    ppermute x26, starting transfers between devices, swap(): lax.ppermute(value, 'dp', [(i, i ^ flip) for i in range(lax.axis_size('dp...  46.9 us
    all_to_all x3, blocking collectives, swap_all(): return lax.all_to_all(value, axis, 0, 0)  28.5 us
    convert_element_type x13, other arithmetic, halve(): return (mine.astype(F32) + got.astype(F32)).astype(BF16)  12.5 us
    all_to_all x2, starting transfers between devices, swap_chips(): return lax.all_to_all(value, 'dp', 0, 0, axis_index_groups=groups)  11.5 us
    squeeze x12, local copies, waits for them, and re-layouts, halve(): lax.dynamic_index_in_dim(halves, 1 - side, 0, keepdims=False)  8.14 us
  transfers between devices with their start and end apart: 45, of which 19 were waited for; matrix products, arithmetic and copies ran while one was open for 13% of the time, Pallas kernels for 14%

profile of v3, /device:TPU:1, one launch (start us, length us, event | category | flops | bytes accessed | tf_op | source)
XLA Modules:
  0.0 401.3 jit_solution(4065305277620717972)
XLA Ops:
  12.1 9.3 %all-to-all-start = ((bf16[16,128,256]{2,1,0:T(8,128)(2,1)}), bf16[16,128,256]{2,1,0:T(8,128)(2,1)S(1)}, u32[]{:S(2)}, u32[]{:S(2)}) async-start(bf16[16,128,256]{2,1,0:T(8,128)(2,1)} %get-tuple-element.109), calls=%async_computation | async-start | bytes 2097152 | tf_op jit(solution)/shard_map/all_to_all | solution.py:394
  22.9 15.7 %all-to-all-done.kv_ref = bf16[16,128,256]{2,1,0:T(8,128)(2,1)S(1)} async-done(((bf16[16,128,256]{2,1,0:T(8,128)(2,1)}), bf16[16,128,256]{2,1,0:T(8,128)(2,1)S(1)}, u32[]{:S(2)}, u32[]{:S(2)}) %all-to-all-start) | async-done | bytes 1048608 | tf_op jit(solution)/shard_map/all_to_all | solution.py:394
  38.6 3.6 shard_map.221
  42.2 4.6 %all-to-all-start.1 = ((bf16[8,16,1024]{2,1,0:T(8,128)(2,1)}), bf16[8,16,1024]{2,1,0:T(8,128)(2,1)S(1)}, u32[]{:S(2)}, u32[]{:S(2)}) async-start(bf16[8,16,1024]{2,1,0:T(8,128)(2,1)} %get-tuple-element.110), calls=%async_computation.1 | async-start | bytes 524288 | tf_op jit(solution)/shard_map/all_to_all | solution.py:394
  48.1 5.2 %all-to-all-done.1.parts_ref = bf16[8,16,1024]{2,1,0:T(8,128)(2,1)S(1)} async-done(((bf16[8,16,1024]{2,1,0:T(8,128)(2,1)}), bf16[8,16,1024]{2,1,0:T(8,128)(2,1)S(1)}, u32[]{:S(2)}, u32[]{:S(2)}) %all-to-all-start.1) | async-done | bytes 262176 | tf_op jit(solution)/shard_map/all_to_all | solution.py:394
  55.1 3.4 all-to-all-start.2
  59.2 5.5 %all-to-all-done.2 = bf16[8,16,1024]{2,1,0:T(8,128)(2,1)S(1)} async-done(((bf16[8,16,1024]{2,1,0:T(8,128)(2,1)}), bf16[8,16,1024]{2,1,0:T(8,128)(2,1)S(1)}, u32[]{:S(2)}, u32[]{:S(2)}) %all-to-all-start.2) | async-done | bytes 262176 | tf_op jit(solution)/shard_map/all_to_all | solution.py:394
  67.5 3.4 all-to-all-start.3
  71.5 5.5 %all-to-all-done.3.parts_ref = bf16[8,16,1024]{2,1,0:T(8,128)(2,1)S(1)} async-done(((bf16[8,16,1024]{2,1,0:T(8,128)(2,1)}), bf16[8,16,1024]{2,1,0:T(8,128)(2,1)S(1)}, u32[]{:S(2)}, u32[]{:S(2)}) %all-to-all-start.3) | async-done | bytes 262176 | tf_op jit(solution)/shard_map/all_to_all | solution.py:394
  78.8 9.5 %all_to_all.100 = bf16[8,16,1024]{2,1,0:T(8,128)(2,1)S(1)} all-to-all(bf16[8,16,1024]{2,1,0:T(8,128)(2,1)} %get-tuple-element.114), channel_id=1, replica_groups=mesh['tensor'=8,'dp'=16] {'tensor'}, dimensions={0} | all-to-all | bytes 524288 | tf_op jit(solution)/shard_map/all_to_all | solution.py:394
  90.9 9.9 %all-to-all-start.5 = ((bf16[16,128,256]{2,1,0:T(8,128)(2,1)}), bf16[16,128,256]{2,1,0:T(8,128)(2,1)S(1)}, u32[]{:S(2)}, u32[]{:S(2)}) async-start(bf16[16,128,256]{2,1,0:T(8,128)(2,1)} %get-tuple-element.116), calls=%async_computation.5 | async-start | bytes 2097152 | tf_op jit(solution)/shard_map/all_to_all | solution.py:394
  101.5 16.5 %all-to-all-done.5.kv_ref = bf16[16,128,256]{2,1,0:T(8,128)(2,1)S(1)} async-done(((bf16[16,128,256]{2,1,0:T(8,128)(2,1)}), bf16[16,128,256]{2,1,0:T(8,128)(2,1)S(1)}, u32[]{:S(2)}, u32[]{:S(2)}) %all-to-all-start.5) | async-done | bytes 1048608 | tf_op jit(solution)/shard_map/all_to_all | solution.py:394
  118.0 3.6 shard_map.226
  121.6 9.6 %all_to_all.101.parts_ref = bf16[8,16,1024]{2,1,0:T(8,128)(2,1)S(1)} all-to-all(bf16[8,16,1024]{2,1,0:T(8,128)(2,1)} %get-tuple-element.117), channel_id=1, replica_groups=mesh['tensor'=8,'dp'=16] {'tensor'}, dimensions={0} | all-to-all | bytes 524288 | tf_op jit(solution)/shard_map/all_to_all | solution.py:394
  133.0 9.5 %all_to_all.102 = bf16[8,16,1024]{2,1,0:T(8,128)(2,1)S(1)} all-to-all(bf16[8,16,1024]{2,1,0:T(8,128)(2,1)} %get-tuple-element.119), channel_id=1, replica_groups=mesh['tensor'=8,'dp'=16] {'tensor'}, dimensions={0} | all-to-all | bytes 524288 | tf_op jit(solution)/shard_map/all_to_all | solution.py:394
  142.5 3.8 shard_map.228
  146.3 4.2 %all-to-all-start.8 = ((bf16[8,32,1024]{2,1,0:T(8,128)(2,1)}), bf16[8,32,1024]{2,1,0:T(8,128)(2,1)}, u32[]{:S(2)}, u32[]{:S(2)}) async-start(bf16[8,32,1024]{2,1,0:T(8,128)(2,1)} %get-tuple-element.120), calls=%async_computation.8 | async-start | bytes 1048576 | tf_op jit(solution)/shard_map/all_to_all | solution.py:394
  151.1 3.0 shard_map.243
  154.1 3.9 all-to-all-done.8.parts_ref
  160.1 3.5 all-to-all-start.9
  166.0 4.2 %collective-permute-start.22 = (bf16[512,1024]{1,0:T(8,128)(2,1)}, bf16[512,1024]{1,0:T(8,128)(2,1)}, u32[]{:S(2)}, u32[]{:S(2)}) collective-permute-start(bf16[512,1024]{1,0:T(8,128)(2,1)} %dynamic-slice_bitcast_fusion), channel_id=1, source_target_pairs={{0,1},{1,0},{2,3},{3,2},{4,5},{5,4},{6,7},{7,6},{8,9},{9,8},{10,11... | collective-permute-start | bytes 3145736 | tf_op jit(solution)/shard_map/ppermute | solution.py:409
  173.3 10.8 %all-to-all-start.10 = ((bf16[16,144,128]{2,1,0:T(8,128)(2,1)}), bf16[16,144,128]{2,1,0:T(8,128)(2,1)}, u32[]{:S(2)}, u32[]{:S(2)}) async-start(bf16[16,144,128]{2,1,0:T(8,128)(2,1)} %get-tuple-element.131), calls=%async_computation.10 | async-start | bytes 1179648 | tf_op jit(solution)/shard_map/all_to_all | solution.py:394
  189.1 6.9 %all-to-all-done.10.got_ref = bf16[16,144,128]{2,1,0:T(8,128)(2,1)} async-done(((bf16[16,144,128]{2,1,0:T(8,128)(2,1)}), bf16[16,144,128]{2,1,0:T(8,128)(2,1)}, u32[]{:S(2)}, u32[]{:S(2)}) %all-to-all-start.10) | async-done | bytes 589856 | tf_op jit(solution)/shard_map/all_to_all | solution.py:394
  200.2 4.0 shard_map.232
  204.2 3.4 all-to-all-start.11
  216.9 3.4 all-to-all-start.12
  223.4 3.1 all-to-all-done.12
  226.6 3.2 shard_map.234
  229.8 3.4 all-to-all-start.13
  233.2 3.0 shard_map.241
  250.9 4.7 %all-to-all-start.14 = ((bf16[8,16,1024]{2,1,0:T(8,128)(2,1)}), bf16[8,16,1024]{2,1,0:T(8,128)(2,1)S(1)}, u32[]{:S(2)}, u32[]{:S(2)}) async-start(bf16[8,16,1024]{2,1,0:T(8,128)(2,1)} %get-tuple-element.144), calls=%async_computation.14 | async-start | bytes 524288 | tf_op jit(solution)/shard_map/all_to_all | solution.py:394
  258.2 4.9 %all-to-all-done.14.gy_ref = bf16[8,16,1024]{2,1,0:T(8,128)(2,1)S(1)} async-done(((bf16[8,16,1024]{2,1,0:T(8,128)(2,1)}), bf16[8,16,1024]{2,1,0:T(8,128)(2,1)S(1)}, u32[]{:S(2)}, u32[]{:S(2)}) %all-to-all-start.14) | async-done | bytes 262176 | tf_op jit(solution)/shard_map/all_to_all | solution.py:394
  265.3 4.7 %all-to-all-start.15 = ((bf16[16,144,128]{2,1,0:T(8,128)(2,1)}), bf16[16,144,128]{2,1,0:T(8,128)(2,1)S(1)}, u32[]{:S(2)}, u32[]{:S(2)}) async-start(bf16[16,144,128]{2,1,0:T(8,128)(2,1)} %get-tuple-element.147), calls=%async_computation.15 | async-start | bytes 1179648 | tf_op jit(solution)/shard_map/all_to_all | solution.py:394
  270.0 2.9 shard_map.237.gq_ref
  275.0 2.9 collective-permute-start.15
  279.3 5.4 %all-to-all-done.15.got_ref = bf16[16,144,128]{2,1,0:T(8,128)(2,1)S(1)} async-done(((bf16[16,144,128]{2,1,0:T(8,128)(2,1)}), bf16[16,144,128]{2,1,0:T(8,128)(2,1)S(1)}, u32[]{:S(2)}, u32[]{:S(2)}) %all-to-all-start.15) | async-done | bytes 589856 | tf_op jit(solution)/shard_map/all_to_all | solution.py:394
  284.7 3.9 shard_map.238
  288.6 3.5 all-to-all-start.16
  304.4 4.3 %all-to-all-start.17 = ((bf16[8,24,1024]{2,1,0:T(8,128)(2,1)}), bf16[8,24,1024]{2,1,0:T(8,128)(2,1)S(1)}, u32[]{:S(2)}, u32[]{:S(2)}) async-start(bf16[8,24,1024]{2,1,0:T(8,128)(2,1)} %pad_maximum_fusion.4), calls=%async_computation.17 | async-start | bytes 786432 | tf_op jit(solution)/shard_map/all_to_all | solution.py:394
  311.3 4.8 %all-to-all-done.17 = bf16[8,24,1024]{2,1,0:T(8,128)(2,1)S(1)} async-done(((bf16[8,24,1024]{2,1,0:T(8,128)(2,1)}), bf16[8,24,1024]{2,1,0:T(8,128)(2,1)S(1)}, u32[]{:S(2)}, u32[]{:S(2)}) %all-to-all-start.17) | async-done | bytes 393248 | tf_op jit(solution)/shard_map/all_to_all | solution.py:394
  329.0 4.7 %all-to-all-start.18 = ((bf16[8,8,4224]{2,1,0:T(8,128)(2,1)}), bf16[8,8,4224]{2,1,0:T(8,128)(2,1)S(1)}, u32[]{:S(2)}, u32[]{:S(2)}) async-start(bf16[8,8,4224]{2,1,0:T(8,128)(2,1)} %fusion.1), calls=%async_computation.18 | async-start | bytes 1081344 | tf_op jit(solution)/shard_map/all_to_all | solution.py:451
  336.3 3.0 collective-permute-start.18
  347.7 3.0 collective-permute-start.20
  355.7 6.8 %all-to-all-start.19 = ((bf16[8,8,4224]{2,1,0:T(8,128)(2,1)}), bf16[8,8,4224]{2,1,0:T(8,128)(2,1)S(1)}, u32[]{:S(2)}, u32[]{:S(2)}) async-start(bf16[8,8,4224]{2,1,0:T(8,128)(2,1)} %broadcast_in_dim.15), calls=%async_computation.19 | async-start | bytes 1081344 | tf_op jit(solution)/shard_map/all_to_all | solution.py:451
  363.7 5.2 %collective-permute-start.21 = (bf16[256,1024]{1,0:T(8,128)(2,1)S(1)}, bf16[256,1024]{1,0:T(8,128)(2,1)}, u32[]{:S(2)}, u32[]{:S(2)}) collective-permute-start(bf16[256,1024]{1,0:T(8,128)(2,1)S(1)} %pad_maximum_fusion.3.f_own), channel_id=1, source_target_pairs={{0,1},{1,0},{2,3},{3,2},{4,5},{5,4},{6,7},{7,6},{8,9},{9,8},{10,11... | collective-permute-start | bytes 1572872 | tf_op jit(solution)/shard_map/ppermute | solution.py:409
  371.1 6.3 %collective-permute-start.5 = (bf16[8,8,4224]{2,1,0:T(8,128)(2,1)S(1)}, bf16[8,8,4224]{2,1,0:T(8,128)(2,1)}, u32[]{:S(2)}, u32[]{:S(2)}) collective-permute-start(bf16[8,8,4224]{2,1,0:T(8,128)(2,1)S(1)} %all-to-all-done.19.late_own), channel_id=1, source_target_pairs={{0,1},{1,0},{2,3},{3,2},{4,5},{5,4},{6,7},{7,6},{8,9},{9,8},{10,11... | collective-permute-start | bytes 1622024 | tf_op jit(solution)/shard_map/ppermute | solution.py:409
  380.6 6.2 %shard_map.245 = (f32[2,512,1024]{2,1,0:T(8,128)}, f32[2,1024,512]{2,1,0:T(8,128)}) custom-call(s32[1]{0:T(128)} %bitcast.39.side_ref, bf16[256,1024]{1,0:T(8,128)(2,1)} %copy-done.11, bf16[256,1024]{1,0:T(8,128)(2,1)} %collective-permute-done.13.p_got, bf16[256,1024]{1,0:T(8,128)(2,1)} %copy-done.10, bf16[256,1024]{1,0:T(8,128)(2,1)} %collective-permute-done.21.f_got, ...), custom_call_target="tpu_custom_call" | custom-call | flops 1000 | bytes 1000 | tf_op jit(solution)/shard_map/pallas_call | solution.py:65
  390.8 3.7 shard_map.244
  (250 shorter events, 126.7 us)
Async XLA Ops:
  12.1 34.8 %copy-start.17 = (bf16[128,1024]{1,0:T(8,128)(2,1)S(1)}, bf16[128,1024]{1,0:T(8,128)(2,1)}, u32[]{:S(2)}) copy-start(bf16[128,1024]{1,0:T(8,128)(2,1)} %x_ref.1) | copy-start | bytes 786436
  12.1 35.4 %copy-start.21 = (bf16[2,1024]{1,0:T(2,128)(2,1)S(1)}, bf16[2,1024]{1,0:T(2,128)(2,1)}, u32[]{:S(2)}) copy-start(bf16[2,1024]{1,0:T(2,128)(2,1)} %param.20) | copy-start | bytes 12292
  12.1 26.5 %all-to-all-start = ((bf16[16,128,256]{2,1,0:T(8,128)(2,1)}), bf16[16,128,256]{2,1,0:T(8,128)(2,1)S(1)}, u32[]{:S(2)}, u32[]{:S(2)}) async-start(bf16[16,128,256]{2,1,0:T(8,128)(2,1)} %get-tuple-element.109), calls=%async_computation | async-start | bytes 2097152 | tf_op jit(solution)/shard_map/all_to_all | solution.py:394
  21.4 37.2 %copy-start.29 = (bf16[2,512]{1,0:T(2,128)(2,1)S(1)}, bf16[2,512]{1,0:T(2,128)(2,1)}, u32[]{:S(2)}) copy-start(bf16[2,512]{1,0:T(2,128)(2,1)} %param.22) | copy-start | bytes 6148
  42.2 11.1 %all-to-all-start.1 = ((bf16[8,16,1024]{2,1,0:T(8,128)(2,1)}), bf16[8,16,1024]{2,1,0:T(8,128)(2,1)S(1)}, u32[]{:S(2)}, u32[]{:S(2)}) async-start(bf16[8,16,1024]{2,1,0:T(8,128)(2,1)} %get-tuple-element.110), calls=%async_computation.1 | async-start | bytes 524288 | tf_op jit(solution)/shard_map/all_to_all | solution.py:394
  55.1 9.5 %all-to-all-start.2 = ((bf16[8,16,1024]{2,1,0:T(8,128)(2,1)}), bf16[8,16,1024]{2,1,0:T(8,128)(2,1)S(1)}, u32[]{:S(2)}, u32[]{:S(2)}) async-start(bf16[8,16,1024]{2,1,0:T(8,128)(2,1)} %get-tuple-element.111), calls=%async_computation.2 | async-start | bytes 524288 | tf_op jit(solution)/shard_map/all_to_all | solution.py:394
  67.5 9.5 %all-to-all-start.3 = ((bf16[8,16,1024]{2,1,0:T(8,128)(2,1)}), bf16[8,16,1024]{2,1,0:T(8,128)(2,1)S(1)}, u32[]{:S(2)}, u32[]{:S(2)}) async-start(bf16[8,16,1024]{2,1,0:T(8,128)(2,1)} %get-tuple-element.112), calls=%async_computation.3 | async-start | bytes 524288 | tf_op jit(solution)/shard_map/all_to_all | solution.py:394
  90.9 27.1 %all-to-all-start.5 = ((bf16[16,128,256]{2,1,0:T(8,128)(2,1)}), bf16[16,128,256]{2,1,0:T(8,128)(2,1)S(1)}, u32[]{:S(2)}, u32[]{:S(2)}) async-start(bf16[16,128,256]{2,1,0:T(8,128)(2,1)} %get-tuple-element.116), calls=%async_computation.5 | async-start | bytes 2097152 | tf_op jit(solution)/shard_map/all_to_all | solution.py:394
  100.8 72.6 %all-gather.2.cloned.1.call-start = ((), (), s32[]{:S(2)}) async-start(), calls=%async_computation.20 | async-start | bytes 1114112 | tf_op jit(solution)/shard_map/all_gather | solution.py:561
  146.3 11.8 %all-to-all-start.8 = ((bf16[8,32,1024]{2,1,0:T(8,128)(2,1)}), bf16[8,32,1024]{2,1,0:T(8,128)(2,1)}, u32[]{:S(2)}, u32[]{:S(2)}) async-start(bf16[8,32,1024]{2,1,0:T(8,128)(2,1)} %get-tuple-element.120), calls=%async_computation.8 | async-start | bytes 1048576 | tf_op jit(solution)/shard_map/all_to_all | solution.py:394
  160.1 11.0 %all-to-all-start.9 = ((bf16[8,32,1024]{2,1,0:T(8,128)(2,1)}), bf16[8,32,1024]{2,1,0:T(8,128)(2,1)S(1)}, u32[]{:S(2)}, u32[]{:S(2)}) async-start(bf16[8,32,1024]{2,1,0:T(8,128)(2,1)} %get-tuple-element.124), calls=%async_computation.9 | async-start | bytes 1048576 | tf_op jit(solution)/shard_map/all_to_all | solution.py:394
  166.0 23.1 %collective-permute-start.22 = (bf16[512,1024]{1,0:T(8,128)(2,1)}, bf16[512,1024]{1,0:T(8,128)(2,1)}, u32[]{:S(2)}, u32[]{:S(2)}) collective-permute-start(bf16[512,1024]{1,0:T(8,128)(2,1)} %dynamic-slice_bitcast_fusion), channel_id=1, source_target_pairs={{0,1},{1,0},{2,3},{3,2},{4,5},{5,4},{6,7},{7,6},{8,9},{9,8},{10,11... | collective-permute-start | bytes 3145736 | tf_op jit(solution)/shard_map/ppermute | solution.py:409
  173.3 22.6 %all-to-all-start.10 = ((bf16[16,144,128]{2,1,0:T(8,128)(2,1)}), bf16[16,144,128]{2,1,0:T(8,128)(2,1)}, u32[]{:S(2)}, u32[]{:S(2)}) async-start(bf16[16,144,128]{2,1,0:T(8,128)(2,1)} %get-tuple-element.131), calls=%async_computation.10 | async-start | bytes 1179648 | tf_op jit(solution)/shard_map/all_to_all | solution.py:394
  198.8 48.3 %collective-permute-start.23 = (bf16[256,1024]{1,0:T(8,128)(2,1)}, bf16[256,1024]{1,0:T(8,128)(2,1)}, u32[]{:S(2)}, u32[]{:S(2)}) collective-permute-start(bf16[256,1024]{1,0:T(8,128)(2,1)} %dynamic-slice_bitcast_fusion.1), channel_id=1, source_target_pairs={{0,2},{1,3},{2,0},{3,1},{4,6},{5,7},{6,4},{7,5},{8,10},{9,11},{10,... | collective-permute-start | bytes 1572872 | tf_op jit(solution)/shard_map/ppermute | solution.py:409
  204.2 10.9 %all-to-all-start.11 = ((bf16[8,16,1024]{2,1,0:T(8,128)(2,1)}), bf16[8,16,1024]{2,1,0:T(8,128)(2,1)S(1)}, u32[]{:S(2)}, u32[]{:S(2)}) async-start(bf16[8,16,1024]{2,1,0:T(8,128)(2,1)} %get-tuple-element.134), calls=%async_computation.11 | async-start | bytes 524288 | tf_op jit(solution)/shard_map/all_to_all | solution.py:394
  211.1 30.5 %collective-permute-start.1 = (bf16[256,1024]{1,0:T(8,128)(2,1)S(1)}, bf16[256,1024]{1,0:T(8,128)(2,1)}, u32[]{:S(2)}, u32[]{:S(2)}) collective-permute-start(bf16[256,1024]{1,0:T(8,128)(2,1)S(1)} %dynamic-slice_bitcast_fusion.4), channel_id=1, source_target_pairs={{0,1},{1,0},{2,3},{3,2},{4,5},{5,4},{6,7},{7,6},{8,9},{9,8},{10,11... | collective-permute-start | bytes 1572872 | tf_op jit(solution)/shard_map/ppermute | solution.py:409
  216.9 9.7 %all-to-all-start.12 = ((bf16[8,16,1024]{2,1,0:T(8,128)(2,1)}), bf16[8,16,1024]{2,1,0:T(8,128)(2,1)S(1)}, u32[]{:S(2)}, u32[]{:S(2)}) async-start(bf16[8,16,1024]{2,1,0:T(8,128)(2,1)} %get-tuple-element.138), calls=%async_computation.12 | async-start | bytes 524288 | tf_op jit(solution)/shard_map/all_to_all | solution.py:394
  229.8 19.4 %all-to-all-start.13 = ((bf16[8,16,1024]{2,1,0:T(8,128)(2,1)}), bf16[8,16,1024]{2,1,0:T(8,128)(2,1)S(1)}, u32[]{:S(2)}, u32[]{:S(2)}) async-start(bf16[8,16,1024]{2,1,0:T(8,128)(2,1)} %get-tuple-element.140), calls=%async_computation.13 | async-start | bytes 524288 | tf_op jit(solution)/shard_map/all_to_all | solution.py:394
  238.8 34.2 %collective-permute-start.14 = (bf16[256,1024]{1,0:T(8,128)(2,1)}, bf16[256,1024]{1,0:T(8,128)(2,1)}, u32[]{:S(2)}, u32[]{:S(2)}) collective-permute-start(bf16[256,1024]{1,0:T(8,128)(2,1)} %dynamic-slice_bitcast_fusion.2), channel_id=1, source_target_pairs={{0,1},{1,0},{2,3},{3,2},{4,5},{5,4},{6,7},{7,6},{8,9},{9,8},{10,11... | collective-permute-start | bytes 1572872 | tf_op jit(solution)/shard_map/ppermute | solution.py:409
  243.6 12.8 %collective-permute-start.2 = (bf16[128,1024]{1,0:T(8,128)(2,1)}, bf16[128,1024]{1,0:T(8,128)(2,1)}, u32[]{:S(2)}, u32[]{:S(2)}) collective-permute-start(bf16[128,1024]{1,0:T(8,128)(2,1)} %dynamic-slice_bitcast_fusion.7), channel_id=1, source_target_pairs={{0,2},{1,3},{2,0},{3,1},{4,6},{5,7},{6,4},{7,5},{8,10},{9,11},{10,... | collective-permute-start | bytes 786440 | tf_op jit(solution)/shard_map/ppermute | solution.py:409
  246.8 31.0 %collective-permute-start.6 = (bf16[256,1024]{1,0:T(8,128)(2,1)}, bf16[256,1024]{1,0:T(8,128)(2,1)}, u32[]{:S(2)}, u32[]{:S(2)}) collective-permute-start(bf16[256,1024]{1,0:T(8,128)(2,1)} %dynamic-slice_bitcast_fusion.3), channel_id=1, source_target_pairs={{0,1},{1,0},{2,3},{3,2},{4,5},{5,4},{6,7},{7,6},{8,9},{9,8},{10,11... | collective-permute-start | bytes 1572872 | tf_op jit(solution)/shard_map/ppermute | solution.py:409
  250.9 12.2 %all-to-all-start.14 = ((bf16[8,16,1024]{2,1,0:T(8,128)(2,1)}), bf16[8,16,1024]{2,1,0:T(8,128)(2,1)S(1)}, u32[]{:S(2)}, u32[]{:S(2)}) async-start(bf16[8,16,1024]{2,1,0:T(8,128)(2,1)} %get-tuple-element.144), calls=%async_computation.14 | async-start | bytes 524288 | tf_op jit(solution)/shard_map/all_to_all | solution.py:394
  255.7 54.7 %all-reduce.4.cloned.1.call-start = ((), (), s32[]{:S(2)}) async-start(), calls=%async_computation.21 | async-start | bytes 1572864 | tf_op jit(solution)/shard_map/psum | solution.py:446
  265.3 19.4 %all-to-all-start.15 = ((bf16[16,144,128]{2,1,0:T(8,128)(2,1)}), bf16[16,144,128]{2,1,0:T(8,128)(2,1)S(1)}, u32[]{:S(2)}, u32[]{:S(2)}) async-start(bf16[16,144,128]{2,1,0:T(8,128)(2,1)} %get-tuple-element.147), calls=%async_computation.15 | async-start | bytes 1179648 | tf_op jit(solution)/shard_map/all_to_all | solution.py:394
  275.0 17.2 %collective-permute-start.15 = (bf16[128,1024]{1,0:T(8,128)(2,1)}, bf16[128,1024]{1,0:T(8,128)(2,1)}, u32[]{:S(2)}, u32[]{:S(2)}) collective-permute-start(bf16[128,1024]{1,0:T(8,128)(2,1)} %dynamic-slice_bitcast_fusion.5), channel_id=1, source_target_pairs={{0,2},{1,3},{2,0},{3,1},{4,6},{5,7},{6,4},{7,5},{8,10},{9,11},{10,... | collective-permute-start | bytes 786440 | tf_op jit(solution)/shard_map/ppermute | solution.py:409
  279.2 15.3 %collective-permute-start.7 = (bf16[128,1024]{1,0:T(8,128)(2,1)S(1)}, bf16[128,1024]{1,0:T(8,128)(2,1)}, u32[]{:S(2)}, u32[]{:S(2)}) collective-permute-start(bf16[128,1024]{1,0:T(8,128)(2,1)S(1)} %dynamic-slice_bitcast_fusion.6), channel_id=1, source_target_pairs={{0,2},{1,3},{2,0},{3,1},{4,6},{5,7},{6,4},{7,5},{8,10},{9,11},{10,... | collective-permute-start | bytes 786440 | tf_op jit(solution)/shard_map/ppermute | solution.py:409
  288.6 10.9 %all-to-all-start.16 = ((bf16[8,16,1024]{2,1,0:T(8,128)(2,1)}), bf16[8,16,1024]{2,1,0:T(8,128)(2,1)S(1)}, u32[]{:S(2)}, u32[]{:S(2)}) async-start(bf16[8,16,1024]{2,1,0:T(8,128)(2,1)} %get-tuple-element.150), calls=%async_computation.16 | async-start | bytes 524288 | tf_op jit(solution)/shard_map/all_to_all | solution.py:394
  293.3 18.0 %collective-permute-start.16 = (bf16[64,1024]{1,0:T(8,128)(2,1)S(1)}, bf16[64,1024]{1,0:T(8,128)(2,1)S(1)}, u32[]{:S(2)}, u32[]{:S(2)}) collective-permute-start(bf16[64,1024]{1,0:T(8,128)(2,1)S(1)} %dynamic-slice_bitcast_fusion.8), channel_id=1, source_target_pairs={{0,4},{1,5},{2,6},{3,7},{4,0},{5,1},{6,2},{7,3},{8,12},{9,13},{10,... | collective-permute-start | bytes 393224 | tf_op jit(solution)/shard_map/ppermute | solution.py:409
  304.4 11.6 %all-to-all-start.17 = ((bf16[8,24,1024]{2,1,0:T(8,128)(2,1)}), bf16[8,24,1024]{2,1,0:T(8,128)(2,1)S(1)}, u32[]{:S(2)}, u32[]{:S(2)}) async-start(bf16[8,24,1024]{2,1,0:T(8,128)(2,1)} %pad_maximum_fusion.4), calls=%async_computation.17 | async-start | bytes 786432 | tf_op jit(solution)/shard_map/all_to_all | solution.py:394
  308.8 16.9 %collective-permute-start.8 = (bf16[64,1024]{1,0:T(8,128)(2,1)S(1)}, bf16[64,1024]{1,0:T(8,128)(2,1)S(1)}, u32[]{:S(2)}, u32[]{:S(2)}) collective-permute-start(bf16[64,1024]{1,0:T(8,128)(2,1)S(1)} %dynamic-slice_bitcast_fusion.9), channel_id=1, source_target_pairs={{0,12},{1,13},{2,14},{3,15},{4,8},{5,9},{6,10},{7,11},{8,4},{9,5},... | collective-permute-start | bytes 393224 | tf_op jit(solution)/shard_map/ppermute | solution.py:409
  310.4 23.2 %collective-permute-start.24 = (bf16[256,1024]{1,0:T(8,128)(2,1)}, bf16[256,1024]{1,0:T(8,128)(2,1)}, u32[]{:S(2)}, u32[]{:S(2)}) collective-permute-start(bf16[256,1024]{1,0:T(8,128)(2,1)} %get-tuple-element.200), channel_id=1, source_target_pairs={{0,2},{1,3},{2,0},{3,1},{4,6},{5,7},{6,4},{7,5},{8,10},{9,11},{10,... | collective-permute-start | bytes 1572872 | tf_op jit(solution)/shard_map/ppermute | solution.py:409
  321.7 6.4 %collective-permute-start = (bf16[8,8,4224]{2,1,0:T(8,128)(2,1)S(1)}, bf16[8,8,4224]{2,1,0:T(8,128)(2,1)S(1)}, u32[]{:S(2)}, u32[]{:S(2)}) collective-permute-start(bf16[8,8,4224]{2,1,0:T(8,128)(2,1)S(1)} %fusion.7), channel_id=1, source_target_pairs={{0,1},{1,0},{2,3},{3,2},{4,5},{5,4},{6,7},{7,6},{8,9},{9,8},{10,11... | collective-permute-start | bytes 1622024 | tf_op jit(solution)/shard_map/ppermute | solution.py:409
  324.2 12.1 %collective-permute-start.17 = (bf16[32,1024]{1,0:T(8,128)(2,1)S(1)}, bf16[32,1024]{1,0:T(8,128)(2,1)S(1)}, u32[]{:S(2)}, u32[]{:S(2)}) collective-permute-start(bf16[32,1024]{1,0:T(8,128)(2,1)S(1)} %dynamic-slice_bitcast_fusion.10), channel_id=1, source_target_pairs={{0,12},{1,13},{2,14},{3,15},{4,8},{5,9},{6,10},{7,11},{8,4},{9,5},... | collective-permute-start | bytes 196616 | tf_op jit(solution)/shard_map/ppermute | solution.py:409
  326.4 13.0 %collective-permute-start.9 = (bf16[32,1024]{1,0:T(8,128)(2,1)}, bf16[32,1024]{1,0:T(8,128)(2,1)S(1)}, u32[]{:S(2)}, u32[]{:S(2)}) collective-permute-start(bf16[32,1024]{1,0:T(8,128)(2,1)} %dynamic-slice_bitcast_fusion.11), channel_id=1, source_target_pairs={{0,4},{1,5},{2,6},{3,7},{4,0},{5,1},{6,2},{7,3},{8,12},{9,13},{10,... | collective-permute-start | bytes 196616 | tf_op jit(solution)/shard_map/ppermute | solution.py:409
  326.9 12.6 %collective-permute-start.3 = (bf16[128,1024]{1,0:T(8,128)(2,1)S(1)}, bf16[128,1024]{1,0:T(8,128)(2,1)S(1)}, u32[]{:S(2)}, u32[]{:S(2)}) collective-permute-start(bf16[128,1024]{1,0:T(8,128)(2,1)S(1)} %copy-done.20), channel_id=1, source_target_pairs={{0,2},{1,3},{2,0},{3,1},{4,6},{5,7},{6,4},{7,5},{8,10},{9,11},{10,... | collective-permute-start | bytes 786440 | tf_op jit(solution)/shard_map/ppermute | solution.py:409
  329.0 23.1 %all-to-all-start.18 = ((bf16[8,8,4224]{2,1,0:T(8,128)(2,1)}), bf16[8,8,4224]{2,1,0:T(8,128)(2,1)S(1)}, u32[]{:S(2)}, u32[]{:S(2)}) async-start(bf16[8,8,4224]{2,1,0:T(8,128)(2,1)} %fusion.1), calls=%async_computation.18 | async-start | bytes 1081344 | tf_op jit(solution)/shard_map/all_to_all | solution.py:451
  335.1 45.6 %collective-permute-start.25 = (bf16[512,1024]{1,0:T(8,128)(2,1)S(1)}, bf16[512,1024]{1,0:T(8,128)(2,1)}, u32[]{:S(2)}, u32[]{:S(2)}) collective-permute-start(bf16[512,1024]{1,0:T(8,128)(2,1)S(1)} %pad_maximum_fusion.own_ref), channel_id=1, source_target_pairs={{0,1},{1,0},{2,3},{3,2},{4,5},{5,4},{6,7},{7,6},{8,9},{9,8},{10,11... | collective-permute-start | bytes 3145736 | tf_op jit(solution)/shard_map/ppermute | solution.py:409
  336.3 6.7 %collective-permute-start.18 = (bf16[32,1024]{1,0:T(8,128)(2,1)S(1)}, bf16[32,1024]{1,0:T(8,128)(2,1)S(1)}, u32[]{:S(2)}, u32[]{:S(2)}) collective-permute-start(bf16[32,1024]{1,0:T(8,128)(2,1)S(1)} %fusion.15), channel_id=1, source_target_pairs={{0,12},{1,13},{2,14},{3,15},{4,8},{5,9},{6,10},{7,11},{8,4},{9,5},... | collective-permute-start | bytes 196616 | tf_op jit(solution)/shard_map/ppermute | solution.py:409
  339.4 4.1 %collective-permute-start.10 = (bf16[32,1024]{1,0:T(8,128)(2,1)S(1)}, bf16[32,1024]{1,0:T(8,128)(2,1)S(1)}, u32[]{:S(2)}, u32[]{:S(2)}) collective-permute-start(bf16[32,1024]{1,0:T(8,128)(2,1)S(1)} %fusion.16), channel_id=1, source_target_pairs={{0,4},{1,5},{2,6},{3,7},{4,0},{5,1},{6,2},{7,3},{8,12},{9,13},{10,... | collective-permute-start | bytes 196616 | tf_op jit(solution)/shard_map/ppermute | solution.py:409
  339.6 31.2 %collective-permute-start.4 = (bf16[256,1024]{1,0:T(8,128)(2,1)S(1)}, bf16[256,1024]{1,0:T(8,128)(2,1)}, u32[]{:S(2)}, u32[]{:S(2)}) collective-permute-start(bf16[256,1024]{1,0:T(8,128)(2,1)S(1)} %pad_maximum_fusion.1.own_ref), channel_id=1, source_target_pairs={{0,1},{1,0},{2,3},{3,2},{4,5},{5,4},{6,7},{7,6},{8,9},{9,8},{10,11... | collective-permute-start | bytes 1572872 | tf_op jit(solution)/shard_map/ppermute | solution.py:409
  343.0 3.9 collective-permute-start.19
  343.5 7.3 %collective-permute-start.11 = (bf16[64,1024]{1,0:T(8,128)(2,1)S(1)}, bf16[64,1024]{1,0:T(8,128)(2,1)S(1)}, u32[]{:S(2)}, u32[]{:S(2)}) collective-permute-start(bf16[64,1024]{1,0:T(8,128)(2,1)S(1)} %pad_maximum_fusion.7), channel_id=1, source_target_pairs={{0,12},{1,13},{2,14},{3,15},{4,8},{5,9},{6,10},{7,11},{8,4},{9,5},... | collective-permute-start | bytes 393224 | tf_op jit(solution)/shard_map/ppermute | solution.py:409
  347.7 7.1 %collective-permute-start.20 = (bf16[128,1024]{1,0:T(8,128)(2,1)}, bf16[128,1024]{1,0:T(8,128)(2,1)}, u32[]{:S(2)}, u32[]{:S(2)}) collective-permute-start(bf16[128,1024]{1,0:T(8,128)(2,1)} %pad_maximum_fusion.6), channel_id=1, source_target_pairs={{0,2},{1,3},{2,0},{3,1},{4,6},{5,7},{6,4},{7,5},{8,10},{9,11},{10,... | collective-permute-start | bytes 786440 | tf_op jit(solution)/shard_map/ppermute | solution.py:409
  351.6 17.3 %collective-permute-start.12 = (bf16[128,1024]{1,0:T(8,128)(2,1)}, bf16[128,1024]{1,0:T(8,128)(2,1)}, u32[]{:S(2)}, u32[]{:S(2)}) collective-permute-start(bf16[128,1024]{1,0:T(8,128)(2,1)} %pad_maximum_fusion.5), channel_id=1, source_target_pairs={{0,2},{1,3},{2,0},{3,1},{4,6},{5,7},{6,4},{7,5},{8,10},{9,11},{10,... | collective-permute-start | bytes 786440 | tf_op jit(solution)/shard_map/ppermute | solution.py:409
  355.7 15.5 %all-to-all-start.19 = ((bf16[8,8,4224]{2,1,0:T(8,128)(2,1)}), bf16[8,8,4224]{2,1,0:T(8,128)(2,1)S(1)}, u32[]{:S(2)}, u32[]{:S(2)}) async-start(bf16[8,8,4224]{2,1,0:T(8,128)(2,1)} %broadcast_in_dim.15), calls=%async_computation.19 | async-start | bytes 1081344 | tf_op jit(solution)/shard_map/all_to_all | solution.py:451
  363.7 16.9 %collective-permute-start.21 = (bf16[256,1024]{1,0:T(8,128)(2,1)S(1)}, bf16[256,1024]{1,0:T(8,128)(2,1)}, u32[]{:S(2)}, u32[]{:S(2)}) collective-permute-start(bf16[256,1024]{1,0:T(8,128)(2,1)S(1)} %pad_maximum_fusion.3.f_own), channel_id=1, source_target_pairs={{0,1},{1,0},{2,3},{3,2},{4,5},{5,4},{6,7},{7,6},{8,9},{9,8},{10,11... | collective-permute-start | bytes 1572872 | tf_op jit(solution)/shard_map/ppermute | solution.py:409
  371.1 15.7 %collective-permute-start.5 = (bf16[8,8,4224]{2,1,0:T(8,128)(2,1)S(1)}, bf16[8,8,4224]{2,1,0:T(8,128)(2,1)}, u32[]{:S(2)}, u32[]{:S(2)}) collective-permute-start(bf16[8,8,4224]{2,1,0:T(8,128)(2,1)S(1)} %all-to-all-done.19.late_own), channel_id=1, source_target_pairs={{0,1},{1,0},{2,3},{3,2},{4,5},{5,4},{6,7},{7,6},{8,9},{9,8},{10,11... | collective-permute-start | bytes 1622024 | tf_op jit(solution)/shard_map/ppermute | solution.py:409
  378.5 2.1 collective-permute-start.13
  (30 other events, 324.3 us)
Sparse Core Ops, SparseCore 0:
  104.0 44.8 all-gather.1
  260.1 46.7 all-reduce.3

commit v4 on v3

--- a/solution.py
+++ b/solution.py
@@ -435,9 +435,9 @@
     steps = ((4, x_low ^ x_high), (12, x_high)) if turn else ((12, x_high), (4, x_low ^ x_high))
     for (flip, side), event in zip(steps, events):
         value = halve(value, flip, event, side)
-    for flip, side in steps[::-1]:
-        value = rejoin(value, flip, side)
-    value = rejoin(value, DEPTH, None, events[-1])
+    for (flip, side), event in zip(steps[::-1], (None, events[-1])):
+        value = rejoin(value, flip, side, event)
+    value = rejoin(value, DEPTH)
     return value, swap(value, CORE)
 
 

time: 405 us -> 397 us (0.980)
  starting transfers between devices: 135 us -> 128 us
    ppermute x26, starting transfers between devices: 46.9 us -> 40 us  [swap(): lax.ppermute(value, 'dp', [(i, i ^ flip) for i in range(lax.axis_size('dp...]
    ppermute x26, waiting for transfers between devices: 6.15 us -> 1.9 us  [swap(): lax.ppermute(value, 'dp', [(i, i ^ flip) for i in range(lax.axis_size('dp...]
  transfers between devices with their start and end apart: 45 -> 45, of which waited for: 19 -> 17; matrix products, arithmetic and copies ran while one was open for 13% -> 12% of each run, Pallas kernels for 14% -> 14%
where the time goes in v4:
time: 397 us; the launch traced here: 393 us
  starting transfers between devices  128 us (32%)
  waiting for transfers between devices  89.4 us (23%)
  Pallas kernels  74.1 us (19%)
  other arithmetic  37.5 us (9%)
  blocking collectives  28.5 us (7%)
  local copies, waits for them, and re-layouts  20.4 us (5%)
  between operations  14.9 us (4%)
    all_to_all x15, waiting for transfers between devices, swap_all(): return lax.all_to_all(value, axis, 0, 0)  84 us
    all_to_all x15, starting transfers between devices, swap_all(): return lax.all_to_all(value, axis, 0, 0)  76.8 us
    pallas_call x26, Pallas kernels, call(): pl.pallas_call(kernel, grid=(1,), in_specs=[spec(index, arg) for index, a...  74.1 us
    ppermute x26, starting transfers between devices, swap(): lax.ppermute(value, 'dp', [(i, i ^ flip) for i in range(lax.axis_size('dp...  40 us
    all_to_all x3, blocking collectives, swap_all(): return lax.all_to_all(value, axis, 0, 0)  28.5 us
    convert_element_type x13, other arithmetic, halve(): return (mine.astype(F32) + got.astype(F32)).astype(BF16)  12.5 us
    all_to_all x2, starting transfers between devices, swap_chips(): return lax.all_to_all(value, 'dp', 0, 0, axis_index_groups=groups)  11.1 us
    squeeze x12, local copies, waits for them, and re-layouts, halve(): lax.dynamic_index_in_dim(halves, 1 - side, 0, keepdims=False)  8.13 us
  transfers between devices with their start and end apart: 45, of which 17 were waited for; matrix products, arithmetic and copies ran while one was open for 12% of the time, Pallas kernels for 14%

profile of v4, /device:TPU:1, one launch (start us, length us, event | category | flops | bytes accessed | tf_op | source)
XLA Modules:
  0.0 392.6 jit_solution(9471925454884840931)
XLA Ops:
  12.1 9.3 %all-to-all-start = ((bf16[16,128,256]{2,1,0:T(8,128)(2,1)}), bf16[16,128,256]{2,1,0:T(8,128)(2,1)S(1)}, u32[]{:S(2)}, u32[]{:S(2)}) async-start(bf16[16,128,256]{2,1,0:T(8,128)(2,1)} %get-tuple-element.109), calls=%async_computation | async-start | bytes 2097152 | tf_op jit(solution)/shard_map/all_to_all | solution.py:394
  22.9 15.7 %all-to-all-done.kv_ref = bf16[16,128,256]{2,1,0:T(8,128)(2,1)S(1)} async-done(((bf16[16,128,256]{2,1,0:T(8,128)(2,1)}), bf16[16,128,256]{2,1,0:T(8,128)(2,1)S(1)}, u32[]{:S(2)}, u32[]{:S(2)}) %all-to-all-start) | async-done | bytes 1048608 | tf_op jit(solution)/shard_map/all_to_all | solution.py:394
  38.6 3.6 shard_map.221
  42.2 4.6 %all-to-all-start.1 = ((bf16[8,16,1024]{2,1,0:T(8,128)(2,1)}), bf16[8,16,1024]{2,1,0:T(8,128)(2,1)S(1)}, u32[]{:S(2)}, u32[]{:S(2)}) async-start(bf16[8,16,1024]{2,1,0:T(8,128)(2,1)} %get-tuple-element.110), calls=%async_computation.1 | async-start | bytes 524288 | tf_op jit(solution)/shard_map/all_to_all | solution.py:394
  48.1 5.2 %all-to-all-done.1.parts_ref = bf16[8,16,1024]{2,1,0:T(8,128)(2,1)S(1)} async-done(((bf16[8,16,1024]{2,1,0:T(8,128)(2,1)}), bf16[8,16,1024]{2,1,0:T(8,128)(2,1)S(1)}, u32[]{:S(2)}, u32[]{:S(2)}) %all-to-all-start.1) | async-done | bytes 262176 | tf_op jit(solution)/shard_map/all_to_all | solution.py:394
  55.1 3.4 all-to-all-start.2
  59.2 5.5 %all-to-all-done.2 = bf16[8,16,1024]{2,1,0:T(8,128)(2,1)S(1)} async-done(((bf16[8,16,1024]{2,1,0:T(8,128)(2,1)}), bf16[8,16,1024]{2,1,0:T(8,128)(2,1)S(1)}, u32[]{:S(2)}, u32[]{:S(2)}) %all-to-all-start.2) | async-done | bytes 262176 | tf_op jit(solution)/shard_map/all_to_all | solution.py:394
  67.5 3.4 all-to-all-start.3
  71.5 5.5 %all-to-all-done.3.parts_ref = bf16[8,16,1024]{2,1,0:T(8,128)(2,1)S(1)} async-done(((bf16[8,16,1024]{2,1,0:T(8,128)(2,1)}), bf16[8,16,1024]{2,1,0:T(8,128)(2,1)S(1)}, u32[]{:S(2)}, u32[]{:S(2)}) %all-to-all-start.3) | async-done | bytes 262176 | tf_op jit(solution)/shard_map/all_to_all | solution.py:394
  78.8 9.5 %all_to_all.100 = bf16[8,16,1024]{2,1,0:T(8,128)(2,1)S(1)} all-to-all(bf16[8,16,1024]{2,1,0:T(8,128)(2,1)} %get-tuple-element.114), channel_id=1, replica_groups=mesh['tensor'=8,'dp'=16] {'tensor'}, dimensions={0} | all-to-all | bytes 524288 | tf_op jit(solution)/shard_map/all_to_all | solution.py:394
  90.9 9.9 %all-to-all-start.5 = ((bf16[16,128,256]{2,1,0:T(8,128)(2,1)}), bf16[16,128,256]{2,1,0:T(8,128)(2,1)S(1)}, u32[]{:S(2)}, u32[]{:S(2)}) async-start(bf16[16,128,256]{2,1,0:T(8,128)(2,1)} %get-tuple-element.116), calls=%async_computation.5 | async-start | bytes 2097152 | tf_op jit(solution)/shard_map/all_to_all | solution.py:394
  101.5 16.5 %all-to-all-done.5.kv_ref = bf16[16,128,256]{2,1,0:T(8,128)(2,1)S(1)} async-done(((bf16[16,128,256]{2,1,0:T(8,128)(2,1)}), bf16[16,128,256]{2,1,0:T(8,128)(2,1)S(1)}, u32[]{:S(2)}, u32[]{:S(2)}) %all-to-all-start.5) | async-done | bytes 1048608 | tf_op jit(solution)/shard_map/all_to_all | solution.py:394
  118.0 3.6 shard_map.226
  121.6 9.6 %all_to_all.101.parts_ref = bf16[8,16,1024]{2,1,0:T(8,128)(2,1)S(1)} all-to-all(bf16[8,16,1024]{2,1,0:T(8,128)(2,1)} %get-tuple-element.117), channel_id=1, replica_groups=mesh['tensor'=8,'dp'=16] {'tensor'}, dimensions={0} | all-to-all | bytes 524288 | tf_op jit(solution)/shard_map/all_to_all | solution.py:394
  133.0 9.5 %all_to_all.102 = bf16[8,16,1024]{2,1,0:T(8,128)(2,1)S(1)} all-to-all(bf16[8,16,1024]{2,1,0:T(8,128)(2,1)} %get-tuple-element.119), channel_id=1, replica_groups=mesh['tensor'=8,'dp'=16] {'tensor'}, dimensions={0} | all-to-all | bytes 524288 | tf_op jit(solution)/shard_map/all_to_all | solution.py:394
  142.5 3.8 shard_map.228
  146.3 4.1 %all-to-all-start.8 = ((bf16[8,32,1024]{2,1,0:T(8,128)(2,1)}), bf16[8,32,1024]{2,1,0:T(8,128)(2,1)}, u32[]{:S(2)}, u32[]{:S(2)}) async-start(bf16[8,32,1024]{2,1,0:T(8,128)(2,1)} %get-tuple-element.120), calls=%async_computation.8 | async-start | bytes 1048576 | tf_op jit(solution)/shard_map/all_to_all | solution.py:394
  151.1 3.0 shard_map.243
  154.1 3.9 %all-to-all-done.8.parts_ref = bf16[8,32,1024]{2,1,0:T(8,128)(2,1)} async-done(((bf16[8,32,1024]{2,1,0:T(8,128)(2,1)}), bf16[8,32,1024]{2,1,0:T(8,128)(2,1)}, u32[]{:S(2)}, u32[]{:S(2)}) %all-to-all-start.8) | async-done | bytes 524320 | tf_op jit(solution)/shard_map/all_to_all | solution.py:394
  160.1 3.5 all-to-all-start.9
  166.0 4.2 %collective-permute-start.22 = (bf16[512,1024]{1,0:T(8,128)(2,1)}, bf16[512,1024]{1,0:T(8,128)(2,1)}, u32[]{:S(2)}, u32[]{:S(2)}) collective-permute-start(bf16[512,1024]{1,0:T(8,128)(2,1)} %dynamic-slice_bitcast_fusion), channel_id=1, source_target_pairs={{0,1},{1,0},{2,3},{3,2},{4,5},{5,4},{6,7},{7,6},{8,9},{9,8},{10,11... | collective-permute-start | bytes 3145736 | tf_op jit(solution)/shard_map/ppermute | solution.py:409
  173.3 10.8 %all-to-all-start.10 = ((bf16[16,144,128]{2,1,0:T(8,128)(2,1)}), bf16[16,144,128]{2,1,0:T(8,128)(2,1)}, u32[]{:S(2)}, u32[]{:S(2)}) async-start(bf16[16,144,128]{2,1,0:T(8,128)(2,1)} %get-tuple-element.131), calls=%async_computation.10 | async-start | bytes 1179648 | tf_op jit(solution)/shard_map/all_to_all | solution.py:394
  185.0 2.9 shard_map.231.gq_ref
  187.9 8.0 %all-to-all-done.10.got_ref = bf16[16,144,128]{2,1,0:T(8,128)(2,1)} async-done(((bf16[16,144,128]{2,1,0:T(8,128)(2,1)}), bf16[16,144,128]{2,1,0:T(8,128)(2,1)}, u32[]{:S(2)}, u32[]{:S(2)}) %all-to-all-start.10) | async-done | bytes 589856 | tf_op jit(solution)/shard_map/all_to_all | solution.py:394
  200.2 4.0 %shard_map.232 = (bf16[128,256]{1,0:T(8,128)(2,1)}, bf16[8,16,1024]{2,1,0:T(8,128)(2,1)}) custom-call(s32[1]{0:T(128)} %bitcast.start_ref, s32[128,1]{1,0:T(8,128)} %copy.41.own_ref, s32[1,2048]{1,0:T(1,128)} %bitcast.183, bf16[128,256]{1,0:T(8,128)(2,1)} %get-tuple-element.130.kv_ref, bf16[2048,256]{1,0:T(8,128)(2,1)} %all-gather.2.cloned.1.call-done.q_ref, ...), custom_call_target="tpu_custom_call" | custom-call | flops 1000 | bytes 1000 | tf_op jit(solution)/shard_map/pallas_call | solution.py:65
  204.2 3.4 all-to-all-start.11
  216.9 3.4 all-to-all-start.12
  222.4 4.2 %all-to-all-done.12 = bf16[8,16,1024]{2,1,0:T(8,128)(2,1)S(1)} async-done(((bf16[8,16,1024]{2,1,0:T(8,128)(2,1)}), bf16[8,16,1024]{2,1,0:T(8,128)(2,1)S(1)}, u32[]{:S(2)}, u32[]{:S(2)}) %all-to-all-start.12) | async-done | bytes 262176 | tf_op jit(solution)/shard_map/all_to_all | solution.py:394
  226.5 3.2 shard_map.234
  229.8 3.4 all-to-all-start.13
  233.2 3.0 shard_map.241
  249.9 4.7 %all-to-all-start.14 = ((bf16[8,16,1024]{2,1,0:T(8,128)(2,1)}), bf16[8,16,1024]{2,1,0:T(8,128)(2,1)S(1)}, u32[]{:S(2)}, u32[]{:S(2)}) async-start(bf16[8,16,1024]{2,1,0:T(8,128)(2,1)} %get-tuple-element.144), calls=%async_computation.14 | async-start | bytes 524288 | tf_op jit(solution)/shard_map/all_to_all | solution.py:394
  257.2 4.9 %all-to-all-done.14.gy_ref = bf16[8,16,1024]{2,1,0:T(8,128)(2,1)S(1)} async-done(((bf16[8,16,1024]{2,1,0:T(8,128)(2,1)}), bf16[8,16,1024]{2,1,0:T(8,128)(2,1)S(1)}, u32[]{:S(2)}, u32[]{:S(2)}) %all-to-all-start.14) | async-done | bytes 262176 | tf_op jit(solution)/shard_map/all_to_all | solution.py:394
  264.3 5.2 %all-to-all-start.15 = ((bf16[16,144,128]{2,1,0:T(8,128)(2,1)}), bf16[16,144,128]{2,1,0:T(8,128)(2,1)S(1)}, u32[]{:S(2)}, u32[]{:S(2)}) async-start(bf16[16,144,128]{2,1,0:T(8,128)(2,1)} %get-tuple-element.147), calls=%async_computation.15 | async-start | bytes 1179648 | tf_op jit(solution)/shard_map/all_to_all | solution.py:394
  269.5 2.9 shard_map.237.gq_ref
  274.4 2.9 collective-permute-start.15
  278.8 5.4 %all-to-all-done.15.got_ref = bf16[16,144,128]{2,1,0:T(8,128)(2,1)S(1)} async-done(((bf16[16,144,128]{2,1,0:T(8,128)(2,1)}), bf16[16,144,128]{2,1,0:T(8,128)(2,1)S(1)}, u32[]{:S(2)}, u32[]{:S(2)}) %all-to-all-start.15) | async-done | bytes 589856 | tf_op jit(solution)/shard_map/all_to_all | solution.py:394
  284.2 3.9 shard_map.238
  288.1 3.4 all-to-all-start.16
  303.8 4.1 %all-to-all-start.17 = ((bf16[8,24,1024]{2,1,0:T(8,128)(2,1)}), bf16[8,24,1024]{2,1,0:T(8,128)(2,1)S(1)}, u32[]{:S(2)}, u32[]{:S(2)}) async-start(bf16[8,24,1024]{2,1,0:T(8,128)(2,1)} %pad_maximum_fusion.4), calls=%async_computation.17 | async-start | bytes 786432 | tf_op jit(solution)/shard_map/all_to_all | solution.py:394
  310.4 4.8 %all-to-all-done.17 = bf16[8,24,1024]{2,1,0:T(8,128)(2,1)S(1)} async-done(((bf16[8,24,1024]{2,1,0:T(8,128)(2,1)}), bf16[8,24,1024]{2,1,0:T(8,128)(2,1)S(1)}, u32[]{:S(2)}, u32[]{:S(2)}) %all-to-all-start.17) | async-done | bytes 393248 | tf_op jit(solution)/shard_map/all_to_all | solution.py:394
  324.2 4.7 %all-to-all-start.18 = ((bf16[8,8,4224]{2,1,0:T(8,128)(2,1)}), bf16[8,8,4224]{2,1,0:T(8,128)(2,1)S(1)}, u32[]{:S(2)}, u32[]{:S(2)}) async-start(bf16[8,8,4224]{2,1,0:T(8,128)(2,1)} %fusion.1), calls=%async_computation.18 | async-start | bytes 1081344 | tf_op jit(solution)/shard_map/all_to_all | solution.py:451
  331.6 3.0 collective-permute-start.18
  350.1 6.4 %all-to-all-start.19 = ((bf16[8,8,4224]{2,1,0:T(8,128)(2,1)}), bf16[8,8,4224]{2,1,0:T(8,128)(2,1)S(1)}, u32[]{:S(2)}, u32[]{:S(2)}) async-start(bf16[8,8,4224]{2,1,0:T(8,128)(2,1)} %broadcast_in_dim.15), calls=%async_computation.19 | async-start | bytes 1081344 | tf_op jit(solution)/shard_map/all_to_all | solution.py:451
  361.8 3.4 all-to-all-done.19.late_own
  365.2 3.5 collective-permute-start.5
  371.9 6.2 %shard_map.245 = (f32[2,512,1024]{2,1,0:T(8,128)}, f32[2,1024,512]{2,1,0:T(8,128)}) custom-call(s32[1]{0:T(128)} %bitcast.39.side_ref, bf16[256,1024]{1,0:T(8,128)(2,1)} %copy-done.11, bf16[256,1024]{1,0:T(8,128)(2,1)} %collective-permute-done.13.p_got, bf16[256,1024]{1,0:T(8,128)(2,1)} %copy-done.10, bf16[256,1024]{1,0:T(8,128)(2,1)} %collective-permute-done.21.f_got, ...), custom_call_target="tpu_custom_call" | custom-call | flops 1000 | bytes 1000 | tf_op jit(solution)/shard_map/pallas_call | solution.py:65
  382.1 3.7 shard_map.244
  (246 shorter events, 120.9 us)
Async XLA Ops:
  12.1 34.8 %copy-start.17 = (bf16[128,1024]{1,0:T(8,128)(2,1)S(1)}, bf16[128,1024]{1,0:T(8,128)(2,1)}, u32[]{:S(2)}) copy-start(bf16[128,1024]{1,0:T(8,128)(2,1)} %x_ref.1) | copy-start | bytes 786436
  12.1 35.4 %copy-start.21 = (bf16[2,1024]{1,0:T(2,128)(2,1)S(1)}, bf16[2,1024]{1,0:T(2,128)(2,1)}, u32[]{:S(2)}) copy-start(bf16[2,1024]{1,0:T(2,128)(2,1)} %param.20) | copy-start | bytes 12292
  12.1 26.5 %all-to-all-start = ((bf16[16,128,256]{2,1,0:T(8,128)(2,1)}), bf16[16,128,256]{2,1,0:T(8,128)(2,1)S(1)}, u32[]{:S(2)}, u32[]{:S(2)}) async-start(bf16[16,128,256]{2,1,0:T(8,128)(2,1)} %get-tuple-element.109), calls=%async_computation | async-start | bytes 2097152 | tf_op jit(solution)/shard_map/all_to_all | solution.py:394
  21.4 37.2 %copy-start.27 = (bf16[2,512]{1,0:T(2,128)(2,1)S(1)}, bf16[2,512]{1,0:T(2,128)(2,1)}, u32[]{:S(2)}) copy-start(bf16[2,512]{1,0:T(2,128)(2,1)} %param.22) | copy-start | bytes 6148
  42.2 11.1 %all-to-all-start.1 = ((bf16[8,16,1024]{2,1,0:T(8,128)(2,1)}), bf16[8,16,1024]{2,1,0:T(8,128)(2,1)S(1)}, u32[]{:S(2)}, u32[]{:S(2)}) async-start(bf16[8,16,1024]{2,1,0:T(8,128)(2,1)} %get-tuple-element.110), calls=%async_computation.1 | async-start | bytes 524288 | tf_op jit(solution)/shard_map/all_to_all | solution.py:394
  55.1 9.5 %all-to-all-start.2 = ((bf16[8,16,1024]{2,1,0:T(8,128)(2,1)}), bf16[8,16,1024]{2,1,0:T(8,128)(2,1)S(1)}, u32[]{:S(2)}, u32[]{:S(2)}) async-start(bf16[8,16,1024]{2,1,0:T(8,128)(2,1)} %get-tuple-element.111), calls=%async_computation.2 | async-start | bytes 524288 | tf_op jit(solution)/shard_map/all_to_all | solution.py:394
  67.5 9.5 %all-to-all-start.3 = ((bf16[8,16,1024]{2,1,0:T(8,128)(2,1)}), bf16[8,16,1024]{2,1,0:T(8,128)(2,1)S(1)}, u32[]{:S(2)}, u32[]{:S(2)}) async-start(bf16[8,16,1024]{2,1,0:T(8,128)(2,1)} %get-tuple-element.112), calls=%async_computation.3 | async-start | bytes 524288 | tf_op jit(solution)/shard_map/all_to_all | solution.py:394
  90.9 27.1 %all-to-all-start.5 = ((bf16[16,128,256]{2,1,0:T(8,128)(2,1)}), bf16[16,128,256]{2,1,0:T(8,128)(2,1)S(1)}, u32[]{:S(2)}, u32[]{:S(2)}) async-start(bf16[16,128,256]{2,1,0:T(8,128)(2,1)} %get-tuple-element.116), calls=%async_computation.5 | async-start | bytes 2097152 | tf_op jit(solution)/shard_map/all_to_all | solution.py:394
  100.8 72.6 %all-gather.2.cloned.1.call-start = ((), (), s32[]{:S(2)}) async-start(), calls=%async_computation.20 | async-start | bytes 1114112 | tf_op jit(solution)/shard_map/all_gather | solution.py:561
  146.3 11.8 %all-to-all-start.8 = ((bf16[8,32,1024]{2,1,0:T(8,128)(2,1)}), bf16[8,32,1024]{2,1,0:T(8,128)(2,1)}, u32[]{:S(2)}, u32[]{:S(2)}) async-start(bf16[8,32,1024]{2,1,0:T(8,128)(2,1)} %get-tuple-element.120), calls=%async_computation.8 | async-start | bytes 1048576 | tf_op jit(solution)/shard_map/all_to_all | solution.py:394
  160.1 11.0 %all-to-all-start.9 = ((bf16[8,32,1024]{2,1,0:T(8,128)(2,1)}), bf16[8,32,1024]{2,1,0:T(8,128)(2,1)S(1)}, u32[]{:S(2)}, u32[]{:S(2)}) async-start(bf16[8,32,1024]{2,1,0:T(8,128)(2,1)} %get-tuple-element.124), calls=%async_computation.9 | async-start | bytes 1048576 | tf_op jit(solution)/shard_map/all_to_all | solution.py:394
  166.0 22.0 %collective-permute-start.22 = (bf16[512,1024]{1,0:T(8,128)(2,1)}, bf16[512,1024]{1,0:T(8,128)(2,1)}, u32[]{:S(2)}, u32[]{:S(2)}) collective-permute-start(bf16[512,1024]{1,0:T(8,128)(2,1)} %dynamic-slice_bitcast_fusion), channel_id=1, source_target_pairs={{0,1},{1,0},{2,3},{3,2},{4,5},{5,4},{6,7},{7,6},{8,9},{9,8},{10,11... | collective-permute-start | bytes 3145736 | tf_op jit(solution)/shard_map/ppermute | solution.py:409
  173.3 22.6 %all-to-all-start.10 = ((bf16[16,144,128]{2,1,0:T(8,128)(2,1)}), bf16[16,144,128]{2,1,0:T(8,128)(2,1)}, u32[]{:S(2)}, u32[]{:S(2)}) async-start(bf16[16,144,128]{2,1,0:T(8,128)(2,1)} %get-tuple-element.131), calls=%async_computation.10 | async-start | bytes 1179648 | tf_op jit(solution)/shard_map/all_to_all | solution.py:394
  198.8 47.3 %collective-permute-start.23 = (bf16[256,1024]{1,0:T(8,128)(2,1)}, bf16[256,1024]{1,0:T(8,128)(2,1)}, u32[]{:S(2)}, u32[]{:S(2)}) collective-permute-start(bf16[256,1024]{1,0:T(8,128)(2,1)} %dynamic-slice_bitcast_fusion.1), channel_id=1, source_target_pairs={{0,2},{1,3},{2,0},{3,1},{4,6},{5,7},{6,4},{7,5},{8,10},{9,11},{10,... | collective-permute-start | bytes 1572872 | tf_op jit(solution)/shard_map/ppermute | solution.py:409
  204.2 10.9 %all-to-all-start.11 = ((bf16[8,16,1024]{2,1,0:T(8,128)(2,1)}), bf16[8,16,1024]{2,1,0:T(8,128)(2,1)S(1)}, u32[]{:S(2)}, u32[]{:S(2)}) async-start(bf16[8,16,1024]{2,1,0:T(8,128)(2,1)} %get-tuple-element.134), calls=%async_computation.11 | async-start | bytes 524288 | tf_op jit(solution)/shard_map/all_to_all | solution.py:394
  211.1 30.5 %collective-permute-start.1 = (bf16[256,1024]{1,0:T(8,128)(2,1)S(1)}, bf16[256,1024]{1,0:T(8,128)(2,1)}, u32[]{:S(2)}, u32[]{:S(2)}) collective-permute-start(bf16[256,1024]{1,0:T(8,128)(2,1)S(1)} %dynamic-slice_bitcast_fusion.4), channel_id=1, source_target_pairs={{0,1},{1,0},{2,3},{3,2},{4,5},{5,4},{6,7},{7,6},{8,9},{9,8},{10,11... | collective-permute-start | bytes 1572872 | tf_op jit(solution)/shard_map/ppermute | solution.py:409
  216.9 9.7 %all-to-all-start.12 = ((bf16[8,16,1024]{2,1,0:T(8,128)(2,1)}), bf16[8,16,1024]{2,1,0:T(8,128)(2,1)S(1)}, u32[]{:S(2)}, u32[]{:S(2)}) async-start(bf16[8,16,1024]{2,1,0:T(8,128)(2,1)} %get-tuple-element.138), calls=%async_computation.12 | async-start | bytes 524288 | tf_op jit(solution)/shard_map/all_to_all | solution.py:394
  229.8 18.4 %all-to-all-start.13 = ((bf16[8,16,1024]{2,1,0:T(8,128)(2,1)}), bf16[8,16,1024]{2,1,0:T(8,128)(2,1)S(1)}, u32[]{:S(2)}, u32[]{:S(2)}) async-start(bf16[8,16,1024]{2,1,0:T(8,128)(2,1)} %get-tuple-element.140), calls=%async_computation.13 | async-start | bytes 524288 | tf_op jit(solution)/shard_map/all_to_all | solution.py:394
  238.8 33.7 %collective-permute-start.14 = (bf16[256,1024]{1,0:T(8,128)(2,1)}, bf16[256,1024]{1,0:T(8,128)(2,1)}, u32[]{:S(2)}, u32[]{:S(2)}) collective-permute-start(bf16[256,1024]{1,0:T(8,128)(2,1)} %dynamic-slice_bitcast_fusion.2), channel_id=1, source_target_pairs={{0,1},{1,0},{2,3},{3,2},{4,5},{5,4},{6,7},{7,6},{8,9},{9,8},{10,11... | collective-permute-start | bytes 1572872 | tf_op jit(solution)/shard_map/ppermute | solution.py:409
  243.6 11.9 %collective-permute-start.2 = (bf16[128,1024]{1,0:T(8,128)(2,1)}, bf16[128,1024]{1,0:T(8,128)(2,1)}, u32[]{:S(2)}, u32[]{:S(2)}) collective-permute-start(bf16[128,1024]{1,0:T(8,128)(2,1)} %dynamic-slice_bitcast_fusion.7), channel_id=1, source_target_pairs={{0,2},{1,3},{2,0},{3,1},{4,6},{5,7},{6,4},{7,5},{8,10},{9,11},{10,... | collective-permute-start | bytes 786440 | tf_op jit(solution)/shard_map/ppermute | solution.py:409
  245.7 31.6 %collective-permute-start.6 = (bf16[256,1024]{1,0:T(8,128)(2,1)}, bf16[256,1024]{1,0:T(8,128)(2,1)}, u32[]{:S(2)}, u32[]{:S(2)}) collective-permute-start(bf16[256,1024]{1,0:T(8,128)(2,1)} %dynamic-slice_bitcast_fusion.3), channel_id=1, source_target_pairs={{0,1},{1,0},{2,3},{3,2},{4,5},{5,4},{6,7},{7,6},{8,9},{9,8},{10,11... | collective-permute-start | bytes 1572872 | tf_op jit(solution)/shard_map/ppermute | solution.py:409
  249.9 12.2 %all-to-all-start.14 = ((bf16[8,16,1024]{2,1,0:T(8,128)(2,1)}), bf16[8,16,1024]{2,1,0:T(8,128)(2,1)S(1)}, u32[]{:S(2)}, u32[]{:S(2)}) async-start(bf16[8,16,1024]{2,1,0:T(8,128)(2,1)} %get-tuple-element.144), calls=%async_computation.14 | async-start | bytes 524288 | tf_op jit(solution)/shard_map/all_to_all | solution.py:394
  254.7 54.6 %all-reduce.4.cloned.1.call-start = ((), (), s32[]{:S(2)}) async-start(), calls=%async_computation.21 | async-start | bytes 1572864 | tf_op jit(solution)/shard_map/psum | solution.py:446
  264.3 19.9 %all-to-all-start.15 = ((bf16[16,144,128]{2,1,0:T(8,128)(2,1)}), bf16[16,144,128]{2,1,0:T(8,128)(2,1)S(1)}, u32[]{:S(2)}, u32[]{:S(2)}) async-start(bf16[16,144,128]{2,1,0:T(8,128)(2,1)} %get-tuple-element.147), calls=%async_computation.15 | async-start | bytes 1179648 | tf_op jit(solution)/shard_map/all_to_all | solution.py:394
  274.4 17.1 %collective-permute-start.15 = (bf16[128,1024]{1,0:T(8,128)(2,1)}, bf16[128,1024]{1,0:T(8,128)(2,1)}, u32[]{:S(2)}, u32[]{:S(2)}) collective-permute-start(bf16[128,1024]{1,0:T(8,128)(2,1)} %dynamic-slice_bitcast_fusion.5), channel_id=1, source_target_pairs={{0,2},{1,3},{2,0},{3,1},{4,6},{5,7},{6,4},{7,5},{8,10},{9,11},{10,... | collective-permute-start | bytes 786440 | tf_op jit(solution)/shard_map/ppermute | solution.py:409
  278.6 15.1 %collective-permute-start.7 = (bf16[128,1024]{1,0:T(8,128)(2,1)S(1)}, bf16[128,1024]{1,0:T(8,128)(2,1)}, u32[]{:S(2)}, u32[]{:S(2)}) collective-permute-start(bf16[128,1024]{1,0:T(8,128)(2,1)S(1)} %dynamic-slice_bitcast_fusion.6), channel_id=1, source_target_pairs={{0,2},{1,3},{2,0},{3,1},{4,6},{5,7},{6,4},{7,5},{8,10},{9,11},{10,... | collective-permute-start | bytes 786440 | tf_op jit(solution)/shard_map/ppermute | solution.py:409
  288.1 10.8 %all-to-all-start.16 = ((bf16[8,16,1024]{2,1,0:T(8,128)(2,1)}), bf16[8,16,1024]{2,1,0:T(8,128)(2,1)S(1)}, u32[]{:S(2)}, u32[]{:S(2)}) async-start(bf16[8,16,1024]{2,1,0:T(8,128)(2,1)} %get-tuple-element.150), calls=%async_computation.16 | async-start | bytes 524288 | tf_op jit(solution)/shard_map/all_to_all | solution.py:394
  292.6 17.8 %collective-permute-start.16 = (bf16[64,1024]{1,0:T(8,128)(2,1)S(1)}, bf16[64,1024]{1,0:T(8,128)(2,1)S(1)}, u32[]{:S(2)}, u32[]{:S(2)}) collective-permute-start(bf16[64,1024]{1,0:T(8,128)(2,1)S(1)} %dynamic-slice_bitcast_fusion.8), channel_id=1, source_target_pairs={{0,4},{1,5},{2,6},{3,7},{4,0},{5,1},{6,2},{7,3},{8,12},{9,13},{10,... | collective-permute-start | bytes 393224 | tf_op jit(solution)/shard_map/ppermute | solution.py:409
  303.8 11.4 %all-to-all-start.17 = ((bf16[8,24,1024]{2,1,0:T(8,128)(2,1)}), bf16[8,24,1024]{2,1,0:T(8,128)(2,1)S(1)}, u32[]{:S(2)}, u32[]{:S(2)}) async-start(bf16[8,24,1024]{2,1,0:T(8,128)(2,1)} %pad_maximum_fusion.4), calls=%async_computation.17 | async-start | bytes 786432 | tf_op jit(solution)/shard_map/all_to_all | solution.py:394
  307.9 12.8 %collective-permute-start.8 = (bf16[64,1024]{1,0:T(8,128)(2,1)S(1)}, bf16[64,1024]{1,0:T(8,128)(2,1)S(1)}, u32[]{:S(2)}, u32[]{:S(2)}) collective-permute-start(bf16[64,1024]{1,0:T(8,128)(2,1)S(1)} %dynamic-slice_bitcast_fusion.9), channel_id=1, source_target_pairs={{0,12},{1,13},{2,14},{3,15},{4,8},{5,9},{6,10},{7,11},{8,4},{9,5},... | collective-permute-start | bytes 393224 | tf_op jit(solution)/shard_map/ppermute | solution.py:409
  309.3 19.6 %collective-permute-start.24 = (bf16[256,1024]{1,0:T(8,128)(2,1)}, bf16[256,1024]{1,0:T(8,128)(2,1)}, u32[]{:S(2)}, u32[]{:S(2)}) collective-permute-start(bf16[256,1024]{1,0:T(8,128)(2,1)} %get-tuple-element.200), channel_id=1, source_target_pairs={{0,2},{1,3},{2,0},{3,1},{4,6},{5,7},{6,4},{7,5},{8,10},{9,11},{10,... | collective-permute-start | bytes 1572872 | tf_op jit(solution)/shard_map/ppermute | solution.py:409
  317.0 6.3 %collective-permute-start = (bf16[8,8,4224]{2,1,0:T(8,128)(2,1)S(1)}, bf16[8,8,4224]{2,1,0:T(8,128)(2,1)S(1)}, u32[]{:S(2)}, u32[]{:S(2)}) collective-permute-start(bf16[8,8,4224]{2,1,0:T(8,128)(2,1)S(1)} %fusion.7), channel_id=1, source_target_pairs={{0,1},{1,0},{2,3},{3,2},{4,5},{5,4},{6,7},{7,6},{8,9},{9,8},{10,11... | collective-permute-start | bytes 1622024 | tf_op jit(solution)/shard_map/ppermute | solution.py:409
  319.4 12.1 %collective-permute-start.17 = (bf16[32,1024]{1,0:T(8,128)(2,1)S(1)}, bf16[32,1024]{1,0:T(8,128)(2,1)S(1)}, u32[]{:S(2)}, u32[]{:S(2)}) collective-permute-start(bf16[32,1024]{1,0:T(8,128)(2,1)S(1)} %dynamic-slice_bitcast_fusion.10), channel_id=1, source_target_pairs={{0,12},{1,13},{2,14},{3,15},{4,8},{5,9},{6,10},{7,11},{8,4},{9,5},... | collective-permute-start | bytes 196616 | tf_op jit(solution)/shard_map/ppermute | solution.py:409
  321.4 13.2 %collective-permute-start.9 = (bf16[32,1024]{1,0:T(8,128)(2,1)}, bf16[32,1024]{1,0:T(8,128)(2,1)S(1)}, u32[]{:S(2)}, u32[]{:S(2)}) collective-permute-start(bf16[32,1024]{1,0:T(8,128)(2,1)} %dynamic-slice_bitcast_fusion.11), channel_id=1, source_target_pairs={{0,4},{1,5},{2,6},{3,7},{4,0},{5,1},{6,2},{7,3},{8,12},{9,13},{10,... | collective-permute-start | bytes 196616 | tf_op jit(solution)/shard_map/ppermute | solution.py:409
  322.1 12.6 %collective-permute-start.3 = (bf16[128,1024]{1,0:T(8,128)(2,1)}, bf16[128,1024]{1,0:T(8,128)(2,1)}, u32[]{:S(2)}, u32[]{:S(2)}) collective-permute-start(bf16[128,1024]{1,0:T(8,128)(2,1)} %get-tuple-element.180), channel_id=1, source_target_pairs={{0,2},{1,3},{2,0},{3,1},{4,6},{5,7},{6,4},{7,5},{8,10},{9,11},{10,... | collective-permute-start | bytes 786440 | tf_op jit(solution)/shard_map/ppermute | solution.py:409
  324.2 17.9 %all-to-all-start.18 = ((bf16[8,8,4224]{2,1,0:T(8,128)(2,1)}), bf16[8,8,4224]{2,1,0:T(8,128)(2,1)S(1)}, u32[]{:S(2)}, u32[]{:S(2)}) async-start(bf16[8,8,4224]{2,1,0:T(8,128)(2,1)} %fusion.1), calls=%async_computation.18 | async-start | bytes 1081344 | tf_op jit(solution)/shard_map/all_to_all | solution.py:451
  330.3 41.5 %collective-permute-start.25 = (bf16[512,1024]{1,0:T(8,128)(2,1)S(1)}, bf16[512,1024]{1,0:T(8,128)(2,1)}, u32[]{:S(2)}, u32[]{:S(2)}) collective-permute-start(bf16[512,1024]{1,0:T(8,128)(2,1)S(1)} %pad_maximum_fusion.own_ref), channel_id=1, source_target_pairs={{0,1},{1,0},{2,3},{3,2},{4,5},{5,4},{6,7},{7,6},{8,9},{9,8},{10,11... | collective-permute-start | bytes 3145736 | tf_op jit(solution)/shard_map/ppermute | solution.py:409
  331.6 6.7 %collective-permute-start.18 = (bf16[32,1024]{1,0:T(8,128)(2,1)S(1)}, bf16[32,1024]{1,0:T(8,128)(2,1)S(1)}, u32[]{:S(2)}, u32[]{:S(2)}) collective-permute-start(bf16[32,1024]{1,0:T(8,128)(2,1)S(1)} %fusion.15), channel_id=1, source_target_pairs={{0,12},{1,13},{2,14},{3,15},{4,8},{5,9},{6,10},{7,11},{8,4},{9,5},... | collective-permute-start | bytes 196616 | tf_op jit(solution)/shard_map/ppermute | solution.py:409
  334.6 4.1 %collective-permute-start.10 = (bf16[32,1024]{1,0:T(8,128)(2,1)S(1)}, bf16[32,1024]{1,0:T(8,128)(2,1)S(1)}, u32[]{:S(2)}, u32[]{:S(2)}) collective-permute-start(bf16[32,1024]{1,0:T(8,128)(2,1)S(1)} %fusion.16), channel_id=1, source_target_pairs={{0,4},{1,5},{2,6},{3,7},{4,0},{5,1},{6,2},{7,3},{8,12},{9,13},{10,... | collective-permute-start | bytes 196616 | tf_op jit(solution)/shard_map/ppermute | solution.py:409
  335.9 26.0 %collective-permute-start.4 = (bf16[256,1024]{1,0:T(8,128)(2,1)S(1)}, bf16[256,1024]{1,0:T(8,128)(2,1)}, u32[]{:S(2)}, u32[]{:S(2)}) collective-permute-start(bf16[256,1024]{1,0:T(8,128)(2,1)S(1)} %pad_maximum_fusion.1.own_ref), channel_id=1, source_target_pairs={{0,1},{1,0},{2,3},{3,2},{4,5},{5,4},{6,7},{7,6},{8,9},{9,8},{10,11... | collective-permute-start | bytes 1572872 | tf_op jit(solution)/shard_map/ppermute | solution.py:409
  338.3 4.5 %collective-permute-start.19 = (bf16[64,1024]{1,0:T(8,128)(2,1)S(1)}, bf16[64,1024]{1,0:T(8,128)(2,1)}, u32[]{:S(2)}, u32[]{:S(2)}) collective-permute-start(bf16[64,1024]{1,0:T(8,128)(2,1)S(1)} %pad_maximum_fusion.8), channel_id=1, source_target_pairs={{0,4},{1,5},{2,6},{3,7},{4,0},{5,1},{6,2},{7,3},{8,12},{9,13},{10,... | collective-permute-start | bytes 393224 | tf_op jit(solution)/shard_map/ppermute | solution.py:409
  339.4 7.6 %collective-permute-start.11 = (bf16[64,1024]{1,0:T(8,128)(2,1)}, bf16[64,1024]{1,0:T(8,128)(2,1)}, u32[]{:S(2)}, u32[]{:S(2)}) collective-permute-start(bf16[64,1024]{1,0:T(8,128)(2,1)} %pad_maximum_fusion.7), channel_id=1, source_target_pairs={{0,12},{1,13},{2,14},{3,15},{4,8},{5,9},{6,10},{7,11},{8,4},{9,5},... | collective-permute-start | bytes 393224 | tf_op jit(solution)/shard_map/ppermute | solution.py:409
  344.5 12.0 %collective-permute-start.20 = (bf16[128,1024]{1,0:T(8,128)(2,1)}, bf16[128,1024]{1,0:T(8,128)(2,1)}, u32[]{:S(2)}, u32[]{:S(2)}) collective-permute-start(bf16[128,1024]{1,0:T(8,128)(2,1)} %pad_maximum_fusion.6), channel_id=1, source_target_pairs={{0,2},{1,3},{2,0},{3,1},{4,6},{5,7},{6,4},{7,5},{8,10},{9,11},{10,... | collective-permute-start | bytes 786440 | tf_op jit(solution)/shard_map/ppermute | solution.py:409
  348.8 11.2 %collective-permute-start.12 = (bf16[128,1024]{1,0:T(8,128)(2,1)}, bf16[128,1024]{1,0:T(8,128)(2,1)}, u32[]{:S(2)}, u32[]{:S(2)}) collective-permute-start(bf16[128,1024]{1,0:T(8,128)(2,1)} %pad_maximum_fusion.5), channel_id=1, source_target_pairs={{0,2},{1,3},{2,0},{3,1},{4,6},{5,7},{6,4},{7,5},{8,10},{9,11},{10,... | collective-permute-start | bytes 786440 | tf_op jit(solution)/shard_map/ppermute | solution.py:409
  350.1 15.1 %all-to-all-start.19 = ((bf16[8,8,4224]{2,1,0:T(8,128)(2,1)}), bf16[8,8,4224]{2,1,0:T(8,128)(2,1)S(1)}, u32[]{:S(2)}, u32[]{:S(2)}) async-start(bf16[8,8,4224]{2,1,0:T(8,128)(2,1)} %broadcast_in_dim.15), calls=%async_computation.19 | async-start | bytes 1081344 | tf_op jit(solution)/shard_map/all_to_all | solution.py:451
  357.6 14.2 %collective-permute-start.21 = (bf16[256,1024]{1,0:T(8,128)(2,1)S(1)}, bf16[256,1024]{1,0:T(8,128)(2,1)}, u32[]{:S(2)}, u32[]{:S(2)}) collective-permute-start(bf16[256,1024]{1,0:T(8,128)(2,1)S(1)} %pad_maximum_fusion.3.f_own), channel_id=1, source_target_pairs={{0,1},{1,0},{2,3},{3,2},{4,5},{5,4},{6,7},{7,6},{8,9},{9,8},{10,11... | collective-permute-start | bytes 1572872 | tf_op jit(solution)/shard_map/ppermute | solution.py:409
  365.2 12.9 %collective-permute-start.5 = (bf16[8,8,4224]{2,1,0:T(8,128)(2,1)S(1)}, bf16[8,8,4224]{2,1,0:T(8,128)(2,1)}, u32[]{:S(2)}, u32[]{:S(2)}) collective-permute-start(bf16[8,8,4224]{2,1,0:T(8,128)(2,1)S(1)} %all-to-all-done.19.late_own), channel_id=1, source_target_pairs={{0,1},{1,0},{2,3},{3,2},{4,5},{5,4},{6,7},{7,6},{8,9},{9,8},{10,11... | collective-permute-start | bytes 1622024 | tf_op jit(solution)/shard_map/ppermute | solution.py:409
  369.8 2.1 collective-permute-start.13
  (28 other events, 271.8 us)
Sparse Core Ops, SparseCore 0:
  104.0 44.8 all-gather.1
  259.1 47.3 all-reduce.3

commit v5 on v4

--- a/solution.py
+++ b/solution.py
@@ -727,7 +727,8 @@
     starts = [halve(halve(part, CORE, grad_b), DEPTH, g_kv) for part in (end_pack[:hidden], end_pack[hidden:])]
     events = (grad, half, mine)
     end_parts = [part for turn, value in enumerate(starts) for part in finish_sums(value, turn, events)]
-    end_last, attend_last = [rejoin(after(part, grad), DEPTH, None, half) for part in done[1]]
+    end_last = rejoin(after(done[1][0], grad), DEPTH, None, half)
+    attend_last = rejoin(after(done[1][1], half), DEPTH)
     side = side_of(CORE)
     sides = side.astype(jnp.int32).reshape(1)
     g_w_proj, g_w_fc = call(

time: 397 us -> 397 us (level)
  waiting for transfers between devices: 89.4 us -> 97 us
  starting transfers between devices: 128 us -> 122 us
    ppermute x26, waiting for transfers between devices: 1.9 us -> 10.4 us  [swap(): lax.ppermute(value, 'dp', [(i, i ^ flip) for i in range(lax.axis_size('dp...]
  transfers between devices with their start and end apart: 45 -> 45, of which waited for: 17 -> 20; matrix products, arithmetic and copies ran while one was open for 12% -> 12% of each run, Pallas kernels for 14% -> 14%
where the time goes in v5:
time: 397 us; the launch traced here: 393 us
  starting transfers between devices  122 us (31%)
  waiting for transfers between devices  97 us (24%)
  Pallas kernels  74.1 us (19%)
  other arithmetic  36.4 us (9%)
  blocking collectives  28.5 us (7%)
  local copies, waits for them, and re-layouts  19.8 us (5%)
  between operations  14.9 us (4%)
    all_to_all x15, waiting for transfers between devices, swap_all(): return lax.all_to_all(value, axis, 0, 0)  84 us
    all_to_all x15, starting transfers between devices, swap_all(): return lax.all_to_all(value, axis, 0, 0)  76.8 us
    pallas_call x26, Pallas kernels, call(): pl.pallas_call(kernel, grid=(1,), in_specs=[spec(index, arg) for index, a...  74.1 us
    ppermute x26, starting transfers between devices, swap(): lax.ppermute(value, 'dp', [(i, i ^ flip) for i in range(lax.axis_size('dp...  37.1 us
    all_to_all x3, blocking collectives, swap_all(): return lax.all_to_all(value, axis, 0, 0)  28.5 us
    convert_element_type x13, other arithmetic, halve(): return (mine.astype(F32) + got.astype(F32)).astype(BF16)  12.5 us
    ppermute x26, waiting for transfers between devices, swap(): lax.ppermute(value, 'dp', [(i, i ^ flip) for i in range(lax.axis_size('dp...  10.4 us
    all_to_all x2, starting transfers between devices, swap_chips(): return lax.all_to_all(value, 'dp', 0, 0, axis_index_groups=groups)  8.27 us
  transfers between devices with their start and end apart: 45, of which 20 were waited for; matrix products, arithmetic and copies ran while one was open for 12% of the time, Pallas kernels for 14%

profile of v5, /device:TPU:1, one launch (start us, length us, event | category | flops | bytes accessed | tf_op | source)
XLA Modules:
  0.0 393.0 jit_solution(4268817827735445820)
XLA Ops:
  12.1 9.3 %all-to-all-start = ((bf16[16,128,256]{2,1,0:T(8,128)(2,1)}), bf16[16,128,256]{2,1,0:T(8,128)(2,1)S(1)}, u32[]{:S(2)}, u32[]{:S(2)}) async-start(bf16[16,128,256]{2,1,0:T(8,128)(2,1)} %get-tuple-element.108), calls=%async_computation | async-start | bytes 2097152 | tf_op jit(solution)/shard_map/all_to_all | solution.py:394
  22.9 15.7 %all-to-all-done.kv_ref = bf16[16,128,256]{2,1,0:T(8,128)(2,1)S(1)} async-done(((bf16[16,128,256]{2,1,0:T(8,128)(2,1)}), bf16[16,128,256]{2,1,0:T(8,128)(2,1)S(1)}, u32[]{:S(2)}, u32[]{:S(2)}) %all-to-all-start) | async-done | bytes 1048608 | tf_op jit(solution)/shard_map/all_to_all | solution.py:394
  38.6 3.6 shard_map.221
  42.2 4.7 %all-to-all-start.1 = ((bf16[8,16,1024]{2,1,0:T(8,128)(2,1)}), bf16[8,16,1024]{2,1,0:T(8,128)(2,1)S(1)}, u32[]{:S(2)}, u32[]{:S(2)}) async-start(bf16[8,16,1024]{2,1,0:T(8,128)(2,1)} %get-tuple-element.109), calls=%async_computation.1 | async-start | bytes 524288 | tf_op jit(solution)/shard_map/all_to_all | solution.py:394
  48.1 5.2 %all-to-all-done.1.parts_ref = bf16[8,16,1024]{2,1,0:T(8,128)(2,1)S(1)} async-done(((bf16[8,16,1024]{2,1,0:T(8,128)(2,1)}), bf16[8,16,1024]{2,1,0:T(8,128)(2,1)S(1)}, u32[]{:S(2)}, u32[]{:S(2)}) %all-to-all-start.1) | async-done | bytes 262176 | tf_op jit(solution)/shard_map/all_to_all | solution.py:394
  55.1 3.4 all-to-all-start.2
  59.2 5.5 %all-to-all-done.2 = bf16[8,16,1024]{2,1,0:T(8,128)(2,1)S(1)} async-done(((bf16[8,16,1024]{2,1,0:T(8,128)(2,1)}), bf16[8,16,1024]{2,1,0:T(8,128)(2,1)S(1)}, u32[]{:S(2)}, u32[]{:S(2)}) %all-to-all-start.2) | async-done | bytes 262176 | tf_op jit(solution)/shard_map/all_to_all | solution.py:394
  67.5 3.4 all-to-all-start.3
  71.5 5.5 %all-to-all-done.3.parts_ref = bf16[8,16,1024]{2,1,0:T(8,128)(2,1)S(1)} async-done(((bf16[8,16,1024]{2,1,0:T(8,128)(2,1)}), bf16[8,16,1024]{2,1,0:T(8,128)(2,1)S(1)}, u32[]{:S(2)}, u32[]{:S(2)}) %all-to-all-start.3) | async-done | bytes 262176 | tf_op jit(solution)/shard_map/all_to_all | solution.py:394
  78.8 9.5 %all_to_all.100 = bf16[8,16,1024]{2,1,0:T(8,128)(2,1)S(1)} all-to-all(bf16[8,16,1024]{2,1,0:T(8,128)(2,1)} %get-tuple-element.113), channel_id=1, replica_groups=mesh['tensor'=8,'dp'=16] {'tensor'}, dimensions={0} | all-to-all | bytes 524288 | tf_op jit(solution)/shard_map/all_to_all | solution.py:394
  90.9 9.9 %all-to-all-start.5 = ((bf16[16,128,256]{2,1,0:T(8,128)(2,1)}), bf16[16,128,256]{2,1,0:T(8,128)(2,1)S(1)}, u32[]{:S(2)}, u32[]{:S(2)}) async-start(bf16[16,128,256]{2,1,0:T(8,128)(2,1)} %get-tuple-element.115), calls=%async_computation.5 | async-start | bytes 2097152 | tf_op jit(solution)/shard_map/all_to_all | solution.py:394
  101.5 16.5 %all-to-all-done.5.kv_ref = bf16[16,128,256]{2,1,0:T(8,128)(2,1)S(1)} async-done(((bf16[16,128,256]{2,1,0:T(8,128)(2,1)}), bf16[16,128,256]{2,1,0:T(8,128)(2,1)S(1)}, u32[]{:S(2)}, u32[]{:S(2)}) %all-to-all-start.5) | async-done | bytes 1048608 | tf_op jit(solution)/shard_map/all_to_all | solution.py:394
  118.0 3.6 shard_map.226
  121.6 9.6 %all_to_all.101.parts_ref = bf16[8,16,1024]{2,1,0:T(8,128)(2,1)S(1)} all-to-all(bf16[8,16,1024]{2,1,0:T(8,128)(2,1)} %get-tuple-element.116), channel_id=1, replica_groups=mesh['tensor'=8,'dp'=16] {'tensor'}, dimensions={0} | all-to-all | bytes 524288 | tf_op jit(solution)/shard_map/all_to_all | solution.py:394
  133.0 9.5 %all_to_all.102 = bf16[8,16,1024]{2,1,0:T(8,128)(2,1)S(1)} all-to-all(bf16[8,16,1024]{2,1,0:T(8,128)(2,1)} %get-tuple-element.118), channel_id=1, replica_groups=mesh['tensor'=8,'dp'=16] {'tensor'}, dimensions={0} | all-to-all | bytes 524288 | tf_op jit(solution)/shard_map/all_to_all | solution.py:394
  142.5 3.8 shard_map.228
  146.3 4.2 %all-to-all-start.8 = ((bf16[8,32,1024]{2,1,0:T(8,128)(2,1)}), bf16[8,32,1024]{2,1,0:T(8,128)(2,1)}, u32[]{:S(2)}, u32[]{:S(2)}) async-start(bf16[8,32,1024]{2,1,0:T(8,128)(2,1)} %get-tuple-element.119), calls=%async_computation.8 | async-start | bytes 1048576 | tf_op jit(solution)/shard_map/all_to_all | solution.py:394
  151.1 3.0 shard_map.243
  154.1 3.9 %all-to-all-done.8.parts_ref = bf16[8,32,1024]{2,1,0:T(8,128)(2,1)} async-done(((bf16[8,32,1024]{2,1,0:T(8,128)(2,1)}), bf16[8,32,1024]{2,1,0:T(8,128)(2,1)}, u32[]{:S(2)}, u32[]{:S(2)}) %all-to-all-start.8) | async-done | bytes 524320 | tf_op jit(solution)/shard_map/all_to_all | solution.py:394
  160.1 3.5 all-to-all-start.9
  166.0 4.2 %collective-permute-start.22 = (bf16[512,1024]{1,0:T(8,128)(2,1)}, bf16[512,1024]{1,0:T(8,128)(2,1)}, u32[]{:S(2)}, u32[]{:S(2)}) collective-permute-start(bf16[512,1024]{1,0:T(8,128)(2,1)} %dynamic-slice_bitcast_fusion), channel_id=1, source_target_pairs={{0,1},{1,0},{2,3},{3,2},{4,5},{5,4},{6,7},{7,6},{8,9},{9,8},{10,11... | collective-permute-start | bytes 3145736 | tf_op jit(solution)/shard_map/ppermute | solution.py:409
  173.3 10.8 %all-to-all-start.10 = ((bf16[16,144,128]{2,1,0:T(8,128)(2,1)}), bf16[16,144,128]{2,1,0:T(8,128)(2,1)}, u32[]{:S(2)}, u32[]{:S(2)}) async-start(bf16[16,144,128]{2,1,0:T(8,128)(2,1)} %get-tuple-element.130), calls=%async_computation.10 | async-start | bytes 1179648 | tf_op jit(solution)/shard_map/all_to_all | solution.py:394
  185.0 2.9 shard_map.231.gq_ref
  187.9 8.0 %all-to-all-done.10.got_ref = bf16[16,144,128]{2,1,0:T(8,128)(2,1)} async-done(((bf16[16,144,128]{2,1,0:T(8,128)(2,1)}), bf16[16,144,128]{2,1,0:T(8,128)(2,1)}, u32[]{:S(2)}, u32[]{:S(2)}) %all-to-all-start.10) | async-done | bytes 589856 | tf_op jit(solution)/shard_map/all_to_all | solution.py:394
  200.2 4.0 %shard_map.232 = (bf16[128,256]{1,0:T(8,128)(2,1)}, bf16[8,16,1024]{2,1,0:T(8,128)(2,1)}) custom-call(s32[1]{0:T(128)} %bitcast.start_ref, s32[128,1]{1,0:T(8,128)} %copy.41.own_ref, s32[1,2048]{1,0:T(1,128)} %bitcast.183, bf16[128,256]{1,0:T(8,128)(2,1)} %get-tuple-element.129.kv_ref, bf16[2048,256]{1,0:T(8,128)(2,1)} %all-gather.2.cloned.1.call-done.q_ref, ...), custom_call_target="tpu_custom_call" | custom-call | flops 1000 | bytes 1000 | tf_op jit(solution)/shard_map/pallas_call | solution.py:65
  204.2 3.4 all-to-all-start.11
  216.9 3.4 all-to-all-start.12
  222.4 4.2 %all-to-all-done.12 = bf16[8,16,1024]{2,1,0:T(8,128)(2,1)S(1)} async-done(((bf16[8,16,1024]{2,1,0:T(8,128)(2,1)}), bf16[8,16,1024]{2,1,0:T(8,128)(2,1)S(1)}, u32[]{:S(2)}, u32[]{:S(2)}) %all-to-all-start.12) | async-done | bytes 262176 | tf_op jit(solution)/shard_map/all_to_all | solution.py:394
  226.6 3.2 shard_map.234
  229.8 3.4 all-to-all-start.13
  233.2 3.0 shard_map.241
  250.0 4.7 %all-to-all-start.14 = ((bf16[8,16,1024]{2,1,0:T(8,128)(2,1)}), bf16[8,16,1024]{2,1,0:T(8,128)(2,1)S(1)}, u32[]{:S(2)}, u32[]{:S(2)}) async-start(bf16[8,16,1024]{2,1,0:T(8,128)(2,1)} %get-tuple-element.143), calls=%async_computation.14 | async-start | bytes 524288 | tf_op jit(solution)/shard_map/all_to_all | solution.py:394
  257.2 4.9 %all-to-all-done.14.gy_ref = bf16[8,16,1024]{2,1,0:T(8,128)(2,1)S(1)} async-done(((bf16[8,16,1024]{2,1,0:T(8,128)(2,1)}), bf16[8,16,1024]{2,1,0:T(8,128)(2,1)S(1)}, u32[]{:S(2)}, u32[]{:S(2)}) %all-to-all-start.14) | async-done | bytes 262176 | tf_op jit(solution)/shard_map/all_to_all | solution.py:394
  264.3 5.2 %all-to-all-start.15 = ((bf16[16,144,128]{2,1,0:T(8,128)(2,1)}), bf16[16,144,128]{2,1,0:T(8,128)(2,1)S(1)}, u32[]{:S(2)}, u32[]{:S(2)}) async-start(bf16[16,144,128]{2,1,0:T(8,128)(2,1)} %get-tuple-element.146), calls=%async_computation.15 | async-start | bytes 1179648 | tf_op jit(solution)/shard_map/all_to_all | solution.py:394
  269.5 3.0 shard_map.237.gq_ref
  274.5 2.9 collective-permute-start.15
  278.8 5.4 %all-to-all-done.15.got_ref = bf16[16,144,128]{2,1,0:T(8,128)(2,1)S(1)} async-done(((bf16[16,144,128]{2,1,0:T(8,128)(2,1)}), bf16[16,144,128]{2,1,0:T(8,128)(2,1)S(1)}, u32[]{:S(2)}, u32[]{:S(2)}) %all-to-all-start.15) | async-done | bytes 589856 | tf_op jit(solution)/shard_map/all_to_all | solution.py:394
  284.2 3.9 shard_map.238
  288.1 3.4 all-to-all-start.16
  303.8 4.1 %all-to-all-start.17 = ((bf16[8,24,1024]{2,1,0:T(8,128)(2,1)}), bf16[8,24,1024]{2,1,0:T(8,128)(2,1)S(1)}, u32[]{:S(2)}, u32[]{:S(2)}) async-start(bf16[8,24,1024]{2,1,0:T(8,128)(2,1)} %pad_maximum_fusion.4), calls=%async_computation.17 | async-start | bytes 786432 | tf_op jit(solution)/shard_map/all_to_all | solution.py:394
  310.5 4.8 %all-to-all-done.17 = bf16[8,24,1024]{2,1,0:T(8,128)(2,1)S(1)} async-done(((bf16[8,24,1024]{2,1,0:T(8,128)(2,1)}), bf16[8,24,1024]{2,1,0:T(8,128)(2,1)S(1)}, u32[]{:S(2)}, u32[]{:S(2)}) %all-to-all-start.17) | async-done | bytes 393248 | tf_op jit(solution)/shard_map/all_to_all | solution.py:394
  322.5 4.7 %all-to-all-start.18 = ((bf16[8,8,4224]{2,1,0:T(8,128)(2,1)}), bf16[8,8,4224]{2,1,0:T(8,128)(2,1)S(1)}, u32[]{:S(2)}, u32[]{:S(2)}) async-start(bf16[8,8,4224]{2,1,0:T(8,128)(2,1)} %fusion.1), calls=%async_computation.18 | async-start | bytes 1081344 | tf_op jit(solution)/shard_map/all_to_all | solution.py:451
  329.7 2.9 collective-permute-start.18
  340.3 3.9 collective-permute-done.3
  352.8 3.5 all-to-all-start.19
  359.4 4.4 %collective-permute-done.12 = bf16[128,1024]{1,0:T(8,128)(2,1)} collective-permute-done((bf16[128,1024]{1,0:T(8,128)(2,1)}, bf16[128,1024]{1,0:T(8,128)(2,1)}, u32[]{:S(2)}, u32[]{:S(2)}) %collective-permute-start.12) | collective-permute-done | bytes 262176 | tf_op jit(solution)/shard_map/ppermute | solution.py:409
  372.3 6.2 %shard_map.245 = (f32[2,512,1024]{2,1,0:T(8,128)}, f32[2,1024,512]{2,1,0:T(8,128)}) custom-call(s32[1]{0:T(128)} %bitcast.39.side_ref, bf16[256,1024]{1,0:T(8,128)(2,1)} %copy-done.11, bf16[256,1024]{1,0:T(8,128)(2,1)} %collective-permute-done.13.p_got, bf16[256,1024]{1,0:T(8,128)(2,1)} %copy-done.10, bf16[256,1024]{1,0:T(8,128)(2,1)} %collective-permute-done.21.f_got, ...), custom_call_target="tpu_custom_call" | custom-call | flops 1000 | bytes 1000 | tf_op jit(solution)/shard_map/pallas_call | solution.py:65
  382.5 3.7 shard_map.244
  (248 shorter events, 122.8 us)
Async XLA Ops:
  12.1 34.8 %copy-start.17 = (bf16[128,1024]{1,0:T(8,128)(2,1)S(1)}, bf16[128,1024]{1,0:T(8,128)(2,1)}, u32[]{:S(2)}) copy-start(bf16[128,1024]{1,0:T(8,128)(2,1)} %x_ref.1) | copy-start | bytes 786436
  12.1 35.4 %copy-start.22 = (bf16[2,1024]{1,0:T(2,128)(2,1)S(1)}, bf16[2,1024]{1,0:T(2,128)(2,1)}, u32[]{:S(2)}) copy-start(bf16[2,1024]{1,0:T(2,128)(2,1)} %param.20) | copy-start | bytes 12292
  12.1 26.5 %all-to-all-start = ((bf16[16,128,256]{2,1,0:T(8,128)(2,1)}), bf16[16,128,256]{2,1,0:T(8,128)(2,1)S(1)}, u32[]{:S(2)}, u32[]{:S(2)}) async-start(bf16[16,128,256]{2,1,0:T(8,128)(2,1)} %get-tuple-element.108), calls=%async_computation | async-start | bytes 2097152 | tf_op jit(solution)/shard_map/all_to_all | solution.py:394
  21.4 37.2 %copy-start.28 = (bf16[2,512]{1,0:T(2,128)(2,1)S(1)}, bf16[2,512]{1,0:T(2,128)(2,1)}, u32[]{:S(2)}) copy-start(bf16[2,512]{1,0:T(2,128)(2,1)} %param.22) | copy-start | bytes 6148
  42.2 11.1 %all-to-all-start.1 = ((bf16[8,16,1024]{2,1,0:T(8,128)(2,1)}), bf16[8,16,1024]{2,1,0:T(8,128)(2,1)S(1)}, u32[]{:S(2)}, u32[]{:S(2)}) async-start(bf16[8,16,1024]{2,1,0:T(8,128)(2,1)} %get-tuple-element.109), calls=%async_computation.1 | async-start | bytes 524288 | tf_op jit(solution)/shard_map/all_to_all | solution.py:394
  55.1 9.5 %all-to-all-start.2 = ((bf16[8,16,1024]{2,1,0:T(8,128)(2,1)}), bf16[8,16,1024]{2,1,0:T(8,128)(2,1)S(1)}, u32[]{:S(2)}, u32[]{:S(2)}) async-start(bf16[8,16,1024]{2,1,0:T(8,128)(2,1)} %get-tuple-element.110), calls=%async_computation.2 | async-start | bytes 524288 | tf_op jit(solution)/shard_map/all_to_all | solution.py:394
  67.5 9.5 %all-to-all-start.3 = ((bf16[8,16,1024]{2,1,0:T(8,128)(2,1)}), bf16[8,16,1024]{2,1,0:T(8,128)(2,1)S(1)}, u32[]{:S(2)}, u32[]{:S(2)}) async-start(bf16[8,16,1024]{2,1,0:T(8,128)(2,1)} %get-tuple-element.111), calls=%async_computation.3 | async-start | bytes 524288 | tf_op jit(solution)/shard_map/all_to_all | solution.py:394
  90.9 27.1 %all-to-all-start.5 = ((bf16[16,128,256]{2,1,0:T(8,128)(2,1)}), bf16[16,128,256]{2,1,0:T(8,128)(2,1)S(1)}, u32[]{:S(2)}, u32[]{:S(2)}) async-start(bf16[16,128,256]{2,1,0:T(8,128)(2,1)} %get-tuple-element.115), calls=%async_computation.5 | async-start | bytes 2097152 | tf_op jit(solution)/shard_map/all_to_all | solution.py:394
  100.8 72.6 %all-gather.2.cloned.1.call-start = ((), (), s32[]{:S(2)}) async-start(), calls=%async_computation.20 | async-start | bytes 1114112 | tf_op jit(solution)/shard_map/all_gather | solution.py:561
  146.3 11.8 %all-to-all-start.8 = ((bf16[8,32,1024]{2,1,0:T(8,128)(2,1)}), bf16[8,32,1024]{2,1,0:T(8,128)(2,1)}, u32[]{:S(2)}, u32[]{:S(2)}) async-start(bf16[8,32,1024]{2,1,0:T(8,128)(2,1)} %get-tuple-element.119), calls=%async_computation.8 | async-start | bytes 1048576 | tf_op jit(solution)/shard_map/all_to_all | solution.py:394
  160.1 11.0 %all-to-all-start.9 = ((bf16[8,32,1024]{2,1,0:T(8,128)(2,1)}), bf16[8,32,1024]{2,1,0:T(8,128)(2,1)S(1)}, u32[]{:S(2)}, u32[]{:S(2)}) async-start(bf16[8,32,1024]{2,1,0:T(8,128)(2,1)} %get-tuple-element.123), calls=%async_computation.9 | async-start | bytes 1048576 | tf_op jit(solution)/shard_map/all_to_all | solution.py:394
  166.0 22.0 %collective-permute-start.22 = (bf16[512,1024]{1,0:T(8,128)(2,1)}, bf16[512,1024]{1,0:T(8,128)(2,1)}, u32[]{:S(2)}, u32[]{:S(2)}) collective-permute-start(bf16[512,1024]{1,0:T(8,128)(2,1)} %dynamic-slice_bitcast_fusion), channel_id=1, source_target_pairs={{0,1},{1,0},{2,3},{3,2},{4,5},{5,4},{6,7},{7,6},{8,9},{9,8},{10,11... | collective-permute-start | bytes 3145736 | tf_op jit(solution)/shard_map/ppermute | solution.py:409
  173.3 22.6 %all-to-all-start.10 = ((bf16[16,144,128]{2,1,0:T(8,128)(2,1)}), bf16[16,144,128]{2,1,0:T(8,128)(2,1)}, u32[]{:S(2)}, u32[]{:S(2)}) async-start(bf16[16,144,128]{2,1,0:T(8,128)(2,1)} %get-tuple-element.130), calls=%async_computation.10 | async-start | bytes 1179648 | tf_op jit(solution)/shard_map/all_to_all | solution.py:394
  198.8 47.4 %collective-permute-start.23 = (bf16[256,1024]{1,0:T(8,128)(2,1)}, bf16[256,1024]{1,0:T(8,128)(2,1)}, u32[]{:S(2)}, u32[]{:S(2)}) collective-permute-start(bf16[256,1024]{1,0:T(8,128)(2,1)} %dynamic-slice_bitcast_fusion.1), channel_id=1, source_target_pairs={{0,2},{1,3},{2,0},{3,1},{4,6},{5,7},{6,4},{7,5},{8,10},{9,11},{10,... | collective-permute-start | bytes 1572872 | tf_op jit(solution)/shard_map/ppermute | solution.py:409
  204.2 10.9 %all-to-all-start.11 = ((bf16[8,16,1024]{2,1,0:T(8,128)(2,1)}), bf16[8,16,1024]{2,1,0:T(8,128)(2,1)S(1)}, u32[]{:S(2)}, u32[]{:S(2)}) async-start(bf16[8,16,1024]{2,1,0:T(8,128)(2,1)} %get-tuple-element.133), calls=%async_computation.11 | async-start | bytes 524288 | tf_op jit(solution)/shard_map/all_to_all | solution.py:394
  211.1 30.6 %collective-permute-start.1 = (bf16[256,1024]{1,0:T(8,128)(2,1)S(1)}, bf16[256,1024]{1,0:T(8,128)(2,1)}, u32[]{:S(2)}, u32[]{:S(2)}) collective-permute-start(bf16[256,1024]{1,0:T(8,128)(2,1)S(1)} %dynamic-slice_bitcast_fusion.4), channel_id=1, source_target_pairs={{0,1},{1,0},{2,3},{3,2},{4,5},{5,4},{6,7},{7,6},{8,9},{9,8},{10,11... | collective-permute-start | bytes 1572872 | tf_op jit(solution)/shard_map/ppermute | solution.py:409
  216.9 9.7 %all-to-all-start.12 = ((bf16[8,16,1024]{2,1,0:T(8,128)(2,1)}), bf16[8,16,1024]{2,1,0:T(8,128)(2,1)S(1)}, u32[]{:S(2)}, u32[]{:S(2)}) async-start(bf16[8,16,1024]{2,1,0:T(8,128)(2,1)} %get-tuple-element.137), calls=%async_computation.12 | async-start | bytes 524288 | tf_op jit(solution)/shard_map/all_to_all | solution.py:394
  229.8 18.4 %all-to-all-start.13 = ((bf16[8,16,1024]{2,1,0:T(8,128)(2,1)}), bf16[8,16,1024]{2,1,0:T(8,128)(2,1)S(1)}, u32[]{:S(2)}, u32[]{:S(2)}) async-start(bf16[8,16,1024]{2,1,0:T(8,128)(2,1)} %get-tuple-element.139), calls=%async_computation.13 | async-start | bytes 524288 | tf_op jit(solution)/shard_map/all_to_all | solution.py:394
  238.8 33.7 %collective-permute-start.14 = (bf16[256,1024]{1,0:T(8,128)(2,1)}, bf16[256,1024]{1,0:T(8,128)(2,1)}, u32[]{:S(2)}, u32[]{:S(2)}) collective-permute-start(bf16[256,1024]{1,0:T(8,128)(2,1)} %dynamic-slice_bitcast_fusion.2), channel_id=1, source_target_pairs={{0,1},{1,0},{2,3},{3,2},{4,5},{5,4},{6,7},{7,6},{8,9},{9,8},{10,11... | collective-permute-start | bytes 1572872 | tf_op jit(solution)/shard_map/ppermute | solution.py:409
  243.6 11.8 %collective-permute-start.2 = (bf16[128,1024]{1,0:T(8,128)(2,1)}, bf16[128,1024]{1,0:T(8,128)(2,1)}, u32[]{:S(2)}, u32[]{:S(2)}) collective-permute-start(bf16[128,1024]{1,0:T(8,128)(2,1)} %dynamic-slice_bitcast_fusion.7), channel_id=1, source_target_pairs={{0,2},{1,3},{2,0},{3,1},{4,6},{5,7},{6,4},{7,5},{8,10},{9,11},{10,... | collective-permute-start | bytes 786440 | tf_op jit(solution)/shard_map/ppermute | solution.py:409
  245.8 31.6 %collective-permute-start.6 = (bf16[256,1024]{1,0:T(8,128)(2,1)}, bf16[256,1024]{1,0:T(8,128)(2,1)}, u32[]{:S(2)}, u32[]{:S(2)}) collective-permute-start(bf16[256,1024]{1,0:T(8,128)(2,1)} %dynamic-slice_bitcast_fusion.3), channel_id=1, source_target_pairs={{0,1},{1,0},{2,3},{3,2},{4,5},{5,4},{6,7},{7,6},{8,9},{9,8},{10,11... | collective-permute-start | bytes 1572872 | tf_op jit(solution)/shard_map/ppermute | solution.py:409
  250.0 12.2 %all-to-all-start.14 = ((bf16[8,16,1024]{2,1,0:T(8,128)(2,1)}), bf16[8,16,1024]{2,1,0:T(8,128)(2,1)S(1)}, u32[]{:S(2)}, u32[]{:S(2)}) async-start(bf16[8,16,1024]{2,1,0:T(8,128)(2,1)} %get-tuple-element.143), calls=%async_computation.14 | async-start | bytes 524288 | tf_op jit(solution)/shard_map/all_to_all | solution.py:394
  254.7 54.7 %all-reduce.4.cloned.1.call-start = ((), (), s32[]{:S(2)}) async-start(), calls=%async_computation.21 | async-start | bytes 1572864 | tf_op jit(solution)/shard_map/psum | solution.py:446
  264.3 19.9 %all-to-all-start.15 = ((bf16[16,144,128]{2,1,0:T(8,128)(2,1)}), bf16[16,144,128]{2,1,0:T(8,128)(2,1)S(1)}, u32[]{:S(2)}, u32[]{:S(2)}) async-start(bf16[16,144,128]{2,1,0:T(8,128)(2,1)} %get-tuple-element.146), calls=%async_computation.15 | async-start | bytes 1179648 | tf_op jit(solution)/shard_map/all_to_all | solution.py:394
  274.5 17.1 %collective-permute-start.15 = (bf16[128,1024]{1,0:T(8,128)(2,1)}, bf16[128,1024]{1,0:T(8,128)(2,1)}, u32[]{:S(2)}, u32[]{:S(2)}) collective-permute-start(bf16[128,1024]{1,0:T(8,128)(2,1)} %dynamic-slice_bitcast_fusion.5), channel_id=1, source_target_pairs={{0,2},{1,3},{2,0},{3,1},{4,6},{5,7},{6,4},{7,5},{8,10},{9,11},{10,... | collective-permute-start | bytes 786440 | tf_op jit(solution)/shard_map/ppermute | solution.py:409
  278.7 15.1 %collective-permute-start.7 = (bf16[128,1024]{1,0:T(8,128)(2,1)S(1)}, bf16[128,1024]{1,0:T(8,128)(2,1)}, u32[]{:S(2)}, u32[]{:S(2)}) collective-permute-start(bf16[128,1024]{1,0:T(8,128)(2,1)S(1)} %dynamic-slice_bitcast_fusion.6), channel_id=1, source_target_pairs={{0,2},{1,3},{2,0},{3,1},{4,6},{5,7},{6,4},{7,5},{8,10},{9,11},{10,... | collective-permute-start | bytes 786440 | tf_op jit(solution)/shard_map/ppermute | solution.py:409
  288.1 10.8 %all-to-all-start.16 = ((bf16[8,16,1024]{2,1,0:T(8,128)(2,1)}), bf16[8,16,1024]{2,1,0:T(8,128)(2,1)S(1)}, u32[]{:S(2)}, u32[]{:S(2)}) async-start(bf16[8,16,1024]{2,1,0:T(8,128)(2,1)} %get-tuple-element.149), calls=%async_computation.16 | async-start | bytes 524288 | tf_op jit(solution)/shard_map/all_to_all | solution.py:394
  292.6 17.9 %collective-permute-start.16 = (bf16[64,1024]{1,0:T(8,128)(2,1)S(1)}, bf16[64,1024]{1,0:T(8,128)(2,1)S(1)}, u32[]{:S(2)}, u32[]{:S(2)}) collective-permute-start(bf16[64,1024]{1,0:T(8,128)(2,1)S(1)} %dynamic-slice_bitcast_fusion.8), channel_id=1, source_target_pairs={{0,4},{1,5},{2,6},{3,7},{4,0},{5,1},{6,2},{7,3},{8,12},{9,13},{10,... | collective-permute-start | bytes 393224 | tf_op jit(solution)/shard_map/ppermute | solution.py:409
  303.8 11.4 %all-to-all-start.17 = ((bf16[8,24,1024]{2,1,0:T(8,128)(2,1)}), bf16[8,24,1024]{2,1,0:T(8,128)(2,1)S(1)}, u32[]{:S(2)}, u32[]{:S(2)}) async-start(bf16[8,24,1024]{2,1,0:T(8,128)(2,1)} %pad_maximum_fusion.4), calls=%async_computation.17 | async-start | bytes 786432 | tf_op jit(solution)/shard_map/all_to_all | solution.py:394
  307.9 12.9 %collective-permute-start.8 = (bf16[64,1024]{1,0:T(8,128)(2,1)S(1)}, bf16[64,1024]{1,0:T(8,128)(2,1)S(1)}, u32[]{:S(2)}, u32[]{:S(2)}) collective-permute-start(bf16[64,1024]{1,0:T(8,128)(2,1)S(1)} %dynamic-slice_bitcast_fusion.9), channel_id=1, source_target_pairs={{0,12},{1,13},{2,14},{3,15},{4,8},{5,9},{6,10},{7,11},{8,4},{9,5},... | collective-permute-start | bytes 393224 | tf_op jit(solution)/shard_map/ppermute | solution.py:409
  309.4 17.9 %collective-permute-start.24 = (bf16[256,1024]{1,0:T(8,128)(2,1)}, bf16[256,1024]{1,0:T(8,128)(2,1)}, u32[]{:S(2)}, u32[]{:S(2)}) collective-permute-start(bf16[256,1024]{1,0:T(8,128)(2,1)} %get-tuple-element.198), channel_id=1, source_target_pairs={{0,2},{1,3},{2,0},{3,1},{4,6},{5,7},{6,4},{7,5},{8,10},{9,11},{10,... | collective-permute-start | bytes 1572872 | tf_op jit(solution)/shard_map/ppermute | solution.py:409
  317.0 4.6 %collective-permute-start = (bf16[8,8,4224]{2,1,0:T(8,128)(2,1)S(1)}, bf16[8,8,4224]{2,1,0:T(8,128)(2,1)S(1)}, u32[]{:S(2)}, u32[]{:S(2)}) collective-permute-start(bf16[8,8,4224]{2,1,0:T(8,128)(2,1)S(1)} %fusion.7), channel_id=1, source_target_pairs={{0,1},{1,0},{2,3},{3,2},{4,5},{5,4},{6,7},{7,6},{8,9},{9,8},{10,11... | collective-permute-start | bytes 1622024 | tf_op jit(solution)/shard_map/ppermute | solution.py:409
  319.5 10.3 %collective-permute-start.17 = (bf16[32,1024]{1,0:T(8,128)(2,1)S(1)}, bf16[32,1024]{1,0:T(8,128)(2,1)S(1)}, u32[]{:S(2)}, u32[]{:S(2)}) collective-permute-start(bf16[32,1024]{1,0:T(8,128)(2,1)S(1)} %dynamic-slice_bitcast_fusion.10), channel_id=1, source_target_pairs={{0,12},{1,13},{2,14},{3,15},{4,8},{5,9},{6,10},{7,11},{8,4},{9,5},... | collective-permute-start | bytes 196616 | tf_op jit(solution)/shard_map/ppermute | solution.py:409
  320.9 11.8 %collective-permute-start.9 = (bf16[32,1024]{1,0:T(8,128)(2,1)S(1)}, bf16[32,1024]{1,0:T(8,128)(2,1)S(1)}, u32[]{:S(2)}, u32[]{:S(2)}) collective-permute-start(bf16[32,1024]{1,0:T(8,128)(2,1)S(1)} %dynamic-slice_bitcast_fusion.11), channel_id=1, source_target_pairs={{0,4},{1,5},{2,6},{3,7},{4,0},{5,1},{6,2},{7,3},{8,12},{9,13},{10,... | collective-permute-start | bytes 196616 | tf_op jit(solution)/shard_map/ppermute | solution.py:409
  322.5 22.3 %all-to-all-start.18 = ((bf16[8,8,4224]{2,1,0:T(8,128)(2,1)}), bf16[8,8,4224]{2,1,0:T(8,128)(2,1)S(1)}, u32[]{:S(2)}, u32[]{:S(2)}) async-start(bf16[8,8,4224]{2,1,0:T(8,128)(2,1)} %fusion.1), calls=%async_computation.18 | async-start | bytes 1081344 | tf_op jit(solution)/shard_map/all_to_all | solution.py:451
  328.7 43.6 %collective-permute-start.25 = (bf16[512,1024]{1,0:T(8,128)(2,1)S(1)}, bf16[512,1024]{1,0:T(8,128)(2,1)}, u32[]{:S(2)}, u32[]{:S(2)}) collective-permute-start(bf16[512,1024]{1,0:T(8,128)(2,1)S(1)} %pad_maximum_fusion.own_ref), channel_id=1, source_target_pairs={{0,1},{1,0},{2,3},{3,2},{4,5},{5,4},{6,7},{7,6},{8,9},{9,8},{10,11... | collective-permute-start | bytes 3145736 | tf_op jit(solution)/shard_map/ppermute | solution.py:409
  329.7 7.2 %collective-permute-start.18 = (bf16[32,1024]{1,0:T(8,128)(2,1)S(1)}, bf16[32,1024]{1,0:T(8,128)(2,1)S(1)}, u32[]{:S(2)}, u32[]{:S(2)}) collective-permute-start(bf16[32,1024]{1,0:T(8,128)(2,1)S(1)} %fusion.15), channel_id=1, source_target_pairs={{0,12},{1,13},{2,14},{3,15},{4,8},{5,9},{6,10},{7,11},{8,4},{9,5},... | collective-permute-start | bytes 196616 | tf_op jit(solution)/shard_map/ppermute | solution.py:409
  332.7 4.7 %collective-permute-start.10 = (bf16[32,1024]{1,0:T(8,128)(2,1)S(1)}, bf16[32,1024]{1,0:T(8,128)(2,1)S(1)}, u32[]{:S(2)}, u32[]{:S(2)}) collective-permute-start(bf16[32,1024]{1,0:T(8,128)(2,1)S(1)} %fusion.16), channel_id=1, source_target_pairs={{0,4},{1,5},{2,6},{3,7},{4,0},{5,1},{6,2},{7,3},{8,12},{9,13},{10,... | collective-permute-start | bytes 196616 | tf_op jit(solution)/shard_map/ppermute | solution.py:409
  332.8 11.3 %collective-permute-start.3 = (bf16[128,1024]{1,0:T(8,128)(2,1)S(1)}, bf16[128,1024]{1,0:T(8,128)(2,1)S(1)}, u32[]{:S(2)}, u32[]{:S(2)}) collective-permute-start(bf16[128,1024]{1,0:T(8,128)(2,1)S(1)} %copy-done.21), channel_id=1, source_target_pairs={{0,2},{1,3},{2,0},{3,1},{4,6},{5,7},{6,4},{7,5},{8,10},{9,11},{10,... | collective-permute-start | bytes 786440 | tf_op jit(solution)/shard_map/ppermute | solution.py:409
  337.0 8.5 %collective-permute-start.19 = (bf16[64,1024]{1,0:T(8,128)(2,1)S(1)}, bf16[64,1024]{1,0:T(8,128)(2,1)}, u32[]{:S(2)}, u32[]{:S(2)}) collective-permute-start(bf16[64,1024]{1,0:T(8,128)(2,1)S(1)} %pad_maximum_fusion.8), channel_id=1, source_target_pairs={{0,4},{1,5},{2,6},{3,7},{4,0},{5,1},{6,2},{7,3},{8,12},{9,13},{10,... | collective-permute-start | bytes 393224 | tf_op jit(solution)/shard_map/ppermute | solution.py:409
  338.1 10.5 %collective-permute-start.11 = (bf16[64,1024]{1,0:T(8,128)(2,1)}, bf16[64,1024]{1,0:T(8,128)(2,1)}, u32[]{:S(2)}, u32[]{:S(2)}) collective-permute-start(bf16[64,1024]{1,0:T(8,128)(2,1)} %pad_maximum_fusion.7), channel_id=1, source_target_pairs={{0,12},{1,13},{2,14},{3,15},{4,8},{5,9},{6,10},{7,11},{8,4},{9,5},... | collective-permute-start | bytes 393224 | tf_op jit(solution)/shard_map/ppermute | solution.py:409
  344.3 21.4 %collective-permute-start.4 = (bf16[256,1024]{1,0:T(8,128)(2,1)S(1)}, bf16[256,1024]{1,0:T(8,128)(2,1)}, u32[]{:S(2)}, u32[]{:S(2)}) collective-permute-start(bf16[256,1024]{1,0:T(8,128)(2,1)S(1)} %pad_maximum_fusion.1.own_ref), channel_id=1, source_target_pairs={{0,1},{1,0},{2,3},{3,2},{4,5},{5,4},{6,7},{7,6},{8,9},{9,8},{10,11... | collective-permute-start | bytes 1572872 | tf_op jit(solution)/shard_map/ppermute | solution.py:409
  347.3 9.7 %collective-permute-start.20 = (bf16[128,1024]{1,0:T(8,128)(2,1)}, bf16[128,1024]{1,0:T(8,128)(2,1)}, u32[]{:S(2)}, u32[]{:S(2)}) collective-permute-start(bf16[128,1024]{1,0:T(8,128)(2,1)} %pad_maximum_fusion.6), channel_id=1, source_target_pairs={{0,2},{1,3},{2,0},{3,1},{4,6},{5,7},{6,4},{7,5},{8,10},{9,11},{10,... | collective-permute-start | bytes 786440 | tf_op jit(solution)/shard_map/ppermute | solution.py:409
  350.3 13.5 %collective-permute-start.12 = (bf16[128,1024]{1,0:T(8,128)(2,1)}, bf16[128,1024]{1,0:T(8,128)(2,1)}, u32[]{:S(2)}, u32[]{:S(2)}) collective-permute-start(bf16[128,1024]{1,0:T(8,128)(2,1)} %pad_maximum_fusion.5), channel_id=1, source_target_pairs={{0,2},{1,3},{2,0},{3,1},{4,6},{5,7},{6,4},{7,5},{8,10},{9,11},{10,... | collective-permute-start | bytes 786440 | tf_op jit(solution)/shard_map/ppermute | solution.py:409
  352.8 15.5 %all-to-all-start.19 = ((bf16[8,8,4224]{2,1,0:T(8,128)(2,1)}), bf16[8,8,4224]{2,1,0:T(8,128)(2,1)S(1)}, u32[]{:S(2)}, u32[]{:S(2)}) async-start(bf16[8,8,4224]{2,1,0:T(8,128)(2,1)} %broadcast_in_dim.15), calls=%async_computation.19 | async-start | bytes 1081344 | tf_op jit(solution)/shard_map/all_to_all | solution.py:451
  358.1 14.1 %collective-permute-start.21 = (bf16[256,1024]{1,0:T(8,128)(2,1)S(1)}, bf16[256,1024]{1,0:T(8,128)(2,1)}, u32[]{:S(2)}, u32[]{:S(2)}) collective-permute-start(bf16[256,1024]{1,0:T(8,128)(2,1)S(1)} %pad_maximum_fusion.3.f_own), channel_id=1, source_target_pairs={{0,1},{1,0},{2,3},{3,2},{4,5},{5,4},{6,7},{7,6},{8,9},{9,8},{10,11... | collective-permute-start | bytes 1572872 | tf_op jit(solution)/shard_map/ppermute | solution.py:409
  368.3 10.2 %collective-permute-start.5 = (bf16[8,8,4224]{2,1,0:T(8,128)(2,1)S(1)}, bf16[8,8,4224]{2,1,0:T(8,128)(2,1)}, u32[]{:S(2)}, u32[]{:S(2)}) collective-permute-start(bf16[8,8,4224]{2,1,0:T(8,128)(2,1)S(1)} %all-to-all-done.19.late_own), channel_id=1, source_target_pairs={{0,1},{1,0},{2,3},{3,2},{4,5},{5,4},{6,7},{7,6},{8,9},{9,8},{10,11... | collective-permute-start | bytes 1622024 | tf_op jit(solution)/shard_map/ppermute | solution.py:409
  370.2 2.1 collective-permute-start.13
  (29 other events, 283.6 us)
Sparse Core Ops, SparseCore 0:
  104.0 44.8 all-gather.1
  259.1 47.0 all-reduce.3
